TPU v7x, 256 devices: a whole 4x4x8 slice. The times are simulated.
256 devices in a mesh: member: 16 (over x_lo, z), shard: 16 (over x_hi, y, core).
Axes of the slice: x: 4 (x_hi: 2, x_lo: 2; x = x_hi * 2 + x_lo), y: 4, z: 8, core: 2. Of those that a mesh axis runs over, the one named last changes fastest.
Arguments:
- tokens: bfloat16 [65536, 4096], P(('member', 'shard')), may hold values from -24 to 24
- cotangent: bfloat16 [65536, 1024], P(('member', 'shard')), may hold values from -6 to 6
- slow_weight: bfloat16 [4096, 1024], P('shard'), may hold values from -0.09375 to 0.09375
- in_scale: float32 [16, 4096], P('member'), may hold values from 0.1 to 1.9
- out_scale: float32 [16, 1024], P('member'), may hold values from 0.1 to 1.9
Outputs:
- outputs: bfloat16 [65536, 1024], P(('member', 'shard'))
- grad_tokens: bfloat16 [65536, 4096], P(('member', 'shard'))
- grad_weight: float32 [4096, 1024], P('shard')
- grad_in_scale: float32 [16, 4096], P('member')
- grad_out_scale: float32 [16, 1024], P('member')
All inputs are finite; a program needn't handle non-finite values.
Results may differ from a plain program's by a relative error of at most 0.005.
Values may be sent and summed in bfloat16 or wider, within the bound.
No kernel may reach another device: no remote copies, remote signals or barrier semaphores. Data moves between devices by JAX's collectives and lax.ppermute only.
A program may use at most 128 MiB of HBM per device.

v0:
```python
import jax
import jax.numpy as jnp
from jax import lax
from jax.sharding import PartitionSpec as P


def on_device(tokens, cotangent, slow_weight, in_scale, out_scale):
    member_rows = tokens.shape[0] * lax.axis_size("shard")
    member_norm = 1.0 / float(member_rows) ** 0.5
    total_norm = 1.0 / float(member_rows * lax.axis_size("member")) ** 0.5
    grads_f = cotangent.astype(jnp.float32)
    scaled_grad = (grads_f * out_scale).astype(jnp.bfloat16)
    whole_weight = lax.all_gather(slow_weight, "shard", axis=0, tiled=True)
    scaled = (tokens.astype(jnp.float32) * in_scale).astype(jnp.bfloat16)
    pre_out = jnp.dot(scaled, whole_weight, preferred_element_type=jnp.float32)
    back = lax.dot_general(
        scaled_grad, whole_weight, (((1,), (1,)), ((), ())), preferred_element_type=jnp.float32
    )
    grad_in = (back * in_scale).astype(jnp.bfloat16)
    in_part = jnp.sum(tokens.astype(jnp.float32) * back, axis=0, keepdims=True)
    out_part = jnp.sum(grads_f * pre_out, axis=0, keepdims=True)
    in_sum, out_sum = lax.psum((in_part, out_part), "shard")
    weight_part = lax.psum_scatter(
        lax.dot_general(
            scaled, scaled_grad, (((0,), (0,)), ((), ())), preferred_element_type=jnp.float32
        ),
        "shard",
        scatter_dimension=0,
        tiled=True,
    )
    result = (pre_out * out_scale).astype(jnp.bfloat16)
    grad_weight = lax.psum(weight_part, "member") * total_norm
    return (result, grad_in, grad_weight, in_sum * member_norm, out_sum * member_norm)


def solution(mesh):
    placed = (
        P(("member", "shard"), None),
        P(("member", "shard"), None),
        P("shard", None),
        P("member", None),
        P("member", None),
    )
    return jax.shard_map(
        on_device,
        mesh=mesh,
        in_specs=placed,
        out_specs=(
            P(("member", "shard"), None),
            P(("member", "shard"), None),
            P("shard", None),
            P("member", None),
            P("member", None),
        ),
        check_vma=False,
    )
```

profile of v0, /device:TPU:2, one launch (start us, length us, event | category | flops | bytes accessed | tf_op | source)
XLA Modules:
  0.0 395.7 jit_solution(11142766647410300230)
XLA Ops:
  7.2 0.0 all-gather.2.cloned.1.call-start
  7.2 0.7 all-gather.2.cloned.1.call-update
  7.9 0.0 reduce-scatter.2.cloned.1.call-start
  7.9 9.8 %fusion.2 = f32[4096,1024]{1,0:T(8,128)} fusion(bf16[256,4096]{1,0:T(8,128)(2,1)} %param.5, f32[4096]{0:T(1024)} %bitcast.6, bf16[256,1024]{1,0:T(8,128)(2,1)} %param.6, f32[1024]{0:T(1024)} %bitcast.10), kind=kOutput, calls=%fused_computation.5 | convolution fusion | flops 2151415808 | bytes 19419136 | tf_op jit(solution)/shard_map/dot_general | solution.py:24
  17.8 0.0 copy-start
  17.8 0.0 copy-start.1
  17.8 0.0 reduce-scatter.2.cloned.1.call-update
  17.8 0.0 all-reduce.3.cloned.1.call-start
  17.9 73.0 %all-gather.2.cloned.1.call-done = bf16[4096,1024]{1,0:T(8,128)(2,1)} async-done(((bf16[256,1024]{1,0:T(8,128)(2,1)}), bf16[4096,1024]{1,0:T(8,128)(2,1)}) %all-gather.2.cloned.1.call-update) | async-done | bytes 8388624 | tf_op jit(solution)/shard_map/all_gather | solution.py:13
  90.8 0.0 copy-done
  90.8 0.0 copy-done.1
  90.8 0.0 copy-done.2
  90.9 0.0 copy-done.3
  90.9 0.0 copy-start.4
  90.9 6.7 %fusion.7 = (f32[1024]{0:T(1024)S(1)}, bf16[256,1024]{1,0:T(8,128)(2,1)}) fusion(bf16[256,1024]{1,0:T(8,128)(2,1)S(1)} %copy-done.1, f32[1024]{0:T(1024)S(1)} %bitcast.11, bf16[4096,1024]{1,0:T(8,128)(2,1)} %all-gather.2.cloned.1.call-done, bf16[256,4096]{1,0:T(8,128)(2,1)S(1)} %copy-done, f32[4096]{0:T(1024)S(1)} %bitcast.7), kind=kOutput, calls=%fused_computation.10 | convolution fusion | flops 2151939072 | bytes 11558912 | tf_op jit(solution)/shard_map/dot_general | solution.py:15
  97.6 0.0 copy-done.4
  97.6 4.0 %fusion.1 = (f32[4096]{0:T(1024)S(1)}, bf16[256,4096]{1,0:T(8,128)(2,1)}) fusion(bf16[256,4096]{1,0:T(8,128)(2,1)S(1)} %copy-done, f32[4096]{0:T(1024)S(1)} %bitcast.8, bf16[4096,1024]{1,0:T(8,128)(2,1)S(1)} %copy-done.4, bf16[256,1024]{1,0:T(8,128)(2,1)S(1)} %copy-done.1, f32[1024]{0:T(1024)S(1)} %bitcast.12), kind=kOutput, calls=%fused_computation.3 | convolution fusion | flops 2153508864 | bytes 13144064 | tf_op jit(solution)/shard_map/dot_general | solution.py:16
  101.6 66.8 %all-reduce = (f32[1,4096]{1,0:T(1,128)S(1)}, f32[1,1024]{1,0:T(1,128)S(1)}) all-reduce(f32[1,4096]{1,0:T(1,128)S(1)} %bitcast.9, f32[1,1024]{1,0:T(1,128)S(1)} %bitcast.13), channel_id=1, replica_groups=mesh['member'=16,'shard'=16] {'shard'}, use_global_device_ids=true, to_apply=%region_3.0 | all-reduce | flops 5120 | bytes 40960 | tf_op jit(solution)/shard_map/psum | solution.py:22
  168.4 80.4 %reduce-scatter.2.cloned.1.call-done = f32[256,1024]{1,0:T(8,128)} async-done(((f32[4096,1024]{1,0:T(8,128)}), f32[256,1024]{1,0:T(8,128)}) %reduce-scatter.2.cloned.1.call-update) | async-done | bytes 1048592 | tf_op jit(solution)/shard_map/reduce_scatter | solution.py:23
  248.7 0.0 all-reduce.3.cloned.1.call-update
  248.8 0.6 broadcast_multiply_fusion.2
  249.4 0.6 broadcast_multiply_fusion.1
  250.0 136.9 %all-reduce.3.cloned.1.call-done = f32[256,1024]{1,0:T(8,128)} async-done(((f32[256,1024]{1,0:T(8,128)}), f32[256,1024]{1,0:T(8,128)}) %all-reduce.3.cloned.1.call-update) | async-done | bytes 1048592 | tf_op jit(solution)/shard_map/psum | solution.py:32
  386.9 2.3 broadcast_multiply_fusion
  (2 shorter events, 0.0 us)
Async XLA Ops:
  7.2 83.7 %all-gather.2.cloned.1.call-start = ((), (), s32[]{:S(2)}) async-start(), calls=%async_computation.1 | async-start | bytes 8912896 | tf_op jit(solution)/shard_map/all_gather | solution.py:13
  7.9 240.8 %reduce-scatter.2.cloned.1.call-start = ((), (), s32[]{:S(2)}) async-start(), calls=%async_computation.2 | async-start | bytes 17825792 | tf_op jit(solution)/shard_map/reduce_scatter | solution.py:23
  17.8 73.1 %copy-start = (bf16[256,4096]{1,0:T(8,128)(2,1)S(1)}, bf16[256,4096]{1,0:T(8,128)(2,1)}, u32[]{:S(2)}) copy-start(bf16[256,4096]{1,0:T(8,128)(2,1)} %param.5) | copy-start | bytes 6291460
  17.8 73.1 %copy-start.1 = (bf16[256,1024]{1,0:T(8,128)(2,1)S(1)}, bf16[256,1024]{1,0:T(8,128)(2,1)}, u32[]{:S(2)}) copy-start(bf16[256,1024]{1,0:T(8,128)(2,1)} %param.6) | copy-start | bytes 1572868
  17.8 73.1 %copy-start.2 = (f32[1,4096]{1,0:T(1,128)S(1)}, f32[1,4096]{1,0:T(1,128)}, u32[]{:S(2)}) copy-start(f32[1,4096]{1,0:T(1,128)} %param.8) | copy-start | bytes 49156
  17.8 73.1 %copy-start.3 = (f32[1,1024]{1,0:T(1,128)S(1)}, f32[1,1024]{1,0:T(1,128)}, u32[]{:S(2)}) copy-start(f32[1,1024]{1,0:T(1,128)} %param.9) | copy-start | bytes 12292
  17.8 369.1 %all-reduce.3.cloned.1.call-start = ((), (), s32[]{:S(2)}) async-start(), calls=%async_computation.3 | async-start | bytes 2097152 | tf_op jit(solution)/shard_map/psum | solution.py:32
  90.9 6.7 %copy-start.4 = (bf16[4096,1024]{1,0:T(8,128)(2,1)S(1)}, bf16[4096,1024]{1,0:T(8,128)(2,1)}, u32[]{:S(2)}) copy-start(bf16[4096,1024]{1,0:T(8,128)(2,1)} %all-gather.2.cloned.1.call-done) | copy-start | bytes 25165828
Sparse Core Ops, SparseCore 0:
  10.8 80.0 all-gather.1
  95.4 153.2 reduce-scatter.1
  251.4 135.4 all-reduce.2
where the time goes:
time: 397 us; the launch traced here: 396 us
  waiting for transfers between devices  291 us (73%)
  blocking collectives  66.8 us (17%)
  matrix products  20.5 us (5%)
  between operations  13.8 us (3%)
    psum x1, waiting for transfers between devices, on_device(): grad_weight = lax.psum(weight_part, 'member') * total_norm  137 us
    reduce_scatter x1, waiting for transfers between devices, on_device(): lax.psum_scatter(lax.dot_general(scaled, scaled_grad, (((0,), (0,)), ((),...  80.4 us
    all_gather x1, waiting for transfers between devices, on_device(): whole_weight = lax.all_gather(slow_weight, 'shard', axis=0, tiled=True)  73 us
    psum x1, blocking collectives, on_device(): in_sum, out_sum = lax.psum((in_part, out_part), 'shard')  66.8 us
    dot_general x1, matrix products, on_device(): lax.dot_general(scaled, scaled_grad, (((0,), (0,)), ((), ())), preferred_...  9.82 us
  transfers between devices with their start and end apart: 3, of which 3 were waited for; matrix products, arithmetic and copies ran while one was open for 5% of the time, Pallas kernels for 0%

commit v1 on v0

v1 whole, which is shorter than its diff:
```python
import functools

import jax
import jax.numpy as jnp
from jax import lax
from jax.experimental import pallas as pl
from jax.experimental.pallas import tpu as pltpu
from jax.sharding import Mesh, PartitionSpec as P

F32, BF16 = jnp.float32, jnp.bfloat16
XL, Z, XH, Y, C = "xl", "z", "xh", "y", "c"
ROWS, DEPTH, WIDTH, PIECE = 256, 4096, 1024, 256
HALF, LANE = WIDTH // 2, PIECE // 2
VMEM = pl.BlockSpec(memory_space=pltpu.VMEM)
PARAMS = pltpu.CompilerParams(vmem_limit_bytes=40 * 2**20)


def send_y(a, step):
    return lax.ppermute(a, Y, [(i, (i + step) % 4) for i in range(4)])


def send_z(a, step):
    return lax.ppermute(a, Z, [(i, (i + step) % 8) for i in range(8)])


def x_index(place):
    return (place % 2) * 2 + place // 2


def send_x(a, step):
    return lax.ppermute(a, (XL, XH), [(x_index(i), x_index((i + step) % 4)) for i in range(4)])


def pairs_x(a, other):
    return lax.ppermute(a, (XL, XH), [(x_index(i), x_index(other(i))) for i in range(4)])


def swap_core(a):
    return lax.ppermute(a, C, [(0, 1), (1, 0)])


def slice_of(pos, dxh, dy):
    return ((pos[0] // 2 + dxh) % 2) * 4 + (pos[1] + dy) % 4


def cost(flops, bytes_accessed):
    return pl.CostEstimate(flops=flops, bytes_accessed=bytes_accessed, transcendentals=0)


def copy_body(pos, src, dst):
    dst[...] = src[...]


def other_half(pos, tokens):
    return pl.pallas_call(
        copy_body,
        out_shape=jax.ShapeDtypeStruct((ROWS, DEPTH // 2), BF16),
        grid_spec=pltpu.PrefetchScalarGridSpec(
            num_scalar_prefetch=1,
            grid=(8,),
            in_specs=[pl.BlockSpec((ROWS, PIECE), lambda j, pos: (0, 2 * j + 1 - pos[2]))],
            out_specs=pl.BlockSpec((ROWS, PIECE), lambda j, pos: (0, j)),
        ),
        compiler_params=PARAMS,
        cost_estimate=cost(0, 2**21),
    )(pos, tokens)


def partial_body(pos, tok, tok_other, cot, cot_other, in_scale, out_scale, grad_ref, *outs):
    a_refs, b_refs = outs[:4], outs[4:]
    i = pl.program_id(0)

    @pl.when(i == 0)
    def _():
        grad_ref[:ROWS] = (cot[...].astype(F32) * out_scale[...]).astype(BF16)
        grad_ref[ROWS:] = (cot_other[...].astype(F32) * out_scale[...]).astype(BF16)

    y_at = (pos[1] + i) % 4
    for k in range(4):
        x_at = (pos[0] + k) % 4
        place = (x_at // 2) * 4 + y_at
        wide = pl.ds(pl.multiple_of(((place * 2 + pos[2]) * 2 + x_at % 2) * LANE, LANE), LANE)
        narrow = pl.ds(pl.multiple_of((place * 2 + x_at % 2) * LANE, LANE), LANE)
        scale = in_scale[:, wide]
        first = (tok[:, wide].astype(F32) * scale).astype(BF16)
        second = (tok_other[:, narrow].astype(F32) * scale).astype(BF16)
        dims = (((0,), (0,)), ((), ()))
        part = lax.dot_general(first, grad_ref[:ROWS], dims, preferred_element_type=F32)
        part = part + lax.dot_general(second, grad_ref[ROWS:], dims, preferred_element_type=F32)
        part = part.astype(BF16)
        b_refs[k][0] = part[:, HALF:]
        for m in range(4):
            @pl.when(i == m)
            def _():
                a_refs[m][k] = part[:, :HALF]


def partials(pos, tokens, tok_other, cot, cot_other, in_scale, out_scale):
    whole = lambda shape: pl.BlockSpec(shape, lambda i, pos: (0,) * len(shape))
    block = jax.ShapeDtypeStruct((4, LANE, HALF), BF16)
    outs = pl.pallas_call(
        partial_body,
        out_shape=[jax.ShapeDtypeStruct((2 * ROWS, WIDTH), BF16)] + [block] * 8,
        grid_spec=pltpu.PrefetchScalarGridSpec(
            num_scalar_prefetch=1,
            grid=(4,),
            in_specs=[
                whole((ROWS, DEPTH)), whole((ROWS, DEPTH // 2)), whole((ROWS, WIDTH)),
                whole((ROWS, WIDTH)), whole((1, DEPTH)), whole((1, WIDTH)),
            ],
            out_specs=[whole((2 * ROWS, WIDTH))]
            + [whole((4, LANE, HALF))] * 4
            + [pl.BlockSpec((1, LANE, HALF), lambda i, pos: (i, 0, 0))] * 4,
        ),
        compiler_params=PARAMS,
        cost_estimate=cost(2 * 2 * ROWS * DEPTH // 2 * WIDTH, 9 * 2**20),
    )(pos, tokens, tok_other, cot, cot_other, in_scale, out_scale)
    return outs[0], outs[1:5], outs[5:]


def sum_body(own, r1, r2, r3, keep, s1, s2, s3):
    for k, out in enumerate((keep, s1, s2, s3)):
        total = own[k].astype(F32) + r1[k].astype(F32) + r2[k].astype(F32) + r3[k].astype(F32)
        out[...] = total.astype(out.dtype)


def sum_blocks(own, arrived):
    shape = (LANE, HALF)
    return pl.pallas_call(
        sum_body,
        out_shape=[jax.ShapeDtypeStruct(shape, F32)] + [jax.ShapeDtypeStruct(shape, BF16)] * 3,
        in_specs=[VMEM] * 4,
        out_specs=[VMEM] * 4,
        compiler_params=PARAMS,
        cost_estimate=cost(2**20, 5 * 2**19),
    )(own, *arrived)


def join_body(pos, a0, a1, a2, a3, b0, b1, b2, b3, keep, send):
    count = LANE // 2
    mine = pos[3] % 2
    for out, at in ((keep, mine), (send, 1 - mine)):
        rows = pl.ds(pl.multiple_of(at * count, count), count)
        for side, refs in ((0, (a0, a1, a2, a3)), (1, (b0, b1, b2, b3))):
            total = refs[0][rows]
            for ref in refs[1:]:
                total = total + ref[rows].astype(F32)
            out[:, side * HALF : (side + 1) * HALF] = total.astype(out.dtype)


def join(pos, a, b):
    shape = (LANE // 2, WIDTH)
    return pl.pallas_call(
        join_body,
        out_shape=[jax.ShapeDtypeStruct(shape, F32), jax.ShapeDtypeStruct(shape, BF16)],
        in_specs=[pl.BlockSpec(memory_space=pltpu.SMEM)] + [VMEM] * 8,
        out_specs=[VMEM] * 2,
        compiler_params=PARAMS,
        cost_estimate=cost(2**20, 2**21),
    )(pos, *a, *b)


def place_body(scale, pos, own, by_z, by_x, by_both, out):
    count = LANE // 2
    me = (pos[0] % 2) * 2 + pos[3] % 2
    for flip, ref in enumerate((own, by_z, by_x, by_both)):
        at = (me // 2 + flip // 2) % 2 * 2 + (me + flip) % 2
        out[pl.ds(pl.multiple_of(at * count, count), count)] = ref[...].astype(F32) * scale


def place(pos, blocks, scale):
    return pl.pallas_call(
        functools.partial(place_body, scale),
        out_shape=jax.ShapeDtypeStruct((PIECE, WIDTH), F32),
        in_specs=[pl.BlockSpec(memory_space=pltpu.SMEM)] + [VMEM] * 4,
        out_specs=VMEM,
        compiler_params=PARAMS,
        cost_estimate=cost(2**18, 2**20),
    )(pos, *blocks)


def layer_body(order, last, pos, tok, tok_other, grad, in_scale, cot, cot_other, *refs):
    weights, refs = refs[:4], refs[4:]
    if last:
        (pre_in, small_in, _), refs = refs[:3], refs[3:]
        own_ref, other_ref, pre_ref, pre_other, small, total = refs
    else:
        own_ref, other_ref, pre_ref, small = refs
        total = pre_ref
    i = pl.program_id(0)

    @pl.when(i == 0)
    def _():
        if last:
            total[...] = pre_in[...]
            small[...] = small_in[...]
        else:
            small[...] = jnp.zeros_like(small)

    for m, (dxh, dy) in enumerate(order):
        @pl.when(i == m)
        def _():
            at = slice_of(pos, dxh, dy)
            wide = pl.ds(pl.multiple_of((at * 2 + pos[2]) * PIECE, PIECE), PIECE)
            narrow = pl.ds(pl.multiple_of(at * PIECE, PIECE), PIECE)
            scale = in_scale[:, wide]
            weight = weights[m][...]
            sums = jnp.zeros((1, PIECE), F32)
            for part, values in ((0, tok[:, wide]), (1, tok_other[:, narrow])):
                rows = slice(part * ROWS, (part + 1) * ROWS)
                values = values.astype(F32)
                scaled = (values * scale).astype(BF16)
                pre = jnp.dot(scaled, weight, preferred_element_type=F32)
                if m == 0 and not last:
                    total[rows] = pre
                else:
                    total[rows] += pre
                back = lax.dot_general(
                    grad[rows], weight, (((1,), (1,)), ((), ())), preferred_element_type=F32
                )
                (own_ref, other_ref)[part][...] = (back * scale).astype(BF16)
                sums = sums + jnp.sum(values * back, axis=0, keepdims=True)
            small[:, wide] = sums

    if last:
        @pl.when(i == 3)
        def _():
            pre_ref[...] = total[:ROWS]
            pre_other[...] = total[ROWS:].astype(BF16)
            small[:, DEPTH:] = jnp.sum(
                cot[...].astype(F32) * total[:ROWS] + cot_other[...].astype(F32) * total[ROWS:],
                axis=0, keepdims=True,
            )


def layer(pos, order, tokens, tok_other, grad, in_scale, cot, cot_other, weights, before=None):
    whole = lambda shape: pl.BlockSpec(shape, lambda i, pos: (0,) * len(shape))
    shaped = jax.ShapeDtypeStruct
    dxhs = [o[0] for o in order]
    dys = [o[1] for o in order]

    def column(i, pos):
        dxh, dy = dxhs[3], dys[3]
        for m in range(3):
            dxh = jnp.where(i == m, dxhs[m], dxh)
            dy = jnp.where(i == m, dys[m], dy)
        return 0, slice_of(pos, dxh, dy) * 2 + pos[2]

    in_specs = [
        whole((ROWS, DEPTH)), whole((ROWS, DEPTH // 2)), whole((2 * ROWS, WIDTH)), whole((1, DEPTH)),
        whole((ROWS, WIDTH)), whole((ROWS, WIDTH)),
    ] + [whole((PIECE, WIDTH))] * 4
    operands = [tokens, tok_other, grad, in_scale, cot, cot_other, *weights]
    out_shape = [shaped((ROWS, DEPTH), BF16), shaped((ROWS, DEPTH // 4), BF16)]
    out_specs = [pl.BlockSpec((ROWS, PIECE), column), pl.BlockSpec((ROWS, PIECE), lambda i, pos: (0, i))]
    scratch, aliases = [], {}
    small = shaped((1, DEPTH + WIDTH), F32)
    if before is None:
        out_shape += [shaped((2 * ROWS, WIDTH), F32), small]
        out_specs += [whole((2 * ROWS, WIDTH)), whole(small.shape)]
    else:
        own, pre, sums = before
        operands += [pre, sums, own]
        in_specs += [whole((2 * ROWS, WIDTH)), whole(small.shape), pl.BlockSpec(memory_space=pl.ANY)]
        aliases = {len(operands): 0}
        out_shape += [shaped((ROWS, WIDTH), F32), shaped((ROWS, WIDTH), BF16), small]
        out_specs += [whole((ROWS, WIDTH)), whole((ROWS, WIDTH)), whole(small.shape)]
        scratch = [pltpu.VMEM((2 * ROWS, WIDTH), F32)]
    return pl.pallas_call(
        functools.partial(layer_body, order, before is not None),
        out_shape=out_shape,
        grid_spec=pltpu.PrefetchScalarGridSpec(
            num_scalar_prefetch=1, grid=(4,), in_specs=in_specs, out_specs=out_specs,
            scratch_shapes=scratch,
        ),
        input_output_aliases=aliases,
        compiler_params=PARAMS,
        cost_estimate=cost(2 * 2 * 2 * ROWS * WIDTH * WIDTH, 10 * 2**20),
    )(pos, *operands)


def fill_body(pos, first, second, _, out):
    j = pl.program_id(0)

    @pl.when(j < 4)
    def _():
        out[...] = first[...]

    @pl.when(j >= 4)
    def _():
        out[...] = second[...]


def fill(pos, orders, first, second, own):
    flat = orders[0] + orders[1]

    def column(j, pos):
        dxh, dy = flat[7]
        for m in range(7):
            dxh = jnp.where(j == m, flat[m][0], dxh)
            dy = jnp.where(j == m, flat[m][1], dy)
        return 0, slice_of(pos, dxh, dy) * 2 + 1 - pos[2]

    return pl.pallas_call(
        fill_body,
        out_shape=jax.ShapeDtypeStruct((ROWS, DEPTH), BF16),
        grid_spec=pltpu.PrefetchScalarGridSpec(
            num_scalar_prefetch=1,
            grid=(8,),
            in_specs=[
                pl.BlockSpec((ROWS, PIECE), lambda j, pos: (0, jnp.minimum(j, 3))),
                pl.BlockSpec((ROWS, PIECE), lambda j, pos: (0, jnp.maximum(j, 4) - 4)),
                pl.BlockSpec(memory_space=pl.ANY),
            ],
            out_specs=pl.BlockSpec((ROWS, PIECE), column),
        ),
        input_output_aliases={3: 0},
        compiler_params=PARAMS,
        cost_estimate=cost(0, 2**21),
    )(pos, first, second, own)


def on_device(tokens, cotangent, slow_weight, in_scale, out_scale):
    xl, z, xh, y, c = (lax.axis_index(a) for a in (XL, Z, XH, Y, C))
    pos = jnp.stack([2 * xh + xl, y, c, z]).astype(jnp.int32)
    member_norm = 1.0 / float(ROWS * 16) ** 0.5
    total_norm = 1.0 / float(ROWS * 256) ** 0.5

    cot_other = swap_core(cotangent)
    up, down = send_y(slow_weight, 1), send_y(slow_weight, -1)
    far = pairs_x(slow_weight, lambda i: 3 - i)
    tok_other = swap_core(other_half(pos, tokens))

    grad, a_part, b_part = partials(pos, tokens, tok_other, cotangent, cot_other, in_scale, out_scale)
    far, up, down, a_part, b_part = lax.optimization_barrier((far, up, down, a_part, b_part))

    half = PIECE // 2
    far_up = send_y(jnp.concatenate([far, up[:half]], axis=0), 1)
    far_down = send_y(jnp.concatenate([far, down[half:]], axis=0), -1)
    a_in = [send_y(a_part[1], 1), send_y(a_part[3], -1), send_y(a_part[2], 2)]
    b_in = [send_x(b_part[1], 1), send_x(b_part[3], -1), send_x(b_part[2], 2)]
    orders = ((0, 0), (0, 1), (0, 3), (1, 0)), ((0, 2), (1, 3), (1, 1), (1, 2))
    own, others_1, pre, small = layer(
        pos, orders[0], tokens, tok_other, grad, in_scale, cotangent, cot_other,
        (slow_weight, down, up, far),
    )
    far_two_up = send_y(far_up[:half], 1)
    far_two_down = send_y(far_down[half:PIECE], -1)

    a_own, *a_out = sum_blocks(a_part[0], a_in)
    b_own, *b_out = sum_blocks(b_part[0], b_in)
    b_in = [send_y(b_out[0], 1), send_y(b_out[2], -1), send_y(b_out[1], 2)]
    a_in = [send_x(a_out[0], 1), send_x(a_out[2], -1), send_x(a_out[1], 2)]

    two = jnp.concatenate([far_up[PIECE:], far_down[PIECE:]], axis=0)
    far_two = jnp.concatenate([far_two_up, far_two_down], axis=0)
    own, others_2, pre_own, pre_other, small = layer(
        pos, orders[1], tokens, tok_other, grad, in_scale, cotangent, cot_other,
        (two, far_up[:PIECE], far_down[:PIECE], far_two), (own, pre, small),
    )
    pre_other = swap_core(pre_other)
    small = small + swap_core(small)
    others_1, others_2 = swap_core(others_1), swap_core(others_2)

    keep, out = join(pos, [a_own, *a_in], [b_own, *b_in])
    pair = lambda a: lax.ppermute(a, Z, [(i, i ^ 1) for i in range(8)])
    mine = (keep + pair(out).astype(F32)).astype(BF16)
    plus, minus, across = send_z(mine, 2), send_z(mine, -2), send_z(mine, 4)

    result = ((pre_own + pre_other.astype(F32)) * out_scale).astype(BF16)
    grad_tokens = fill(pos, orders, others_1, others_2, own)
    small = small + send_y(small, 2)
    small = small + lax.ppermute(small, Y, [(i, i ^ 1) for i in range(4)])
    small = small + lax.ppermute(small, XH, [(0, 1), (1, 0)])

    summed = (mine.astype(F32) + across.astype(F32)) + (plus.astype(F32) + minus.astype(F32))
    summed = summed.astype(BF16)
    by_z = pair(summed)
    by_x = pairs_x(summed, lambda i: i ^ 1)
    by_both = lax.ppermute(
        summed, (XL, Z), [(i, i ^ 9) for i in range(16)]
    )
    grad_weight = place(pos, (summed, by_z, by_x, by_both), total_norm)
    small = small * member_norm
    return result, grad_tokens, grad_weight, small[:, :DEPTH], small[:, DEPTH:]


def solution(mesh):
    wide = Mesh(mesh.devices.reshape(2, 8, 2, 4, 2), (XL, Z, XH, Y, C))
    row, member, shard = P((XL, Z, XH, Y, C), None), P((XL, Z), None), P((XH, Y, C), None)
    return jax.shard_map(
        on_device,
        mesh=wide,
        in_specs=(row, row, shard, member, member),
        out_specs=(row, row, shard, member, member),
        check_vma=False,
    )
```

time: 397 us -> 127 us (0.32)
  waiting for transfers between devices: 291 us -> 48.6 us
  blocking collectives: 66.8 us -> 0 us
  starting transfers between devices: 0.12 us -> 49.6 us
  Pallas kernels: 0 us -> 23.6 us
  matrix products: 20.5 us -> 0 us
  between operations: 13.8 us -> 0.88 us
    psum x1 -> x0, waiting for transfers between devices: 137 us -> none  [on_device(): grad_weight = lax.psum(weight_part, 'member') * total_norm]
    reduce_scatter x1 -> x0, waiting for transfers between devices: 80.4 us -> none  [on_device(): lax.psum_scatter(lax.dot_general(scaled, scaled_grad, (((0,), (0,)), ((),...]
    all_gather x1 -> x0, waiting for transfers between devices: 73 us -> none  [on_device(): whole_weight = lax.all_gather(slow_weight, 'shard', axis=0, tiled=True)]
    psum x1 -> x0, blocking collectives: 66.8 us -> none  [on_device(): in_sum, out_sum = lax.psum((in_part, out_part), 'shard')]
    ppermute x0 -> x35, starting transfers between devices: none -> 49.6 us  [the longest x13 17.6 us: send_y(): return lax.ppermute(a, Y, [(i, (i + step) % 4) for i in range(4)])]
    ppermute x0 -> x35, waiting for transfers between devices: none -> 48.6 us  [the longest x13 36.8 us: send_y(): return lax.ppermute(a, Y, [(i, (i + step) % 4) for i in range(4)])]
    pallas_call x0 -> x9, Pallas kernels: none -> 23.6 us  [the longest x2 9.38 us: layer(): pl.pallas_call(functools.partial(layer_body, order, before is not None),...]
    dot_general x3 -> x0, matrix products: 20.5 us -> none  [the longest x1 9.82 us: on_device(): lax.dot_general(scaled, scaled_grad, (((0,), (0,)), ((), ())), preferred_...]
  transfers between devices with their start and end apart: 3 -> 35, of which waited for: 3 -> 12; matrix products, arithmetic and copies ran while one was open for 5% -> 2% of each run, Pallas kernels for 0% -> 15%
where the time goes in v1:
time: 127 us
  starting transfers between devices  49.6 us (39%)
  waiting for transfers between devices  48.6 us (38%)
  Pallas kernels  23.6 us (19%)
  local copies, waits for them, and re-layouts  3 us (2%)
  other arithmetic  1.5 us (1%)
    ppermute x13, waiting for transfers between devices, send_y(): return lax.ppermute(a, Y, [(i, (i + step) % 4) for i in range(4)])  36.8 us
    ppermute x13, starting transfers between devices, send_y(): return lax.ppermute(a, Y, [(i, (i + step) % 4) for i in range(4)])  17.6 us
    ppermute x3, starting transfers between devices, send_z(): return lax.ppermute(a, Z, [(i, (i + step) % 8) for i in range(8)])  10.5 us
    ppermute x6, starting transfers between devices, send_x(): lax.ppermute(a, (XL, XH), [(x_index(i), x_index((i + step) % 4)) for i in...  10.5 us
    pallas_call x2, Pallas kernels, layer(): pl.pallas_call(functools.partial(layer_body, order, before is not None),...  9.38 us
    pallas_call x1, Pallas kernels, partials(): pl.pallas_call(partial_body, out_shape=[jax.ShapeDtypeStruct((2 * ROWS, W...  6.78 us
    ppermute x3, waiting for transfers between devices, send_z(): return lax.ppermute(a, Z, [(i, (i + step) % 8) for i in range(8)])  4.92 us
    ppermute x1, waiting for transfers between devices, on_device(): small = small + lax.ppermute(small, Y, [(i, i ^ 1) for i in range(4)])  3.77 us
  transfers between devices with their start and end apart: 35, of which 12 were waited for; matrix products, arithmetic and copies ran while one was open for 2% of the time, Pallas kernels for 15%

profile of v1, /device:TPU:2, one launch (start us, length us, event | category | flops | bytes accessed | tf_op | source)
XLA Modules:
  0.0 127.2 jit_solution(2693936704718052441)
XLA Ops:
  7.1 1.7 %collective-permute-start.4 = (bf16[256,1024]{1,0:T(8,128)(2,1)S(1)}, bf16[256,1024]{1,0:T(8,128)(2,1)S(1)}, u32[]{:S(2)}, u32[]{:S(2)}) collective-permute-start(bf16[256,1024]{1,0:T(8,128)(2,1)S(1)} %copy-done.5), channel_id=1, source_target_pairs={{0,6},{2,0},{4,2},{6,4},{1,7},{3,1},{5,3},{7,5},{8,14},{10,8},{12,... | collective-permute-start | bytes 1572872 | tf_op jit(solution)/shard_map/ppermute | solution.py:19
  8.7 6.8 %shard_map.93 = (bf16[512,1024]{1,0:T(8,128)(2,1)S(1)}, bf16[4,128,512]{2,1,0:T(8,128)(2,1)S(1)}, bf16[4,128,512]{2,1,0:T(8,128)(2,1)S(1)}, bf16[4,128,512]{2,1,...) custom-call(s32[4]{0:T(128)S(1)} %pad_add_fusion.pos, ...), custom_call_target="tpu_custom_call" | custom-call | flops 2147483648 | bytes 9437184 | tf_op jit(solution)/shard_map/pallas_call | solution.py:101
  15.5 3.7 %collective-permute-done.3.refs_2_ = bf16[256,1024]{1,0:T(8,128)(2,1)S(1)} collective-permute-done((bf16[256,1024]{1,0:T(8,128)(2,1)S(1)}, bf16[256,1024]{1,0:T(8,128)(2,1)S(1)}, u32[]{:S(2)}, u32[]{:S(2)}) %collective-permute-start.3) | collective-permute-done | bytes 524320 | tf_op jit(solution)/shard_map/ppermute | solution.py:19
  23.7 1.7 %collective-permute-start.14 = (bf16[4,128,512]{2,1,0:T(8,128)(2,1)S(1)}, bf16[4,128,512]{2,1,0:T(8,128)(2,1)S(1)}, u32[]{:S(2)}, u32[]{:S(2)}) collective-permute-start(bf16[4,128,512]{2,1,0:T(8,128)(2,1)S(1)} %get-tuple-element.67), channel_id=1, source_target_pairs={{0,4},{2,6},{4,0},{6,2},{1,5},{3,7},{5,1},{7,3},{8,12},{10,14},{12... | collective-permute-start | bytes 1572872 | tf_op jit(solution)/shard_map/ppermute | solution.py:19
  27.4 8.0 %collective-permute-done.12.r1 = bf16[4,128,512]{2,1,0:T(8,128)(2,1)S(1)} collective-permute-done((bf16[4,128,512]{2,1,0:T(8,128)(2,1)S(1)}, bf16[4,128,512]{2,1,0:T(8,128)(2,1)S(1)}, u32[]{:S(2)}, u32[]{:S(2)}) %collective-permute-start.12) | collective-permute-done | bytes 524320 | tf_op jit(solution)/shard_map/ppermute | solution.py:19
  35.4 2.7 %collective-permute-start.20 = (bf16[4,128,512]{2,1,0:T(8,128)(2,1)S(1)}, bf16[4,128,512]{2,1,0:T(8,128)(2,1)S(1)}, u32[]{:S(2)}, u32[]{:S(2)}) collective-permute-start(bf16[4,128,512]{2,1,0:T(8,128)(2,1)S(1)} %get-tuple-element.75), channel_id=1, source_target_pairs={{0,8},{128,136},{8,0},{136,128},{1,9},{129,137},{9,1},{137,129},{2... | collective-permute-start | bytes 1572872 | tf_op jit(solution)/shard_map/ppermute | solution.py:31
  38.3 6.5 %collective-permute-done.13.r2 = bf16[4,128,512]{2,1,0:T(8,128)(2,1)S(1)} collective-permute-done((bf16[4,128,512]{2,1,0:T(8,128)(2,1)S(1)}, bf16[4,128,512]{2,1,0:T(8,128)(2,1)S(1)}, u32[]{:S(2)}, u32[]{:S(2)}) %collective-permute-start.13) | collective-permute-done | bytes 524320 | tf_op jit(solution)/shard_map/ppermute | solution.py:19
  44.8 4.2 %collective-permute-done.14.r3 = bf16[4,128,512]{2,1,0:T(8,128)(2,1)S(1)} collective-permute-done((bf16[4,128,512]{2,1,0:T(8,128)(2,1)S(1)}, bf16[4,128,512]{2,1,0:T(8,128)(2,1)S(1)}, u32[]{:S(2)}, u32[]{:S(2)}) %collective-permute-start.14) | collective-permute-done | bytes 524320 | tf_op jit(solution)/shard_map/ppermute | solution.py:19
  51.4 3.6 %collective-permute-start.17 = (bf16[128,512]{1,0:T(8,128)(2,1)S(1)}, bf16[128,512]{1,0:T(8,128)(2,1)S(1)}, u32[]{:S(2)}, u32[]{:S(2)}) collective-permute-start(bf16[128,512]{1,0:T(8,128)(2,1)S(1)} %get-tuple-element.71), channel_id=1, source_target_pairs={{0,8},{128,136},{8,0},{136,128},{1,9},{129,137},{9,1},{137,129},{2... | collective-permute-start | bytes 393224 | tf_op jit(solution)/shard_map/ppermute | solution.py:31
  56.6 2.0 %collective-permute-start.22 = (bf16[128,512]{1,0:T(8,128)(2,1)S(1)}, bf16[128,512]{1,0:T(8,128)(2,1)S(1)}, u32[]{:S(2)}, u32[]{:S(2)}) collective-permute-start(bf16[128,512]{1,0:T(8,128)(2,1)S(1)} %get-tuple-element.78), channel_id=1, source_target_pairs={{0,6},{2,0},{4,2},{6,4},{1,7},{3,1},{5,3},{7,5},{8,14},{10,8},{12,... | collective-permute-start | bytes 393224 | tf_op jit(solution)/shard_map/ppermute | solution.py:19
  59.5 1.7 %collective-permute-start.6 = (bf16[384,1024]{1,0:T(8,128)(2,1)S(1)}, bf16[384,1024]{1,0:T(8,128)(2,1)S(1)}, u32[]{:S(2)}, u32[]{:S(2)}) collective-permute-start(bf16[384,1024]{1,0:T(8,128)(2,1)S(1)} %get-tuple-element.88), channel_id=1, source_target_pairs={{0,6},{2,0},{4,2},{6,4},{1,7},{3,1},{5,3},{7,5},{8,14},{10,8},{12,... | collective-permute-start | bytes 2359304 | tf_op jit(solution)/shard_map/ppermute | solution.py:19
  61.3 6.5 %collective-permute-done.21.b1 = bf16[128,512]{1,0:T(8,128)(2,1)S(1)} collective-permute-done((bf16[128,512]{1,0:T(8,128)(2,1)S(1)}, bf16[128,512]{1,0:T(8,128)(2,1)S(1)}, u32[]{:S(2)}, u32[]{:S(2)}) %collective-permute-start.21) | collective-permute-done | bytes 131104 | tf_op jit(solution)/shard_map/ppermute | solution.py:19
  69.9 2.0 %collective-permute-start.24 = (bf16[64,1024]{1,0:T(8,128)(2,1)S(1)}, bf16[64,1024]{1,0:T(8,128)(2,1)S(1)}, u32[]{:S(2)}, u32[]{:S(2)}) collective-permute-start(bf16[64,1024]{1,0:T(8,128)(2,1)S(1)} %get-tuple-element.81), channel_id=1, source_target_pairs={{0,16},{16,0},{32,48},{48,32},{64,80},{80,64},{96,112},{112,96},{1... | collective-permute-start | bytes 393224 | tf_op jit(solution)/shard_map/ppermute | solution.py:366
  71.9 4.6 %shard_map.94 = (bf16[256,4096]{1,0:T(8,128)(2,1)}, bf16[256,1024]{1,0:T(8,128)(2,1)S(1)}, f32[512,1024]{1,0:T(8,128)S(1)}, f32[1,5120]{1,0:T(1,128)S(1)}) custom-call(s32[4]{0:T(128)S(1)} %pad_add_fusion.pos, bf16[256,4096]{1,0:T(8,128)(2,1)S(1)} %copy-done.1, bf16[256,2048]{1,0:T(8,128)(2,1)S(1)} %collective-permute-done.tok_other, ...), custom_call_target="tpu_custom_call" | custom-call | flops 2147483648 | bytes 10485760 | tf_op jit(solution)/shard_map/pallas_call | solution.py:269
  76.6 6.5 %collective-permute-start.27 = (bf16[64,1024]{1,0:T(8,128)(2,1)S(1)}, bf16[64,1024]{1,0:T(8,128)(2,1)S(1)}, u32[]{:S(2)}, u32[]{:S(2)}) collective-permute-start(bf16[64,1024]{1,0:T(8,128)(2,1)S(1)} %add_convert_fusion.1), channel_id=1, source_target_pairs={{0,96},{16,112},{32,0},{48,16},{64,32},{80,48},{96,64},{112,80},{1... | collective-permute-start | bytes 393224 | tf_op jit(solution)/shard_map/ppermute | solution.py:23
  83.1 4.0 %collective-permute-start.25 = (bf16[64,1024]{1,0:T(8,128)(2,1)S(1)}, bf16[64,1024]{1,0:T(8,128)(2,1)S(1)}, u32[]{:S(2)}, u32[]{:S(2)}) collective-permute-start(bf16[64,1024]{1,0:T(8,128)(2,1)S(1)} %add_convert_fusion.1), channel_id=1, source_target_pairs={{0,64},{16,80},{32,96},{48,112},{64,0},{80,16},{96,32},{112,48},{1... | collective-permute-start | bytes 393224 | tf_op jit(solution)/shard_map/ppermute | solution.py:23
  87.3 3.3 %collective-permute-start.8 = (bf16[128,1024]{1,0:T(8,128)(2,1)S(1)}, bf16[128,1024]{1,0:T(8,128)(2,1)S(1)}, u32[]{:S(2)}, u32[]{:S(2)}) collective-permute-start(bf16[128,1024]{1,0:T(8,128)(2,1)S(1)} %get-tuple-element.85), channel_id=1, source_target_pairs={{0,6},{2,0},{4,2},{6,4},{1,7},{3,1},{5,3},{7,5},{8,14},{10,8},{12,... | collective-permute-start | bytes 786440 | tf_op jit(solution)/shard_map/ppermute | solution.py:19
  90.7 4.9 %collective-permute-done.25 = bf16[64,1024]{1,0:T(8,128)(2,1)S(1)} collective-permute-done((bf16[64,1024]{1,0:T(8,128)(2,1)S(1)}, bf16[64,1024]{1,0:T(8,128)(2,1)S(1)}, u32[]{:S(2)}, u32[]{:S(2)}) %collective-permute-start.25) | collective-permute-done | bytes 131104 | tf_op jit(solution)/shard_map/ppermute | solution.py:23
  97.0 2.2 %collective-permute-start.29 = (bf16[64,1024]{1,0:T(8,128)(2,1)S(1)}, bf16[64,1024]{1,0:T(8,128)(2,1)S(1)}, u32[]{:S(2)}, u32[]{:S(2)}) collective-permute-start(bf16[64,1024]{1,0:T(8,128)(2,1)S(1)} %add_convert_fusion.own), channel_id=1, source_target_pairs={{0,128},{128,0},{8,136},{136,8},{1,129},{129,1},{9,137},{137,9},{2... | collective-permute-start | bytes 393224 | tf_op jit(solution)/shard_map/ppermute | solution.py:35
  100.7 4.8 %shard_map.95 = (bf16[256,4096]{1,0:T(8,128)(2,1)}, bf16[256,1024]{1,0:T(8,128)(2,1)S(1)}, f32[256,1024]{1,0:T(8,128)S(1)}, bf16[256,1024]{1,0:T(8,128)(2,1)S(1)}, f32[1,5120]{1,0:T(1,128)S(1)}) custom-call(s32[4]{0:T(128)S(1)} %pad_add_fusion.pos, bf16[256,4096]{1,0:T(8,128)(2,1)S(1)} %copy-done.1, ...), custom_call_target="tpu_custom_call", output_to_operand_aliasing={{0}: (13, {})} | custom-call | flops 2147483648 | bytes 10485760 | tf_op jit(solution)/shard_map/pallas_call | solution.py:269
  106.8 5.3 %collective-permute-done.32 = f32[1,5120]{1,0:T(1,128)S(1)} collective-permute-done((f32[1,5120]{1,0:T(1,128)S(1)}, f32[1,5120]{1,0:T(1,128)S(1)}, u32[]{:S(2)}, u32[]{:S(2)}) %collective-permute-start.32) | collective-permute-done | bytes 20512 | tf_op jit(solution)/shard_map/ppermute | solution.py:19
  112.2 3.8 %collective-permute-done.33 = f32[1,5120]{1,0:T(1,128)S(1)} collective-permute-done((f32[1,5120]{1,0:T(1,128)S(1)}, f32[1,5120]{1,0:T(1,128)S(1)}, u32[]{:S(2)}, u32[]{:S(2)}) %collective-permute-start.33) | collective-permute-done | bytes 20512 | tf_op jit(solution)/shard_map/ppermute | solution.py:373
  119.5 1.9 %collective-permute-done.34 = f32[1,5120]{1,0:T(1,128)S(1)} collective-permute-done((f32[1,5120]{1,0:T(1,128)S(1)}, f32[1,5120]{1,0:T(1,128)S(1)}, u32[]{:S(2)}, u32[]{:S(2)}) %collective-permute-start.34) | collective-permute-done | bytes 20512 | tf_op jit(solution)/shard_map/ppermute | solution.py:374
  123.5 3.6 %shard_map.96 = bf16[256,4096]{1,0:T(8,128)(2,1)} custom-call(s32[4]{0:T(128)S(1)} %pad_add_fusion.pos, bf16[256,1024]{1,0:T(8,128)(2,1)S(1)} %collective-permute-done.10.first, bf16[256,1024]{1,0:T(8,128)(2,1)S(1)} %collective-permute-done.11.second, bf16[256,4096]{1,0:T(8,128)(2,1)} %get-tuple-element.63._), custom_call_target="tpu_custom_call", output_to_operand_aliasing={{}: (3, {})} | custom-call | bytes 2097152 | tf_op jit(solution)/shard_map/pallas_call | solution.py:304
  (86 shorter events, 30.4 us)
Async XLA Ops:
  4.0 15.2 %collective-permute-start.3 = (bf16[256,1024]{1,0:T(8,128)(2,1)S(1)}, bf16[256,1024]{1,0:T(8,128)(2,1)S(1)}, u32[]{:S(2)}, u32[]{:S(2)}) collective-permute-start(bf16[256,1024]{1,0:T(8,128)(2,1)S(1)} %copy-done.5), channel_id=1, source_target_pairs={{0,2},{2,4},{4,6},{6,0},{1,3},{3,5},{5,7},{7,1},{8,10},{10,12},{12... | collective-permute-start | bytes 1572872 | tf_op jit(solution)/shard_map/ppermute | solution.py:19
  5.6 13.7 %collective-permute-start.2 = (bf16[256,1024]{1,0:T(8,128)(2,1)S(1)}, bf16[256,1024]{1,0:T(8,128)(2,1)S(1)}, u32[]{:S(2)}, u32[]{:S(2)}) collective-permute-start(bf16[256,1024]{1,0:T(8,128)(2,1)S(1)} %copy-done.5), channel_id=1, source_target_pairs={{0,136},{128,8},{8,128},{136,0},{1,137},{129,9},{9,129},{137,1},{2... | collective-permute-start | bytes 1572872 | tf_op jit(solution)/shard_map/ppermute | solution.py:35
  7.1 13.4 %collective-permute-start.4 = (bf16[256,1024]{1,0:T(8,128)(2,1)S(1)}, bf16[256,1024]{1,0:T(8,128)(2,1)S(1)}, u32[]{:S(2)}, u32[]{:S(2)}) collective-permute-start(bf16[256,1024]{1,0:T(8,128)(2,1)S(1)} %copy-done.5), channel_id=1, source_target_pairs={{0,6},{2,0},{4,2},{6,4},{1,7},{3,1},{5,3},{7,5},{8,14},{10,8},{12,... | collective-permute-start | bytes 1572872 | tf_op jit(solution)/shard_map/ppermute | solution.py:19
  20.4 14.9 %collective-permute-start.12 = (bf16[4,128,512]{2,1,0:T(8,128)(2,1)S(1)}, bf16[4,128,512]{2,1,0:T(8,128)(2,1)S(1)}, u32[]{:S(2)}, u32[]{:S(2)}) collective-permute-start(bf16[4,128,512]{2,1,0:T(8,128)(2,1)S(1)} %get-tuple-element.65), channel_id=1, source_target_pairs={{0,2},{2,4},{4,6},{6,0},{1,3},{3,5},{5,7},{7,1},{8,10},{10,12},{12... | collective-permute-start | bytes 1572872 | tf_op jit(solution)/shard_map/ppermute | solution.py:19
  22.0 22.8 %collective-permute-start.13 = (bf16[4,128,512]{2,1,0:T(8,128)(2,1)S(1)}, bf16[4,128,512]{2,1,0:T(8,128)(2,1)S(1)}, u32[]{:S(2)}, u32[]{:S(2)}) collective-permute-start(bf16[4,128,512]{2,1,0:T(8,128)(2,1)S(1)} %get-tuple-element.66), channel_id=1, source_target_pairs={{0,6},{2,0},{4,2},{6,4},{1,7},{3,1},{5,3},{7,5},{8,14},{10,8},{12,... | collective-permute-start | bytes 1572872 | tf_op jit(solution)/shard_map/ppermute | solution.py:19
  23.7 25.3 %collective-permute-start.14 = (bf16[4,128,512]{2,1,0:T(8,128)(2,1)S(1)}, bf16[4,128,512]{2,1,0:T(8,128)(2,1)S(1)}, u32[]{:S(2)}, u32[]{:S(2)}) collective-permute-start(bf16[4,128,512]{2,1,0:T(8,128)(2,1)S(1)} %get-tuple-element.67), channel_id=1, source_target_pairs={{0,4},{2,6},{4,0},{6,2},{1,5},{3,7},{5,1},{7,3},{8,12},{10,14},{12... | collective-permute-start | bytes 1572872 | tf_op jit(solution)/shard_map/ppermute | solution.py:19
  25.4 24.5 %collective-permute-start.18 = (bf16[4,128,512]{2,1,0:T(8,128)(2,1)S(1)}, bf16[4,128,512]{2,1,0:T(8,128)(2,1)S(1)}, u32[]{:S(2)}, u32[]{:S(2)}) collective-permute-start(bf16[4,128,512]{2,1,0:T(8,128)(2,1)S(1)} %get-tuple-element.73), channel_id=1, source_target_pairs={{0,128},{128,8},{8,136},{136,0},{1,129},{129,9},{9,137},{137,1},{2... | collective-permute-start | bytes 1572872 | tf_op jit(solution)/shard_map/ppermute | solution.py:31
  25.9 25.5 %collective-permute-start.19 = (bf16[4,128,512]{2,1,0:T(8,128)(2,1)S(1)}, bf16[4,128,512]{2,1,0:T(8,128)(2,1)S(1)}, u32[]{:S(2)}, u32[]{:S(2)}) collective-permute-start(bf16[4,128,512]{2,1,0:T(8,128)(2,1)S(1)} %get-tuple-element.74), channel_id=1, source_target_pairs={{0,136},{128,0},{8,128},{136,8},{1,137},{129,1},{9,129},{137,9},{2... | collective-permute-start | bytes 1572872 | tf_op jit(solution)/shard_map/ppermute | solution.py:31
  35.4 19.6 %collective-permute-start.20 = (bf16[4,128,512]{2,1,0:T(8,128)(2,1)S(1)}, bf16[4,128,512]{2,1,0:T(8,128)(2,1)S(1)}, u32[]{:S(2)}, u32[]{:S(2)}) collective-permute-start(bf16[4,128,512]{2,1,0:T(8,128)(2,1)S(1)} %get-tuple-element.75), channel_id=1, source_target_pairs={{0,8},{128,136},{8,0},{136,128},{1,9},{129,137},{9,1},{137,129},{2... | collective-permute-start | bytes 1572872 | tf_op jit(solution)/shard_map/ppermute | solution.py:31
  44.8 42.2 %collective-permute-start.5 = (bf16[384,1024]{1,0:T(8,128)(2,1)S(1)}, bf16[384,1024]{1,0:T(8,128)(2,1)S(1)}, u32[]{:S(2)}, u32[]{:S(2)}) collective-permute-start(bf16[384,1024]{1,0:T(8,128)(2,1)S(1)} %get-tuple-element.87), channel_id=1, source_target_pairs={{0,2},{2,4},{4,6},{6,0},{1,3},{3,5},{5,7},{7,1},{8,10},{10,12},{12... | collective-permute-start | bytes 2359304 | tf_op jit(solution)/shard_map/ppermute | solution.py:19
  49.9 8.7 %collective-permute-start.16 = (bf16[128,512]{1,0:T(8,128)(2,1)S(1)}, bf16[128,512]{1,0:T(8,128)(2,1)S(1)}, u32[]{:S(2)}, u32[]{:S(2)}) collective-permute-start(bf16[128,512]{1,0:T(8,128)(2,1)S(1)} %get-tuple-element.70), channel_id=1, source_target_pairs={{0,136},{128,0},{8,128},{136,8},{1,137},{129,1},{9,129},{137,9},{2... | collective-permute-start | bytes 393224 | tf_op jit(solution)/shard_map/ppermute | solution.py:31
  51.4 8.2 %collective-permute-start.17 = (bf16[128,512]{1,0:T(8,128)(2,1)S(1)}, bf16[128,512]{1,0:T(8,128)(2,1)S(1)}, u32[]{:S(2)}, u32[]{:S(2)}) collective-permute-start(bf16[128,512]{1,0:T(8,128)(2,1)S(1)} %get-tuple-element.71), channel_id=1, source_target_pairs={{0,8},{128,136},{8,0},{136,128},{1,9},{129,137},{9,1},{137,129},{2... | collective-permute-start | bytes 393224 | tf_op jit(solution)/shard_map/ppermute | solution.py:31
  55.3 12.5 %collective-permute-start.21 = (bf16[128,512]{1,0:T(8,128)(2,1)S(1)}, bf16[128,512]{1,0:T(8,128)(2,1)S(1)}, u32[]{:S(2)}, u32[]{:S(2)}) collective-permute-start(bf16[128,512]{1,0:T(8,128)(2,1)S(1)} %get-tuple-element.77), channel_id=1, source_target_pairs={{0,2},{2,4},{4,6},{6,0},{1,3},{3,5},{5,7},{7,1},{8,10},{10,12},{12... | collective-permute-start | bytes 393224 | tf_op jit(solution)/shard_map/ppermute | solution.py:19
  56.6 11.2 %collective-permute-start.22 = (bf16[128,512]{1,0:T(8,128)(2,1)S(1)}, bf16[128,512]{1,0:T(8,128)(2,1)S(1)}, u32[]{:S(2)}, u32[]{:S(2)}) collective-permute-start(bf16[128,512]{1,0:T(8,128)(2,1)S(1)} %get-tuple-element.78), channel_id=1, source_target_pairs={{0,6},{2,0},{4,2},{6,4},{1,7},{3,1},{5,3},{7,5},{8,14},{10,8},{12,... | collective-permute-start | bytes 393224 | tf_op jit(solution)/shard_map/ppermute | solution.py:19
  58.6 10.6 %collective-permute-start.23 = (bf16[128,512]{1,0:T(8,128)(2,1)S(1)}, bf16[128,512]{1,0:T(8,128)(2,1)S(1)}, u32[]{:S(2)}, u32[]{:S(2)}) collective-permute-start(bf16[128,512]{1,0:T(8,128)(2,1)S(1)} %get-tuple-element.79), channel_id=1, source_target_pairs={{0,4},{2,6},{4,0},{6,2},{1,5},{3,7},{5,1},{7,3},{8,12},{10,14},{12... | collective-permute-start | bytes 393224 | tf_op jit(solution)/shard_map/ppermute | solution.py:19
  59.5 27.7 %collective-permute-start.6 = (bf16[384,1024]{1,0:T(8,128)(2,1)S(1)}, bf16[384,1024]{1,0:T(8,128)(2,1)S(1)}, u32[]{:S(2)}, u32[]{:S(2)}) collective-permute-start(bf16[384,1024]{1,0:T(8,128)(2,1)S(1)} %get-tuple-element.88), channel_id=1, source_target_pairs={{0,6},{2,0},{4,2},{6,4},{1,7},{3,1},{5,3},{7,5},{8,14},{10,8},{12,... | collective-permute-start | bytes 2359304 | tf_op jit(solution)/shard_map/ppermute | solution.py:19
  76.6 14.1 %collective-permute-start.27 = (bf16[64,1024]{1,0:T(8,128)(2,1)S(1)}, bf16[64,1024]{1,0:T(8,128)(2,1)S(1)}, u32[]{:S(2)}, u32[]{:S(2)}) collective-permute-start(bf16[64,1024]{1,0:T(8,128)(2,1)S(1)} %add_convert_fusion.1), channel_id=1, source_target_pairs={{0,96},{16,112},{32,0},{48,16},{64,32},{80,48},{96,64},{112,80},{1... | collective-permute-start | bytes 393224 | tf_op jit(solution)/shard_map/ppermute | solution.py:23
  83.1 7.6 %collective-permute-start.26 = (bf16[64,1024]{1,0:T(8,128)(2,1)S(1)}, bf16[64,1024]{1,0:T(8,128)(2,1)S(1)}, u32[]{:S(2)}, u32[]{:S(2)}) collective-permute-start(bf16[64,1024]{1,0:T(8,128)(2,1)S(1)} %add_convert_fusion.1), channel_id=1, source_target_pairs={{0,32},{16,48},{32,64},{48,80},{64,96},{80,112},{96,0},{112,16},{1... | collective-permute-start | bytes 393224 | tf_op jit(solution)/shard_map/ppermute | solution.py:23
  83.1 12.5 %collective-permute-start.25 = (bf16[64,1024]{1,0:T(8,128)(2,1)S(1)}, bf16[64,1024]{1,0:T(8,128)(2,1)S(1)}, u32[]{:S(2)}, u32[]{:S(2)}) collective-permute-start(bf16[64,1024]{1,0:T(8,128)(2,1)S(1)} %add_convert_fusion.1), channel_id=1, source_target_pairs={{0,64},{16,80},{32,96},{48,112},{64,0},{80,16},{96,32},{112,48},{1... | collective-permute-start | bytes 393224 | tf_op jit(solution)/shard_map/ppermute | solution.py:23
  87.1 13.5 %collective-permute-start.7 = (bf16[128,1024]{1,0:T(8,128)(2,1)S(1)}, bf16[128,1024]{1,0:T(8,128)(2,1)S(1)}, u32[]{:S(2)}, u32[]{:S(2)}) collective-permute-start(bf16[128,1024]{1,0:T(8,128)(2,1)S(1)} %get-tuple-element.83), channel_id=1, source_target_pairs={{0,2},{2,4},{4,6},{6,0},{1,3},{3,5},{5,7},{7,1},{8,10},{10,12},{12... | collective-permute-start | bytes 786440 | tf_op jit(solution)/shard_map/ppermute | solution.py:19
  87.3 13.4 %collective-permute-start.8 = (bf16[128,1024]{1,0:T(8,128)(2,1)S(1)}, bf16[128,1024]{1,0:T(8,128)(2,1)S(1)}, u32[]{:S(2)}, u32[]{:S(2)}) collective-permute-start(bf16[128,1024]{1,0:T(8,128)(2,1)S(1)} %get-tuple-element.85), channel_id=1, source_target_pairs={{0,6},{2,0},{4,2},{6,4},{1,7},{3,1},{5,3},{7,5},{8,14},{10,8},{12,... | collective-permute-start | bytes 786440 | tf_op jit(solution)/shard_map/ppermute | solution.py:19
  95.7 21.6 %collective-permute-start.30 = (bf16[64,1024]{1,0:T(8,128)(2,1)S(1)}, bf16[64,1024]{1,0:T(8,128)(2,1)S(1)}, u32[]{:S(2)}, u32[]{:S(2)}) collective-permute-start(bf16[64,1024]{1,0:T(8,128)(2,1)S(1)} %add_convert_fusion.own), channel_id=1, source_target_pairs={{0,144},{16,128},{32,176},{48,160},{64,208},{80,192},{96,240},{112... | collective-permute-start | bytes 393224 | tf_op jit(solution)/shard_map/ppermute | solution.py:380
  97.0 20.8 %collective-permute-start.29 = (bf16[64,1024]{1,0:T(8,128)(2,1)S(1)}, bf16[64,1024]{1,0:T(8,128)(2,1)S(1)}, u32[]{:S(2)}, u32[]{:S(2)}) collective-permute-start(bf16[64,1024]{1,0:T(8,128)(2,1)S(1)} %add_convert_fusion.own), channel_id=1, source_target_pairs={{0,128},{128,0},{8,136},{136,8},{1,129},{129,1},{9,137},{137,9},{2... | collective-permute-start | bytes 393224 | tf_op jit(solution)/shard_map/ppermute | solution.py:35
  99.3 18.6 %collective-permute-start.28 = (bf16[64,1024]{1,0:T(8,128)(2,1)S(1)}, bf16[64,1024]{1,0:T(8,128)(2,1)S(1)}, u32[]{:S(2)}, u32[]{:S(2)}) collective-permute-start(bf16[64,1024]{1,0:T(8,128)(2,1)S(1)} %add_convert_fusion.own), channel_id=1, source_target_pairs={{0,16},{16,0},{32,48},{48,32},{64,80},{80,64},{96,112},{112,96},{1... | collective-permute-start | bytes 393224 | tf_op jit(solution)/shard_map/ppermute | solution.py:366
  (17 other events, 100.9 us)

commit v2 on v1

--- a/solution.py
+++ b/solution.py
@@ -47,27 +47,39 @@
     return pl.CostEstimate(flops=flops, bytes_accessed=bytes_accessed, transcendentals=0)
 
 
-def copy_body(pos, src, dst):
-    dst[...] = src[...]
+ANY = pl.BlockSpec(memory_space=pl.ANY)
+SCALARS = pl.BlockSpec(memory_space=pltpu.SMEM)
+
+
+def pick_body(pos, src, out, sems):
+    copies = [
+        pltpu.make_async_copy(
+            src.at[:, pl.ds(pl.multiple_of((2 * j + 1 - pos[2]) * PIECE, PIECE), PIECE)],
+            out.at[:, j * PIECE : (j + 1) * PIECE],
+            sems.at[j],
+        )
+        for j in range(8)
+    ]
+    for copy in copies:
+        copy.start()
+    for copy in copies:
+        copy.wait()
 
 
 def other_half(pos, tokens):
     return pl.pallas_call(
-        copy_body,
+        pick_body,
         out_shape=jax.ShapeDtypeStruct((ROWS, DEPTH // 2), BF16),
-        grid_spec=pltpu.PrefetchScalarGridSpec(
-            num_scalar_prefetch=1,
-            grid=(8,),
-            in_specs=[pl.BlockSpec((ROWS, PIECE), lambda j, pos: (0, 2 * j + 1 - pos[2]))],
-            out_specs=pl.BlockSpec((ROWS, PIECE), lambda j, pos: (0, j)),
-        ),
+        in_specs=[SCALARS, ANY],
+        out_specs=ANY,
+        scratch_shapes=[pltpu.SemaphoreType.DMA((8,))],
         compiler_params=PARAMS,
         cost_estimate=cost(0, 2**21),
     )(pos, tokens)
 
 
-def partial_body(pos, tok, tok_other, cot, cot_other, in_scale, out_scale, grad_ref, *outs):
-    a_refs, b_refs = outs[:4], outs[4:]
+def partial_body(pos, tok, tok_other, cot, cot_other, in_scale, out_scale, grad_ref, *refs):
+    stay, plus, minus, two_low, two_high, left = refs
     i = pl.program_id(0)
 
     @pl.when(i == 0)
@@ -82,25 +94,25 @@
         wide = pl.ds(pl.multiple_of(((place * 2 + pos[2]) * 2 + x_at % 2) * LANE, LANE), LANE)
         narrow = pl.ds(pl.multiple_of((place * 2 + x_at % 2) * LANE, LANE), LANE)
         scale = in_scale[:, wide]
-        first = (tok[:, wide].astype(F32) * scale).astype(BF16)
-        second = (tok_other[:, narrow].astype(F32) * scale).astype(BF16)
-        dims = (((0,), (0,)), ((), ()))
-        part = lax.dot_general(first, grad_ref[:ROWS], dims, preferred_element_type=F32)
-        part = part + lax.dot_general(second, grad_ref[ROWS:], dims, preferred_element_type=F32)
-        part = part.astype(BF16)
-        b_refs[k][0] = part[:, HALF:]
-        for m in range(4):
-            @pl.when(i == m)
-            def _():
-                a_refs[m][k] = part[:, :HALF]
+        left[:ROWS, k * LANE : (k + 1) * LANE] = (tok[:, wide].astype(F32) * scale).astype(BF16)
+        left[ROWS:, k * LANE : (k + 1) * LANE] = (tok_other[:, narrow].astype(F32) * scale).astype(BF16)
+    part = lax.dot_general(
+        left[...], grad_ref[...], (((0,), (0,)), ((), ())), preferred_element_type=F32
+    ).astype(BF16)
+    stay[0] = part[:LANE]
+    plus[0] = part[LANE : 2 * LANE]
+    two_low[0] = part[2 * LANE : 3 * LANE, :HALF]
+    two_high[0] = part[2 * LANE : 3 * LANE, HALF:]
+    minus[0] = part[3 * LANE :]
 
 
 def partials(pos, tokens, tok_other, cot, cot_other, in_scale, out_scale):
     whole = lambda shape: pl.BlockSpec(shape, lambda i, pos: (0,) * len(shape))
-    block = jax.ShapeDtypeStruct((4, LANE, HALF), BF16)
-    outs = pl.pallas_call(
+    columns = (WIDTH, WIDTH, WIDTH, HALF, HALF)
+    return pl.pallas_call(
         partial_body,
-        out_shape=[jax.ShapeDtypeStruct((2 * ROWS, WIDTH), BF16)] + [block] * 8,
+        out_shape=[jax.ShapeDtypeStruct((2 * ROWS, WIDTH), BF16)]
+        + [jax.ShapeDtypeStruct((4, LANE, n), BF16) for n in columns],
         grid_spec=pltpu.PrefetchScalarGridSpec(
             num_scalar_prefetch=1,
             grid=(4,),
@@ -109,55 +121,72 @@
                 whole((ROWS, WIDTH)), whole((1, DEPTH)), whole((1, WIDTH)),
             ],
             out_specs=[whole((2 * ROWS, WIDTH))]
-            + [whole((4, LANE, HALF))] * 4
-            + [pl.BlockSpec((1, LANE, HALF), lambda i, pos: (i, 0, 0))] * 4,
+            + [pl.BlockSpec((1, LANE, n), lambda i, pos: (i, 0, 0)) for n in columns],
+            scratch_shapes=[pltpu.VMEM((2 * ROWS, 4 * LANE), BF16)],
         ),
         compiler_params=PARAMS,
         cost_estimate=cost(2 * 2 * ROWS * DEPTH // 2 * WIDTH, 9 * 2**20),
     )(pos, tokens, tok_other, cot, cot_other, in_scale, out_scale)
-    return outs[0], outs[1:5], outs[5:]
-
-
-def sum_body(own, r1, r2, r3, keep, s1, s2, s3):
+
+
+def add_body(plus, minus, low, high, plus_out, minus_out):
+    plus_out[...] = (plus[...].astype(F32) + low[...].astype(F32)).astype(BF16)
+    minus_out[...] = (minus[...].astype(F32) + high[...].astype(F32)).astype(BF16)
+
+
+def add_halves(plus, minus, low, high):
+    block = (4, LANE, HALF)
+    first, second = pl.BlockSpec(block, lambda i: (0, 0, 0)), pl.BlockSpec(block, lambda i: (0, 0, 1))
+    return pl.pallas_call(
+        add_body,
+        out_shape=[jax.ShapeDtypeStruct((4, LANE, WIDTH), BF16)] * 2,
+        grid=(1,),
+        in_specs=[first, second, first, first],
+        out_specs=[first, second],
+        input_output_aliases={0: 0, 1: 1},
+        compiler_params=PARAMS,
+        cost_estimate=cost(2**20, 3 * 2**20),
+    )(plus, minus, low, high)
+
+
+def sum_body(own, r1, r2, keep, s1, s2, s3):
     for k, out in enumerate((keep, s1, s2, s3)):
-        total = own[k].astype(F32) + r1[k].astype(F32) + r2[k].astype(F32) + r3[k].astype(F32)
-        out[...] = total.astype(out.dtype)
+        out[...] = (own[k].astype(F32) + r1[k].astype(F32) + r2[k].astype(F32)).astype(out.dtype)
 
 
 def sum_blocks(own, arrived):
-    shape = (LANE, HALF)
+    shape = own.shape[1:]
     return pl.pallas_call(
         sum_body,
         out_shape=[jax.ShapeDtypeStruct(shape, F32)] + [jax.ShapeDtypeStruct(shape, BF16)] * 3,
-        in_specs=[VMEM] * 4,
+        in_specs=[VMEM] * 3,
         out_specs=[VMEM] * 4,
         compiler_params=PARAMS,
-        cost_estimate=cost(2**20, 5 * 2**19),
+        cost_estimate=cost(2**20, 4 * 2**20),
     )(own, *arrived)
 
 
-def join_body(pos, a0, a1, a2, a3, b0, b1, b2, b3, keep, send):
+def join_body(pos, own, r1, r2, r3, keep, send):
     count = LANE // 2
     mine = pos[3] % 2
     for out, at in ((keep, mine), (send, 1 - mine)):
         rows = pl.ds(pl.multiple_of(at * count, count), count)
-        for side, refs in ((0, (a0, a1, a2, a3)), (1, (b0, b1, b2, b3))):
-            total = refs[0][rows]
-            for ref in refs[1:]:
-                total = total + ref[rows].astype(F32)
-            out[:, side * HALF : (side + 1) * HALF] = total.astype(out.dtype)
-
-
-def join(pos, a, b):
+        total = own[rows]
+        for ref in (r1, r2, r3):
+            total = total + ref[rows].astype(F32)
+        out[...] = total.astype(out.dtype)
+
+
+def join(pos, own, arrived):
     shape = (LANE // 2, WIDTH)
     return pl.pallas_call(
         join_body,
         out_shape=[jax.ShapeDtypeStruct(shape, F32), jax.ShapeDtypeStruct(shape, BF16)],
-        in_specs=[pl.BlockSpec(memory_space=pltpu.SMEM)] + [VMEM] * 8,
+        in_specs=[SCALARS] + [VMEM] * 4,
         out_specs=[VMEM] * 2,
         compiler_params=PARAMS,
         cost_estimate=cost(2**20, 2**21),
-    )(pos, *a, *b)
+    )(pos, own, *arrived)
 
 
 def place_body(scale, pos, own, by_z, by_x, by_both, out):
@@ -172,7 +201,7 @@
     return pl.pallas_call(
         functools.partial(place_body, scale),
         out_shape=jax.ShapeDtypeStruct((PIECE, WIDTH), F32),
-        in_specs=[pl.BlockSpec(memory_space=pltpu.SMEM)] + [VMEM] * 4,
+        in_specs=[SCALARS] + [VMEM] * 4,
         out_specs=VMEM,
         compiler_params=PARAMS,
         cost_estimate=cost(2**18, 2**20),
@@ -279,45 +308,50 @@
     )(pos, *operands)
 
 
-def fill_body(pos, first, second, _, out):
-    j = pl.program_id(0)
-
-    @pl.when(j < 4)
-    def _():
-        out[...] = first[...]
-
-    @pl.when(j >= 4)
-    def _():
-        out[...] = second[...]
+def fill_body(orders, pos, first, second, _, out, sems):
+    copies = []
+    for b, (order, src) in enumerate(zip(orders, (first, second))):
+        for m, (dxh, dy) in enumerate(order):
+            at = (slice_of(pos, dxh, dy) * 2 + 1 - pos[2]) * PIECE
+            copies.append(pltpu.make_async_copy(
+                src.at[:, m * PIECE : (m + 1) * PIECE],
+                out.at[:, pl.ds(pl.multiple_of(at, PIECE), PIECE)],
+                sems.at[b * 4 + m],
+            ))
+    for copy in copies:
+        copy.start()
+    for copy in copies:
+        copy.wait()
 
 
 def fill(pos, orders, first, second, own):
-    flat = orders[0] + orders[1]
-
-    def column(j, pos):
-        dxh, dy = flat[7]
-        for m in range(7):
-            dxh = jnp.where(j == m, flat[m][0], dxh)
-            dy = jnp.where(j == m, flat[m][1], dy)
-        return 0, slice_of(pos, dxh, dy) * 2 + 1 - pos[2]
-
-    return pl.pallas_call(
-        fill_body,
+    return pl.pallas_call(
+        functools.partial(fill_body, orders),
         out_shape=jax.ShapeDtypeStruct((ROWS, DEPTH), BF16),
-        grid_spec=pltpu.PrefetchScalarGridSpec(
-            num_scalar_prefetch=1,
-            grid=(8,),
-            in_specs=[
-                pl.BlockSpec((ROWS, PIECE), lambda j, pos: (0, jnp.minimum(j, 3))),
-                pl.BlockSpec((ROWS, PIECE), lambda j, pos: (0, jnp.maximum(j, 4) - 4)),
-                pl.BlockSpec(memory_space=pl.ANY),
-            ],
-            out_specs=pl.BlockSpec((ROWS, PIECE), column),
-        ),
+        in_specs=[SCALARS] + [ANY] * 3,
+        out_specs=ANY,
+        scratch_shapes=[pltpu.SemaphoreType.DMA((8,))],
         input_output_aliases={3: 0},
         compiler_params=PARAMS,
         cost_estimate=cost(0, 2**21),
     )(pos, first, second, own)
+
+
+def finish_body(scale, mine, other, in_ref, out_ref):
+    total = (mine[...] + other[...]) * scale
+    in_ref[...] = total[:, :DEPTH]
+    out_ref[...] = total[:, DEPTH:]
+
+
+def finish(mine, other, scale):
+    return pl.pallas_call(
+        functools.partial(finish_body, scale),
+        out_shape=[jax.ShapeDtypeStruct((1, DEPTH), F32), jax.ShapeDtypeStruct((1, WIDTH), F32)],
+        in_specs=[VMEM] * 2,
+        out_specs=[VMEM] * 2,
+        compiler_params=PARAMS,
+        cost_estimate=cost(2**14, 2**16),
+    )(mine, other)
 
 
 def on_device(tokens, cotangent, slow_weight, in_scale, out_scale):
@@ -331,58 +365,69 @@
     far = pairs_x(slow_weight, lambda i: 3 - i)
     tok_other = swap_core(other_half(pos, tokens))
 
-    grad, a_part, b_part = partials(pos, tokens, tok_other, cotangent, cot_other, in_scale, out_scale)
-    far, up, down, a_part, b_part = lax.optimization_barrier((far, up, down, a_part, b_part))
+    grad, stay, plus, minus, two_low, two_high = partials(
+        pos, tokens, tok_other, cotangent, cot_other, in_scale, out_scale
+    )
+    low, high = send_x(two_low, 1), send_x(two_high, -1)
+    far, up, down, grad = lax.optimization_barrier((far, up, down, grad))
 
     half = PIECE // 2
     far_up = send_y(jnp.concatenate([far, up[:half]], axis=0), 1)
     far_down = send_y(jnp.concatenate([far, down[half:]], axis=0), -1)
-    a_in = [send_y(a_part[1], 1), send_y(a_part[3], -1), send_y(a_part[2], 2)]
-    b_in = [send_x(b_part[1], 1), send_x(b_part[3], -1), send_x(b_part[2], 2)]
     orders = ((0, 0), (0, 1), (0, 3), (1, 0)), ((0, 2), (1, 3), (1, 1), (1, 2))
     own, others_1, pre, small = layer(
         pos, orders[0], tokens, tok_other, grad, in_scale, cotangent, cot_other,
         (slow_weight, down, up, far),
     )
+    plus, minus = add_halves(plus, minus, low, high)
+    arrived = [send_x(plus, 1), send_x(minus, -1)]
+    far_up, far_down, own, others_1, pre, small, _ = lax.optimization_barrier(
+        (far_up, far_down, own, others_1, pre, small, plus)
+    )
+
     far_two_up = send_y(far_up[:half], 1)
     far_two_down = send_y(far_down[half:PIECE], -1)
-
-    a_own, *a_out = sum_blocks(a_part[0], a_in)
-    b_own, *b_out = sum_blocks(b_part[0], b_in)
-    b_in = [send_y(b_out[0], 1), send_y(b_out[2], -1), send_y(b_out[1], 2)]
-    a_in = [send_x(a_out[0], 1), send_x(a_out[2], -1), send_x(a_out[1], 2)]
-
     two = jnp.concatenate([far_up[PIECE:], far_down[PIECE:]], axis=0)
     far_two = jnp.concatenate([far_two_up, far_two_down], axis=0)
     own, others_2, pre_own, pre_other, small = layer(
         pos, orders[1], tokens, tok_other, grad, in_scale, cotangent, cot_other,
         (two, far_up[:PIECE], far_down[:PIECE], far_two), (own, pre, small),
     )
+    arrived, own, others_2, pre_own, pre_other, small = lax.optimization_barrier(
+        (arrived, own, others_2, pre_own, pre_other, small)
+    )
+
+    stay, *out = sum_blocks(stay, arrived)
+    arrived = [send_y(out[0], 1), send_y(out[2], -1), send_y(out[1], 2)]
+    small_in = swap_core(small)
     pre_other = swap_core(pre_other)
-    small = small + swap_core(small)
     others_1, others_2 = swap_core(others_1), swap_core(others_2)
-
-    keep, out = join(pos, [a_own, *a_in], [b_own, *b_in])
+    arrived, small_in = lax.optimization_barrier((arrived, small_in))
+
+    keep, out = join(pos, stay, arrived)
     pair = lambda a: lax.ppermute(a, Z, [(i, i ^ 1) for i in range(8)])
-    mine = (keep + pair(out).astype(F32)).astype(BF16)
+    out = pair(out)
+    small = small + small_in
+    small_in = send_y(small, 2)
+    out, small_in = lax.optimization_barrier((out, small_in))
+    mine = (keep + out.astype(F32)).astype(BF16)
     plus, minus, across = send_z(mine, 2), send_z(mine, -2), send_z(mine, 4)
-
-    result = ((pre_own + pre_other.astype(F32)) * out_scale).astype(BF16)
-    grad_tokens = fill(pos, orders, others_1, others_2, own)
-    small = small + send_y(small, 2)
-    small = small + lax.ppermute(small, Y, [(i, i ^ 1) for i in range(4)])
-    small = small + lax.ppermute(small, XH, [(0, 1), (1, 0)])
-
+    small = small + small_in
+    small_in = lax.ppermute(small, Y, [(i, i ^ 1) for i in range(4)])
+    plus, minus, across, small_in = lax.optimization_barrier((plus, minus, across, small_in))
     summed = (mine.astype(F32) + across.astype(F32)) + (plus.astype(F32) + minus.astype(F32))
     summed = summed.astype(BF16)
     by_z = pair(summed)
     by_x = pairs_x(summed, lambda i: i ^ 1)
-    by_both = lax.ppermute(
-        summed, (XL, Z), [(i, i ^ 9) for i in range(16)]
-    )
+    by_both = lax.ppermute(summed, (XL, Z), [(i, i ^ 9) for i in range(16)])
+    small = small + small_in
+    small_far = lax.ppermute(small, XH, [(0, 1), (1, 0)])
+
+    result = ((pre_own + pre_other.astype(F32)) * out_scale).astype(BF16)
+    grad_tokens = fill(pos, orders, others_1, others_2, own)
     grad_weight = place(pos, (summed, by_z, by_x, by_both), total_norm)
-    small = small * member_norm
-    return result, grad_tokens, grad_weight, small[:, :DEPTH], small[:, DEPTH:]
+    grad_in_scale, grad_out_scale = finish(small, small_far, member_norm)
+    return result, grad_tokens, grad_weight, grad_in_scale, grad_out_scale
 
 
 def solution(mesh):

time: 127 us -> 114 us (0.90); the launches traced: 127 us -> 113 us
  starting transfers between devices: 49.6 us -> 39.4 us
  Pallas kernels: 23.6 us -> 19.9 us
    ppermute x6 -> x4, waiting for transfers between devices: 0.02 us -> 14.8 us  [send_x(): lax.ppermute(a, (XL, XH), [(x_index(i), x_index((i + step) % 4)) for i in...]
    ppermute x13 -> x10, waiting for transfers between devices: 36.8 us -> 25.5 us  [send_y(): return lax.ppermute(a, Y, [(i, (i + step) % 4) for i in range(4)])]
    ppermute x6 -> x4, starting transfers between devices: 10.5 us -> 4.13 us  [send_x(): lax.ppermute(a, (XL, XH), [(x_index(i), x_index((i + step) % 4)) for i in...]
    ppermute x2, waiting for transfers between devices: 5.62 us -> 1.35 us  [the longest x1 1.35 us: on_device(): small_far = lax.ppermute(small, XH, [(0, 1), (1, 0)])]
    ppermute x13 -> x10, starting transfers between devices: 17.6 us -> 14.3 us  [send_y(): return lax.ppermute(a, Y, [(i, (i + step) % 4) for i in range(4)])]
    pallas_call x1, Pallas kernels: 6.78 us -> 4.12 us  [partials(): pl.pallas_call(partial_body, out_shape=[jax.ShapeDtypeStruct((2 * ROWS, W...]
    ppermute x2, starting transfers between devices: 3.74 us -> 1.49 us  [pairs_x(): lax.ppermute(a, (XL, XH), [(x_index(i), x_index(other(i))) for i in range...]
    ppermute x1, starting transfers between devices: 1.33 us -> 3.41 us  [on_device(): by_both = lax.ppermute(summed, (XL, Z), [(i, i ^ 9) for i in range(16)])]
  transfers between devices with their start and end apart: 35 -> 30, of which waited for: 12 -> 16; matrix products, arithmetic and copies ran while one was open for 2% -> 1% of each run, Pallas kernels for 15% -> 15%
where the time goes in v2:
time: 114 us; the launch traced here: 113 us
  waiting for transfers between devices  49.4 us (43%)
  starting transfers between devices  39.4 us (35%)
  Pallas kernels  19.9 us (17%)
  local copies, waits for them, and re-layouts  1.92 us (2%)
  other arithmetic  1.39 us (1%)
    ppermute x10, waiting for transfers between devices, send_y(): return lax.ppermute(a, Y, [(i, (i + step) % 4) for i in range(4)])  25.5 us
    ppermute x4, waiting for transfers between devices, send_x(): lax.ppermute(a, (XL, XH), [(x_index(i), x_index((i + step) % 4)) for i in...  14.8 us
    ppermute x10, starting transfers between devices, send_y(): return lax.ppermute(a, Y, [(i, (i + step) % 4) for i in range(4)])  14.3 us
    pallas_call x2, Pallas kernels, layer(): pl.pallas_call(functools.partial(layer_body, order, before is not None),...  9.33 us
    ppermute x3, starting transfers between devices, send_z(): return lax.ppermute(a, Z, [(i, (i + step) % 8) for i in range(8)])  9.08 us
    ppermute x3, waiting for transfers between devices, send_z(): return lax.ppermute(a, Z, [(i, (i + step) % 8) for i in range(8)])  6.57 us
    ppermute x4, starting transfers between devices, send_x(): lax.ppermute(a, (XL, XH), [(x_index(i), x_index((i + step) % 4)) for i in...  4.13 us
    pallas_call x1, Pallas kernels, partials(): pl.pallas_call(partial_body, out_shape=[jax.ShapeDtypeStruct((2 * ROWS, W...  4.12 us
  transfers between devices with their start and end apart: 30, of which 16 were waited for; matrix products, arithmetic and copies ran while one was open for 1% of the time, Pallas kernels for 15%

profile of v2, /device:TPU:2, one launch (start us, length us, event | category | flops | bytes accessed | tf_op | source)
XLA Modules:
  0.0 112.9 jit_solution(3805784789600126825)
XLA Ops:
  0.7 1.6 %copy-done = bf16[256,4096]{1,0:T(8,128)(2,1)S(1)} copy-done((bf16[256,4096]{1,0:T(8,128)(2,1)S(1)}, bf16[256,4096]{1,0:T(8,128)(2,1)}, u32[]{:S(2)}) %copy-start) | copy-done | bytes 2097176
  6.8 1.7 %collective-permute-start.8 = (bf16[256,1024]{1,0:T(8,128)(2,1)S(1)}, bf16[256,1024]{1,0:T(8,128)(2,1)S(1)}, u32[]{:S(2)}, u32[]{:S(2)}) collective-permute-start(bf16[256,1024]{1,0:T(8,128)(2,1)S(1)} %copy-done.5), channel_id=1, source_target_pairs={{0,6},{2,0},{4,2},{6,4},{1,7},{3,1},{5,3},{7,5},{8,14},{10,8},{12,... | collective-permute-start | bytes 1572872 | tf_op jit(solution)/shard_map/ppermute | solution.py:19
  8.5 4.1 %shard_map.93 = (bf16[512,1024]{1,0:T(8,128)(2,1)S(1)}, bf16[4,128,1024]{2,1,0:T(8,128)(2,1)S(1)}, bf16[4,128,1024]{2,1,0:T(8,128)(2,1)S(1)}, bf16[4,128,1024]{2...) custom-call(s32[4]{0:T(128)S(1)} %pad_add_fusion.pos, ...), custom_call_target="tpu_custom_call" | custom-call | flops 2147483648 | bytes 9437184 | tf_op jit(solution)/shard_map/pallas_call | solution.py:112
  12.6 6.4 %collective-permute-done.7.refs_2_ = bf16[256,1024]{1,0:T(8,128)(2,1)S(1)} collective-permute-done((bf16[256,1024]{1,0:T(8,128)(2,1)S(1)}, bf16[256,1024]{1,0:T(8,128)(2,1)S(1)}, u32[]{:S(2)}, u32[]{:S(2)}) %collective-permute-start.7) | collective-permute-done | bytes 524320 | tf_op jit(solution)/shard_map/ppermute | solution.py:19
  20.4 3.0 %collective-permute-start.10 = (bf16[384,1024]{1,0:T(8,128)(2,1)S(1)}, bf16[384,1024]{1,0:T(8,128)(2,1)S(1)}, u32[]{:S(2)}, u32[]{:S(2)}) collective-permute-start(bf16[384,1024]{1,0:T(8,128)(2,1)S(1)} %get-tuple-element.113), channel_id=1, source_target_pairs={{0,6},{2,0},{4,2},{6,4},{1,7},{3,1},{5,3},{7,5},{8,14},{10,8},{12,... | collective-permute-start | bytes 2359304 | tf_op jit(solution)/shard_map/ppermute | solution.py:19
  25.5 4.6 %shard_map.95 = (bf16[256,4096]{1,0:T(8,128)(2,1)}, bf16[256,1024]{1,0:T(8,128)(2,1)S(1)}, f32[512,1024]{1,0:T(8,128)S(1)}, f32[1,5120]{1,0:T(1,128)S(1)}) custom-call(s32[4]{0:T(128)S(1)} %pad_add_fusion.pos, bf16[256,4096]{1,0:T(8,128)(2,1)S(1)} %copy-done, bf16[256,2048]{1,0:T(8,128)(2,1)S(1)} %collective-permute-done.tok_other, ...), custom_call_target="tpu_custom_call" | custom-call | flops 2147483648 | bytes 10485760 | tf_op jit(solution)/shard_map/pallas_call | solution.py:298
  30.0 5.8 %collective-permute-done.2.low = bf16[4,128,512]{2,1,0:T(8,128)(2,1)S(1)} collective-permute-done((bf16[4,128,512]{2,1,0:T(8,128)(2,1)S(1)}, bf16[4,128,512]{2,1,0:T(8,128)(2,1)S(1)}, u32[]{:S(2)}, u32[]{:S(2)}) %collective-permute-start.2) | collective-permute-done | bytes 524320 | tf_op jit(solution)/shard_map/ppermute | solution.py:31
  37.8 1.9 %collective-permute-start.5 = (bf16[4,128,1024]{2,1,0:T(8,128)(2,1)S(1)}, bf16[4,128,1024]{2,1,0:T(8,128)(2,1)S(1)}, u32[]{:S(2)}, u32[]{:S(2)}) collective-permute-start(bf16[4,128,1024]{2,1,0:T(8,128)(2,1)S(1)} %get-tuple-element.62), channel_id=1, source_target_pairs={{0,136},{128,0},{8,128},{136,8},{1,137},{129,1},{9,129},{137,9},{2... | collective-permute-start | bytes 3145736 | tf_op jit(solution)/shard_map/ppermute | solution.py:31
  39.9 2.7 %collective-permute-done.9 = bf16[384,1024]{1,0:T(8,128)(2,1)S(1)} collective-permute-done((bf16[384,1024]{1,0:T(8,128)(2,1)S(1)}, bf16[384,1024]{1,0:T(8,128)(2,1)S(1)}, u32[]{:S(2)}, u32[]{:S(2)}) %collective-permute-start.9) | collective-permute-done | bytes 786464 | tf_op jit(solution)/shard_map/ppermute | solution.py:19
  42.8 3.3 %collective-permute-start.12 = (bf16[128,1024]{1,0:T(8,128)(2,1)S(1)}, bf16[128,1024]{1,0:T(8,128)(2,1)S(1)}, u32[]{:S(2)}, u32[]{:S(2)}) collective-permute-start(bf16[128,1024]{1,0:T(8,128)(2,1)S(1)} %get-tuple-element.111), channel_id=1, source_target_pairs={{0,6},{2,0},{4,2},{6,4},{1,7},{3,1},{5,3},{7,5},{8,14},{10,8},{12,... | collective-permute-start | bytes 786440 | tf_op jit(solution)/shard_map/ppermute | solution.py:19
  46.2 4.1 %collective-permute-done.11 = bf16[128,1024]{1,0:T(8,128)(2,1)S(1)} collective-permute-done((bf16[128,1024]{1,0:T(8,128)(2,1)S(1)}, bf16[128,1024]{1,0:T(8,128)(2,1)S(1)}, u32[]{:S(2)}, u32[]{:S(2)}) %collective-permute-start.11) | collective-permute-done | bytes 262176 | tf_op jit(solution)/shard_map/ppermute | solution.py:19
  50.3 4.7 %shard_map.96 = (bf16[256,4096]{1,0:T(8,128)(2,1)}, bf16[256,1024]{1,0:T(8,128)(2,1)S(1)}, f32[256,1024]{1,0:T(8,128)S(1)}, bf16[256,1024]{1,0:T(8,128)(2,1)S(1)}, f32[1,5120]{1,0:T(1,128)S(1)}) custom-call(s32[4]{0:T(128)S(1)} %pad_add_fusion.pos, bf16[256,4096]{1,0:T(8,128)(2,1)S(1)} %copy-done.1, ...), custom_call_target="tpu_custom_call", output_to_operand_aliasing={{0}: (13, {})} | custom-call | flops 2147483648 | bytes 10485760 | tf_op jit(solution)/shard_map/pallas_call | solution.py:298
  55.1 5.3 %collective-permute-done.5.r2 = bf16[4,128,1024]{2,1,0:T(8,128)(2,1)S(1)} collective-permute-done((bf16[4,128,1024]{2,1,0:T(8,128)(2,1)S(1)}, bf16[4,128,1024]{2,1,0:T(8,128)(2,1)S(1)}, u32[]{:S(2)}, u32[]{:S(2)}) %collective-permute-start.5) | collective-permute-done | bytes 1048608 | tf_op jit(solution)/shard_map/ppermute | solution.py:31
  60.4 2.6 %collective-permute-done.4.r1 = bf16[4,128,1024]{2,1,0:T(8,128)(2,1)S(1)} collective-permute-done((bf16[4,128,1024]{2,1,0:T(8,128)(2,1)S(1)}, bf16[4,128,1024]{2,1,0:T(8,128)(2,1)S(1)}, u32[]{:S(2)}, u32[]{:S(2)}) %collective-permute-start.4) | collective-permute-done | bytes 1048608 | tf_op jit(solution)/shard_map/ppermute | solution.py:31
  63.4 3.2 %collective-permute-start.17 = (bf16[128,1024]{1,0:T(8,128)(2,1)S(1)}, bf16[128,1024]{1,0:T(8,128)(2,1)S(1)}, u32[]{:S(2)}, u32[]{:S(2)}) collective-permute-start(bf16[128,1024]{1,0:T(8,128)(2,1)S(1)} %get-tuple-element.92), channel_id=1, source_target_pairs={{0,6},{2,0},{4,2},{6,4},{1,7},{3,1},{5,3},{7,5},{8,14},{10,8},{12,... | collective-permute-start | bytes 786440 | tf_op jit(solution)/shard_map/ppermute | solution.py:19
  68.7 3.9 %collective-permute-done.16.r1 = bf16[128,1024]{1,0:T(8,128)(2,1)S(1)} collective-permute-done((bf16[128,1024]{1,0:T(8,128)(2,1)S(1)}, bf16[128,1024]{1,0:T(8,128)(2,1)S(1)}, u32[]{:S(2)}, u32[]{:S(2)}) %collective-permute-start.16) | collective-permute-done | bytes 262176 | tf_op jit(solution)/shard_map/ppermute | solution.py:19
  76.1 2.1 %collective-permute-start.20 = (bf16[64,1024]{1,0:T(8,128)(2,1)S(1)}, bf16[64,1024]{1,0:T(8,128)(2,1)S(1)}, u32[]{:S(2)}, u32[]{:S(2)}) collective-permute-start(bf16[64,1024]{1,0:T(8,128)(2,1)S(1)} %get-tuple-element.99), channel_id=1, source_target_pairs={{0,16},{16,0},{32,48},{48,32},{64,80},{80,64},{96,112},{112,96},{1... | collective-permute-start | bytes 393224 | tf_op jit(solution)/shard_map/ppermute | solution.py:408
  79.2 4.4 %collective-permute-done.21 = f32[1,5120]{1,0:T(1,128)S(1)} collective-permute-done((f32[1,5120]{1,0:T(1,128)S(1)}, f32[1,5120]{1,0:T(1,128)S(1)}, u32[]{:S(2)}, u32[]{:S(2)}) %collective-permute-start.21) | collective-permute-done | bytes 20512 | tf_op jit(solution)/shard_map/ppermute | solution.py:19
  85.2 6.2 %collective-permute-start.24 = (bf16[64,1024]{1,0:T(8,128)(2,1)S(1)}, bf16[64,1024]{1,0:T(8,128)(2,1)S(1)}, u32[]{:S(2)}, u32[]{:S(2)}) collective-permute-start(bf16[64,1024]{1,0:T(8,128)(2,1)S(1)} %add_convert_fusion.1), channel_id=1, source_target_pairs={{0,64},{16,80},{32,96},{48,112},{64,0},{80,16},{96,32},{112,48},{1... | collective-permute-start | bytes 393224 | tf_op jit(solution)/shard_map/ppermute | solution.py:23
  92.1 2.2 %collective-permute-start.22 = (bf16[64,1024]{1,0:T(8,128)(2,1)S(1)}, bf16[64,1024]{1,0:T(8,128)(2,1)S(1)}, u32[]{:S(2)}, u32[]{:S(2)}) collective-permute-start(bf16[64,1024]{1,0:T(8,128)(2,1)S(1)} %add_convert_fusion.1), channel_id=1, source_target_pairs={{0,32},{16,48},{32,64},{48,80},{64,96},{80,112},{96,0},{112,16},{1... | collective-permute-start | bytes 393224 | tf_op jit(solution)/shard_map/ppermute | solution.py:23
  94.3 3.9 %collective-permute-done.24 = bf16[64,1024]{1,0:T(8,128)(2,1)S(1)} collective-permute-done((bf16[64,1024]{1,0:T(8,128)(2,1)S(1)}, bf16[64,1024]{1,0:T(8,128)(2,1)S(1)}, u32[]{:S(2)}, u32[]{:S(2)}) %collective-permute-start.24) | collective-permute-done | bytes 131104 | tf_op jit(solution)/shard_map/ppermute | solution.py:23
  98.2 2.7 %collective-permute-done.23 = bf16[64,1024]{1,0:T(8,128)(2,1)S(1)} collective-permute-done((bf16[64,1024]{1,0:T(8,128)(2,1)S(1)}, bf16[64,1024]{1,0:T(8,128)(2,1)S(1)}, u32[]{:S(2)}, u32[]{:S(2)}) %collective-permute-start.23) | collective-permute-done | bytes 131104 | tf_op jit(solution)/shard_map/ppermute | solution.py:23
  101.0 3.4 %collective-permute-start.28 = (bf16[64,1024]{1,0:T(8,128)(2,1)S(1)}, bf16[64,1024]{1,0:T(8,128)(2,1)S(1)}, u32[]{:S(2)}, u32[]{:S(2)}) collective-permute-start(bf16[64,1024]{1,0:T(8,128)(2,1)S(1)} %add_convert_fusion.own), channel_id=1, source_target_pairs={{0,144},{16,128},{32,176},{48,160},{64,208},{80,192},{96,240},{112... | collective-permute-start | bytes 393224 | tf_op jit(solution)/shard_map/ppermute | solution.py:422
  111.3 1.6 %shard_map.100 = f32[256,1024]{1,0:T(8,128)} custom-call(s32[4]{0:T(128)S(1)} %pad_add_fusion.pos, bf16[64,1024]{1,0:T(8,128)(2,1)S(1)} %add_convert_fusion.own, bf16[64,1024]{1,0:T(8,128)(2,1)S(1)} %collective-permute-done.26.by_z, bf16[64,1024]{1,0:T(8,128)(2,1)S(1)} %collective-permute-done.27.by_x, bf16[64,1024]{1,0:T(8,128)(2,1)S(1)} %collective-permute-done.28.by_both), custom_call_target="tpu_custom_call" | custom-call | flops 262144 | bytes 1048576 | tf_op jit(solution)/shard_map/pallas_call | solution.py:201
  (74 shorter events, 26.7 us)
Async XLA Ops:
  3.7 15.2 %collective-permute-start.7 = (bf16[256,1024]{1,0:T(8,128)(2,1)S(1)}, bf16[256,1024]{1,0:T(8,128)(2,1)S(1)}, u32[]{:S(2)}, u32[]{:S(2)}) collective-permute-start(bf16[256,1024]{1,0:T(8,128)(2,1)S(1)} %copy-done.5), channel_id=1, source_target_pairs={{0,2},{2,4},{4,6},{6,0},{1,3},{3,5},{5,7},{7,1},{8,10},{10,12},{12... | collective-permute-start | bytes 1572872 | tf_op jit(solution)/shard_map/ppermute | solution.py:19
  5.3 13.7 %collective-permute-start.6 = (bf16[256,1024]{1,0:T(8,128)(2,1)S(1)}, bf16[256,1024]{1,0:T(8,128)(2,1)S(1)}, u32[]{:S(2)}, u32[]{:S(2)}) collective-permute-start(bf16[256,1024]{1,0:T(8,128)(2,1)S(1)} %copy-done.5), channel_id=1, source_target_pairs={{0,136},{128,8},{8,128},{136,0},{1,137},{129,9},{9,129},{137,1},{2... | collective-permute-start | bytes 1572872 | tf_op jit(solution)/shard_map/ppermute | solution.py:35
  6.8 13.4 %collective-permute-start.8 = (bf16[256,1024]{1,0:T(8,128)(2,1)S(1)}, bf16[256,1024]{1,0:T(8,128)(2,1)S(1)}, u32[]{:S(2)}, u32[]{:S(2)}) collective-permute-start(bf16[256,1024]{1,0:T(8,128)(2,1)S(1)} %copy-done.5), channel_id=1, source_target_pairs={{0,6},{2,0},{4,2},{6,4},{1,7},{3,1},{5,3},{7,5},{8,14},{10,8},{12,... | collective-permute-start | bytes 1572872 | tf_op jit(solution)/shard_map/ppermute | solution.py:19
  20.4 19.5 %collective-permute-start.10 = (bf16[384,1024]{1,0:T(8,128)(2,1)S(1)}, bf16[384,1024]{1,0:T(8,128)(2,1)S(1)}, u32[]{:S(2)}, u32[]{:S(2)}) collective-permute-start(bf16[384,1024]{1,0:T(8,128)(2,1)S(1)} %get-tuple-element.113), channel_id=1, source_target_pairs={{0,6},{2,0},{4,2},{6,4},{1,7},{3,1},{5,3},{7,5},{8,14},{10,8},{12,... | collective-permute-start | bytes 2359304 | tf_op jit(solution)/shard_map/ppermute | solution.py:19
  23.4 19.2 %collective-permute-start.9 = (bf16[384,1024]{1,0:T(8,128)(2,1)S(1)}, bf16[384,1024]{1,0:T(8,128)(2,1)S(1)}, u32[]{:S(2)}, u32[]{:S(2)}) collective-permute-start(bf16[384,1024]{1,0:T(8,128)(2,1)S(1)} %get-tuple-element.114), channel_id=1, source_target_pairs={{0,2},{2,4},{4,6},{6,0},{1,3},{3,5},{5,7},{7,1},{8,10},{10,12},{12... | collective-permute-start | bytes 2359304 | tf_op jit(solution)/shard_map/ppermute | solution.py:19
  23.4 12.4 %collective-permute-start.2 = (bf16[4,128,512]{2,1,0:T(8,128)(2,1)S(1)}, bf16[4,128,512]{2,1,0:T(8,128)(2,1)S(1)}, u32[]{:S(2)}, u32[]{:S(2)}) collective-permute-start(bf16[4,128,512]{2,1,0:T(8,128)(2,1)S(1)} %get-tuple-element.59), channel_id=1, source_target_pairs={{0,128},{128,8},{8,136},{136,0},{1,129},{129,9},{9,137},{137,1},{2... | collective-permute-start | bytes 1572872 | tf_op jit(solution)/shard_map/ppermute | solution.py:31
  24.0 13.0 %collective-permute-start.3 = (bf16[4,128,512]{2,1,0:T(8,128)(2,1)S(1)}, bf16[4,128,512]{2,1,0:T(8,128)(2,1)S(1)}, u32[]{:S(2)}, u32[]{:S(2)}) collective-permute-start(bf16[4,128,512]{2,1,0:T(8,128)(2,1)S(1)} %get-tuple-element.60), channel_id=1, source_target_pairs={{0,136},{128,0},{8,128},{136,8},{1,137},{129,1},{9,129},{137,9},{2... | collective-permute-start | bytes 1572872 | tf_op jit(solution)/shard_map/ppermute | solution.py:31
  37.8 22.6 %collective-permute-start.5 = (bf16[4,128,1024]{2,1,0:T(8,128)(2,1)S(1)}, bf16[4,128,1024]{2,1,0:T(8,128)(2,1)S(1)}, u32[]{:S(2)}, u32[]{:S(2)}) collective-permute-start(bf16[4,128,1024]{2,1,0:T(8,128)(2,1)S(1)} %get-tuple-element.62), channel_id=1, source_target_pairs={{0,136},{128,0},{8,128},{136,8},{1,137},{129,1},{9,129},{137,9},{2... | collective-permute-start | bytes 3145736 | tf_op jit(solution)/shard_map/ppermute | solution.py:31
  39.7 23.3 %collective-permute-start.4 = (bf16[4,128,1024]{2,1,0:T(8,128)(2,1)S(1)}, bf16[4,128,1024]{2,1,0:T(8,128)(2,1)S(1)}, u32[]{:S(2)}, u32[]{:S(2)}) collective-permute-start(bf16[4,128,1024]{2,1,0:T(8,128)(2,1)S(1)} %get-tuple-element.61), channel_id=1, source_target_pairs={{0,128},{128,8},{8,136},{136,0},{1,129},{129,9},{9,137},{137,1},{2... | collective-permute-start | bytes 3145736 | tf_op jit(solution)/shard_map/ppermute | solution.py:31
  42.6 7.7 %collective-permute-start.11 = (bf16[128,1024]{1,0:T(8,128)(2,1)S(1)}, bf16[128,1024]{1,0:T(8,128)(2,1)S(1)}, u32[]{:S(2)}, u32[]{:S(2)}) collective-permute-start(bf16[128,1024]{1,0:T(8,128)(2,1)S(1)} %get-tuple-element.109), channel_id=1, source_target_pairs={{0,2},{2,4},{4,6},{6,0},{1,3},{3,5},{5,7},{7,1},{8,10},{10,12},{12... | collective-permute-start | bytes 786440 | tf_op jit(solution)/shard_map/ppermute | solution.py:19
  42.8 7.5 %collective-permute-start.12 = (bf16[128,1024]{1,0:T(8,128)(2,1)S(1)}, bf16[128,1024]{1,0:T(8,128)(2,1)S(1)}, u32[]{:S(2)}, u32[]{:S(2)}) collective-permute-start(bf16[128,1024]{1,0:T(8,128)(2,1)S(1)} %get-tuple-element.111), channel_id=1, source_target_pairs={{0,6},{2,0},{4,2},{6,4},{1,7},{3,1},{5,3},{7,5},{8,14},{10,8},{12,... | collective-permute-start | bytes 786440 | tf_op jit(solution)/shard_map/ppermute | solution.py:19
  63.3 9.3 %collective-permute-start.16 = (bf16[128,1024]{1,0:T(8,128)(2,1)S(1)}, bf16[128,1024]{1,0:T(8,128)(2,1)S(1)}, u32[]{:S(2)}, u32[]{:S(2)}) collective-permute-start(bf16[128,1024]{1,0:T(8,128)(2,1)S(1)} %get-tuple-element.91), channel_id=1, source_target_pairs={{0,2},{2,4},{4,6},{6,0},{1,3},{3,5},{5,7},{7,1},{8,10},{10,12},{12... | collective-permute-start | bytes 786440 | tf_op jit(solution)/shard_map/ppermute | solution.py:19
  63.4 10.7 %collective-permute-start.17 = (bf16[128,1024]{1,0:T(8,128)(2,1)S(1)}, bf16[128,1024]{1,0:T(8,128)(2,1)S(1)}, u32[]{:S(2)}, u32[]{:S(2)}) collective-permute-start(bf16[128,1024]{1,0:T(8,128)(2,1)S(1)} %get-tuple-element.92), channel_id=1, source_target_pairs={{0,6},{2,0},{4,2},{6,4},{1,7},{3,1},{5,3},{7,5},{8,14},{10,8},{12,... | collective-permute-start | bytes 786440 | tf_op jit(solution)/shard_map/ppermute | solution.py:19
  66.7 8.8 %collective-permute-start.18 = (bf16[128,1024]{1,0:T(8,128)(2,1)S(1)}, bf16[128,1024]{1,0:T(8,128)(2,1)S(1)}, u32[]{:S(2)}, u32[]{:S(2)}) collective-permute-start(bf16[128,1024]{1,0:T(8,128)(2,1)S(1)} %get-tuple-element.93), channel_id=1, source_target_pairs={{0,4},{2,6},{4,0},{6,2},{1,5},{3,7},{5,1},{7,3},{8,12},{10,14},{12... | collective-permute-start | bytes 786440 | tf_op jit(solution)/shard_map/ppermute | solution.py:19
  76.1 7.5 %collective-permute-start.20 = (bf16[64,1024]{1,0:T(8,128)(2,1)S(1)}, bf16[64,1024]{1,0:T(8,128)(2,1)S(1)}, u32[]{:S(2)}, u32[]{:S(2)}) collective-permute-start(bf16[64,1024]{1,0:T(8,128)(2,1)S(1)} %get-tuple-element.99), channel_id=1, source_target_pairs={{0,16},{16,0},{32,48},{48,32},{64,80},{80,64},{96,112},{112,96},{1... | collective-permute-start | bytes 393224 | tf_op jit(solution)/shard_map/ppermute | solution.py:408
  78.7 25.7 %collective-permute-start.14 = (bf16[256,1024]{1,0:T(8,128)(2,1)S(1)}, bf16[256,1024]{1,0:T(8,128)(2,1)S(1)}, u32[]{:S(2)}, u32[]{:S(2)}) collective-permute-start(bf16[256,1024]{1,0:T(8,128)(2,1)S(1)} %get-tuple-element.84), channel_id=1, source_target_pairs={{0,1},{1,0},{2,3},{3,2},{4,5},{5,4},{6,7},{7,6},{8,9},{9,8},{10,11... | collective-permute-start | bytes 1572872 | tf_op jit(solution)/shard_map/ppermute | solution.py:39
  78.7 26.7 %collective-permute-start.13 = (bf16[256,1024]{1,0:T(8,128)(2,1)S(1)}, bf16[256,1024]{1,0:T(8,128)(2,1)S(1)}, u32[]{:S(2)}, u32[]{:S(2)}) collective-permute-start(bf16[256,1024]{1,0:T(8,128)(2,1)S(1)} %get-tuple-element.83), channel_id=1, source_target_pairs={{0,1},{1,0},{2,3},{3,2},{4,5},{5,4},{6,7},{7,6},{8,9},{9,8},{10,11... | collective-permute-start | bytes 1572872 | tf_op jit(solution)/shard_map/ppermute | solution.py:39
  83.6 8.5 %collective-permute-start.25 = (f32[1,5120]{1,0:T(1,128)S(1)}, f32[1,5120]{1,0:T(1,128)S(1)}, u32[]{:S(2)}, u32[]{:S(2)}) collective-permute-start(f32[1,5120]{1,0:T(1,128)S(1)} %add.31), channel_id=1, source_target_pairs={{0,2},{2,0},{4,6},{6,4},{1,3},{3,1},{5,7},{7,5},{8,10},{10,8},{12,... | collective-permute-start | bytes 61448 | tf_op jit(solution)/shard_map/ppermute | solution.py:416
  85.2 13.0 %collective-permute-start.24 = (bf16[64,1024]{1,0:T(8,128)(2,1)S(1)}, bf16[64,1024]{1,0:T(8,128)(2,1)S(1)}, u32[]{:S(2)}, u32[]{:S(2)}) collective-permute-start(bf16[64,1024]{1,0:T(8,128)(2,1)S(1)} %add_convert_fusion.1), channel_id=1, source_target_pairs={{0,64},{16,80},{32,96},{48,112},{64,0},{80,16},{96,32},{112,48},{1... | collective-permute-start | bytes 393224 | tf_op jit(solution)/shard_map/ppermute | solution.py:23
  91.4 9.5 %collective-permute-start.23 = (bf16[64,1024]{1,0:T(8,128)(2,1)S(1)}, bf16[64,1024]{1,0:T(8,128)(2,1)S(1)}, u32[]{:S(2)}, u32[]{:S(2)}) collective-permute-start(bf16[64,1024]{1,0:T(8,128)(2,1)S(1)} %add_convert_fusion.1), channel_id=1, source_target_pairs={{0,96},{16,112},{32,0},{48,16},{64,32},{80,48},{96,64},{112,80},{1... | collective-permute-start | bytes 393224 | tf_op jit(solution)/shard_map/ppermute | solution.py:23
  92.1 8.7 %collective-permute-start.22 = (bf16[64,1024]{1,0:T(8,128)(2,1)S(1)}, bf16[64,1024]{1,0:T(8,128)(2,1)S(1)}, u32[]{:S(2)}, u32[]{:S(2)}) collective-permute-start(bf16[64,1024]{1,0:T(8,128)(2,1)S(1)} %add_convert_fusion.1), channel_id=1, source_target_pairs={{0,32},{16,48},{32,64},{48,80},{64,96},{80,112},{96,0},{112,16},{1... | collective-permute-start | bytes 393224 | tf_op jit(solution)/shard_map/ppermute | solution.py:23
  98.2 9.5 %collective-permute-start.15 = (bf16[256,1024]{1,0:T(8,128)(2,1)S(1)}, bf16[256,1024]{1,0:T(8,128)(2,1)S(1)}, u32[]{:S(2)}, u32[]{:S(2)}) collective-permute-start(bf16[256,1024]{1,0:T(8,128)(2,1)S(1)} %get-tuple-element.85), channel_id=1, source_target_pairs={{0,1},{1,0},{2,3},{3,2},{4,5},{5,4},{6,7},{7,6},{8,9},{9,8},{10,11... | collective-permute-start | bytes 1572872 | tf_op jit(solution)/shard_map/ppermute | solution.py:39
  101.0 10.3 %collective-permute-start.28 = (bf16[64,1024]{1,0:T(8,128)(2,1)S(1)}, bf16[64,1024]{1,0:T(8,128)(2,1)S(1)}, u32[]{:S(2)}, u32[]{:S(2)}) collective-permute-start(bf16[64,1024]{1,0:T(8,128)(2,1)S(1)} %add_convert_fusion.own), channel_id=1, source_target_pairs={{0,144},{16,128},{32,176},{48,160},{64,208},{80,192},{96,240},{112... | collective-permute-start | bytes 393224 | tf_op jit(solution)/shard_map/ppermute | solution.py:422
  104.4 6.9 %collective-permute-start.27 = (bf16[64,1024]{1,0:T(8,128)(2,1)S(1)}, bf16[64,1024]{1,0:T(8,128)(2,1)S(1)}, u32[]{:S(2)}, u32[]{:S(2)}) collective-permute-start(bf16[64,1024]{1,0:T(8,128)(2,1)S(1)} %add_convert_fusion.own), channel_id=1, source_target_pairs={{0,128},{128,0},{8,136},{136,8},{1,129},{129,1},{9,137},{137,9},{2... | collective-permute-start | bytes 393224 | tf_op jit(solution)/shard_map/ppermute | solution.py:35
  (12 other events, 56.5 us)

commit v3 on v2

v3 whole, which is shorter than its diff:
```python
import functools

import jax
import jax.numpy as jnp
from jax import lax
from jax.experimental import pallas as pl
from jax.experimental.pallas import tpu as pltpu
from jax.sharding import Mesh, PartitionSpec as P

F32, BF16 = jnp.float32, jnp.bfloat16
XL, Z, XH, Y, C = "xl", "z", "xh", "y", "c"
ROWS, DEPTH, WIDTH, PIECE = 256, 4096, 1024, 256
LOW, LANE = 640, PIECE // 2
HIGH = WIDTH - LOW
PASSING = 4 * 2**30
VMEM = pl.BlockSpec(memory_space=pltpu.VMEM)
PARAMS = pltpu.CompilerParams(vmem_limit_bytes=40 * 2**20)


def swap_core(a):
    return lax.ppermute(a, C, [(0, 1), (1, 0)])


def swap_y(a, flip):
    return lax.ppermute(a, Y, [(i, i ^ flip) for i in range(4)])


def x_index(place):
    return (place % 2) * 2 + place // 2


def swap_x(a, flip):
    return lax.ppermute(a, (XL, XH), [(x_index(i), x_index(i ^ flip)) for i in range(4)])


def swap_z(a, partners):
    return lax.ppermute(a, Z, list(enumerate(partners)))


NEAR = (1, 0, 3, 2, 5, 4, 7, 6)
NEXT = (7, 2, 1, 4, 3, 6, 5, 0)
FAR = (3, 6, 5, 0, 7, 2, 1, 4)


def slice_of(pos, dxh, dy):
    return ((pos[0] // 2) ^ dxh) * 4 + (pos[1] ^ dy)


def cost(flops, bytes_accessed):
    return pl.CostEstimate(flops=flops, bytes_accessed=bytes_accessed, transcendentals=0)


ANY = pl.BlockSpec(memory_space=pl.ANY)
SCALARS = pl.BlockSpec(memory_space=pltpu.SMEM)


def pick_body(pos, src, out, sems):
    copies = [
        pltpu.make_async_copy(
            src.at[:, pl.ds(pl.multiple_of((2 * j + 1 - pos[2]) * PIECE, PIECE), PIECE)],
            out.at[:, j * PIECE : (j + 1) * PIECE],
            sems.at[j],
        )
        for j in range(8)
    ]
    for copy in copies:
        copy.start()
    for copy in copies:
        copy.wait()


def other_half(pos, tokens):
    return pl.pallas_call(
        pick_body,
        out_shape=jax.ShapeDtypeStruct((ROWS, DEPTH // 2), BF16),
        in_specs=[SCALARS, ANY],
        out_specs=ANY,
        scratch_shapes=[pltpu.SemaphoreType.DMA((8,))],
        compiler_params=PARAMS,
        cost_estimate=cost(0, 2**21),
    )(pos, tokens)


def partial_body(pos, tok, tok_other, cot, cot_other, in_scale, out_scale, grad_ref, *refs):
    stay, one, early_one, three, late_one, late_three, left = refs
    i = pl.program_id(0)

    @pl.when(i == 0)
    def _():
        grad_ref[:ROWS] = (cot[...].astype(F32) * out_scale[...]).astype(BF16)
        grad_ref[ROWS:] = (cot_other[...].astype(F32) * out_scale[...]).astype(BF16)

    y_at = pos[1] ^ i
    for k in range(4):
        x_at = pos[0] ^ k
        place = (x_at // 2) * 4 + y_at
        wide = pl.ds(pl.multiple_of(((place * 2 + pos[2]) * 2 + x_at % 2) * LANE, LANE), LANE)
        narrow = pl.ds(pl.multiple_of((place * 2 + x_at % 2) * LANE, LANE), LANE)
        scale = in_scale[:, wide]
        left[:ROWS, k * LANE : (k + 1) * LANE] = (tok[:, wide].astype(F32) * scale).astype(BF16)
        left[ROWS:, k * LANE : (k + 1) * LANE] = (tok_other[:, narrow].astype(F32) * scale).astype(BF16)
    part = lax.dot_general(
        left[...], grad_ref[...], (((0,), (0,)), ((), ())), preferred_element_type=F32
    ).astype(BF16)
    stay[0] = part[:LANE]
    low, high = slice(0, LOW), slice(LOW, WIDTH)
    one[0] = part[2 * LANE : 3 * LANE, low]
    early_one[0] = part[LANE : 2 * LANE, low]
    three[0, :, :HIGH] = part[2 * LANE : 3 * LANE, high]
    three[0, :, HIGH:] = part[3 * LANE :, high]
    late_one[0] = part[LANE : 2 * LANE, high]
    late_three[0] = part[3 * LANE :, low]


def partials(pos, tokens, tok_other, cot, cot_other, in_scale, out_scale):
    whole = lambda shape: pl.BlockSpec(shape, lambda i, pos: (0,) * len(shape))
    columns = (WIDTH, LOW, LOW, 2 * HIGH, HIGH, LOW)
    return pl.pallas_call(
        partial_body,
        out_shape=[jax.ShapeDtypeStruct((2 * ROWS, WIDTH), BF16)]
        + [jax.ShapeDtypeStruct((4, LANE, n), BF16) for n in columns],
        grid_spec=pltpu.PrefetchScalarGridSpec(
            num_scalar_prefetch=1,
            grid=(4,),
            in_specs=[
                whole((ROWS, DEPTH)), whole((ROWS, DEPTH // 2)), whole((ROWS, WIDTH)),
                whole((ROWS, WIDTH)), whole((1, DEPTH)), whole((1, WIDTH)),
            ],
            out_specs=[whole((2 * ROWS, WIDTH))]
            + [pl.BlockSpec((1, LANE, n), lambda i, pos: (i, 0, 0)) for n in columns],
            scratch_shapes=[pltpu.VMEM((2 * ROWS, 4 * LANE), BF16)],
        ),
        compiler_params=PARAMS,
        cost_estimate=cost(2 * 2 * ROWS * DEPTH // 2 * WIDTH, 9 * 2**20),
    )(pos, tokens, tok_other, cot, cot_other, in_scale, out_scale)


def add_body(late_one, late_three, one, three, one_out, three_out):
    one_out[...] = (late_one[...].astype(F32) + three[:, :, :HIGH].astype(F32)).astype(BF16)
    three_out[...] = (late_three[...].astype(F32) + one[...].astype(F32)).astype(BF16)


def add_passing(late_one, late_three, one, three):
    return pl.pallas_call(
        add_body,
        out_shape=[jax.ShapeDtypeStruct(late_one.shape, BF16), jax.ShapeDtypeStruct(late_three.shape, BF16)],
        in_specs=[VMEM] * 4,
        out_specs=[VMEM] * 2,
        compiler_params=PARAMS,
        cost_estimate=cost(PASSING, 3 * 2**20),
    )(late_one, late_three, one, three)


def sum_body(own, early_one, three, late_one, late_three, keep, s1, s2, s3):
    low, high = slice(0, LOW), slice(LOW, WIDTH)
    for k, out in enumerate((keep, s1, s2, s3)):
        for at, early, late in ((low, early_one[k], late_three[k]), (high, three[k, :, HIGH:], late_one[k])):
            total = own[k, :, at].astype(F32) + early.astype(F32) + late.astype(F32)
            out[:, at] = total.astype(out.dtype)


def sum_blocks(own, arrived):
    shape = own.shape[1:]
    return pl.pallas_call(
        sum_body,
        out_shape=[jax.ShapeDtypeStruct(shape, F32)] + [jax.ShapeDtypeStruct(shape, BF16)] * 3,
        in_specs=[VMEM] * 5,
        out_specs=[VMEM] * 4,
        compiler_params=PARAMS,
        cost_estimate=cost(2**20, 4 * 2**20),
    )(own, *arrived)


def join_body(pos, own, r1, r2, r3, keep, send):
    count = LANE // 2
    mine = pos[3]
    for out, at in ((keep, mine), (send, 1 - mine)):
        rows = pl.ds(pl.multiple_of(at * count, count), count)
        total = own[rows]
        for ref in (r1, r2, r3):
            total = total + ref[rows].astype(F32)
        out[...] = total.astype(out.dtype)


def join(pos, own, arrived):
    shape = (LANE // 2, WIDTH)
    return pl.pallas_call(
        join_body,
        out_shape=[jax.ShapeDtypeStruct(shape, F32), jax.ShapeDtypeStruct(shape, BF16)],
        in_specs=[SCALARS] + [VMEM] * 4,
        out_specs=[VMEM] * 2,
        compiler_params=PARAMS,
        cost_estimate=cost(2**20, 2**21),
    )(pos, own, *arrived)


def place_body(scale, pos, own, by_z, by_x, by_both, out):
    count = LANE // 2
    me = (pos[0] % 2) * 2 + pos[3]
    for flip, ref in enumerate((own, by_z, by_x, by_both)):
        at = me ^ flip
        out[pl.ds(pl.multiple_of(at * count, count), count)] = ref[...].astype(F32) * scale


def place(pos, blocks, scale):
    return pl.pallas_call(
        functools.partial(place_body, scale),
        out_shape=jax.ShapeDtypeStruct((PIECE, WIDTH), F32),
        in_specs=[SCALARS] + [VMEM] * 4,
        out_specs=VMEM,
        compiler_params=PARAMS,
        cost_estimate=cost(2**18, 2**20),
    )(pos, *blocks)


def layer_body(order, first, last, pos, tok, tok_other, grad, in_scale, cot, cot_other, *refs):
    count = len(order)
    weights, refs = refs[:count], refs[count:]
    if not first:
        (pre_in, small_in), refs = refs[:2], refs[4:]
    own_ref, other_ref, small = refs[:3]
    if last:
        pre_ref, pre_other, total = refs[3:]
    else:
        (total,) = refs[3:]
    i = pl.program_id(0)

    @pl.when(i == 0)
    def _():
        if first:
            small[...] = jnp.zeros_like(small)
        else:
            total[...] = pre_in[...]
            small[...] = small_in[...]

    for m, (dxh, dy) in enumerate(order):
        @pl.when(i == m)
        def _():
            at = slice_of(pos, dxh, dy)
            wide = pl.ds(pl.multiple_of((at * 2 + pos[2]) * PIECE, PIECE), PIECE)
            narrow = pl.ds(pl.multiple_of(at * PIECE, PIECE), PIECE)
            scale = in_scale[:, wide]
            weight = weights[m][...]
            sums = jnp.zeros((1, PIECE), F32)
            for part, values in ((0, tok[:, wide]), (1, tok_other[:, narrow])):
                rows = slice(part * ROWS, (part + 1) * ROWS)
                values = values.astype(F32)
                scaled = (values * scale).astype(BF16)
                pre = jnp.dot(scaled, weight, preferred_element_type=F32)
                if m == 0 and first:
                    total[rows] = pre
                else:
                    total[rows] += pre
                back = lax.dot_general(
                    grad[rows], weight, (((1,), (1,)), ((), ())), preferred_element_type=F32
                )
                (own_ref, other_ref)[part][...] = (back * scale).astype(BF16)
                sums = sums + jnp.sum(values * back, axis=0, keepdims=True)
            place = at * 2 + pos[2]
            lane = pl.ds(pl.multiple_of((place % 4) * PIECE, PIECE), PIECE)
            small[pl.ds(place // 4, 1), lane] = sums

    if last:
        @pl.when(i == count - 1)
        def _():
            pre_ref[...] = total[:ROWS]
            pre_other[...] = total[ROWS:].astype(BF16)
            small[4:5] = jnp.sum(
                cot[...].astype(F32) * total[:ROWS] + cot_other[...].astype(F32) * total[ROWS:],
                axis=0, keepdims=True,
            )


def layer(pos, orders, step, tokens, tok_other, grad, in_scale, cot, cot_other, weights, before=()):
    whole = lambda shape: pl.BlockSpec(shape, lambda i, pos: (0,) * len(shape))
    shaped = jax.ShapeDtypeStruct
    order, first, last = orders[step], step == 0, step == len(orders) - 1
    start = sum(map(len, orders[:step]))

    def column(i, pos):
        dxh, dy = order[-1]
        for m, flips in enumerate(order[:-1]):
            dxh = jnp.where(i == m, flips[0], dxh)
            dy = jnp.where(i == m, flips[1], dy)
        return 0, slice_of(pos, dxh, dy) * 2 + pos[2]

    both, half = (2 * ROWS, WIDTH), (ROWS, WIDTH)
    small = (8, WIDTH)
    in_specs = [
        whole((ROWS, DEPTH)), whole((ROWS, DEPTH // 2)), whole(both), whole((1, DEPTH)), whole(half), whole(half),
    ] + [whole((PIECE, WIDTH))] * len(order)
    operands = [tokens, tok_other, grad, in_scale, cot, cot_other, *weights]
    aliases = {}
    if not first:
        own, others, sums, pre = before
        aliases = {len(operands) + 3: 0, len(operands) + 4: 1}
        operands += [pre, sums, own, others]
        in_specs += [whole(both), whole(small), ANY, ANY]
    out_shape = [shaped((ROWS, DEPTH), BF16), shaped((ROWS, DEPTH // 2), BF16), shaped(small, F32)]
    out_specs = [
        pl.BlockSpec((ROWS, PIECE), column),
        pl.BlockSpec((ROWS, PIECE), lambda i, pos: (0, i + start)),
        whole(small),
    ]
    if last:
        out_shape += [shaped(half, F32), shaped(half, BF16)]
        out_specs += [whole(half), whole(half)]
    else:
        out_shape += [shaped(both, F32)]
        out_specs += [whole(both)]
    return pl.pallas_call(
        functools.partial(layer_body, order, first, last),
        out_shape=out_shape,
        grid_spec=pltpu.PrefetchScalarGridSpec(
            num_scalar_prefetch=1, grid=(len(order),), in_specs=in_specs, out_specs=out_specs,
            scratch_shapes=[pltpu.VMEM(both, F32)] if last else [],
        ),
        input_output_aliases=aliases,
        compiler_params=PARAMS,
        cost_estimate=cost(1, 1),
    )(pos, *operands)


def fill_body(flips, pos, src, _, out, sems):
    copies = []
    for m, (dxh, dy) in enumerate(flips):
        at = (slice_of(pos, dxh, dy) * 2 + 1 - pos[2]) * PIECE
        copies.append(pltpu.make_async_copy(
            src.at[:, m * PIECE : (m + 1) * PIECE],
            out.at[:, pl.ds(pl.multiple_of(at, PIECE), PIECE)],
            sems.at[m],
        ))
    for copy in copies:
        copy.start()
    for copy in copies:
        copy.wait()


def fill(pos, flips, others, own):
    return pl.pallas_call(
        functools.partial(fill_body, flips),
        out_shape=jax.ShapeDtypeStruct((ROWS, DEPTH), BF16),
        in_specs=[SCALARS, ANY, ANY],
        out_specs=ANY,
        scratch_shapes=[pltpu.SemaphoreType.DMA((8,))],
        input_output_aliases={2: 0},
        compiler_params=PARAMS,
        cost_estimate=cost(0, 2**21),
    )(pos, others, own)


def finish_body(scale, mine, other, in_ref, out_ref):
    total = (mine[...] + other[...]) * scale
    for k in range(4):
        in_ref[:, k * WIDTH : (k + 1) * WIDTH] = total[k : k + 1]
    out_ref[...] = total[4:5]


def finish(mine, other, scale):
    return pl.pallas_call(
        functools.partial(finish_body, scale),
        out_shape=[jax.ShapeDtypeStruct((1, DEPTH), F32), jax.ShapeDtypeStruct((1, WIDTH), F32)],
        in_specs=[VMEM] * 2,
        out_specs=[VMEM] * 2,
        compiler_params=PARAMS,
        cost_estimate=cost(2**14, 2**16),
    )(mine, other)


def on_device(tokens, cotangent, slow_weight, in_scale, out_scale):
    xl, z, xh, y, c = (lax.axis_index(a) for a in (XL, Z, XH, Y, C))
    pos = jnp.stack([2 * xh + xl, y, c, (z ^ (z // 2)) % 2]).astype(jnp.int32)
    member_norm = 1.0 / float(ROWS * 16) ** 0.5
    total_norm = 1.0 / float(ROWS * 256) ** 0.5

    cot_other = swap_core(cotangent)
    one, three = swap_y(slow_weight, 1), swap_y(slow_weight, 3)
    far = swap_x(slow_weight, 3)
    tok_other = swap_core(other_half(pos, tokens))
    grad, stay, by_one, early_one, by_three, late_one, late_three = partials(
        pos, tokens, tok_other, cotangent, cot_other, in_scale, out_scale
    )
    by_one, early_one, by_three = swap_x(by_one, 1), swap_x(early_one, 1), swap_x(by_three, 3)
    far, one, three, grad = lax.optimization_barrier((far, one, three, grad))

    half = PIECE // 2
    far_one = swap_y(jnp.concatenate([far, three[:half]], axis=0), 1)
    far_three = swap_y(jnp.concatenate([far, one[half:]], axis=0), 3)
    orders = ((0, 0), (0, 1), (0, 3), (1, 0)), ((0, 2), (1, 1), (1, 3)), ((1, 2),)
    run = functools.partial(layer, pos, orders)
    common = (tokens, tok_other, grad, in_scale, cotangent, cot_other)
    state = run(0, *common, (slow_weight, one, three, far))
    late_one, late_three = add_passing(late_one, late_three, by_one, by_three)
    arrived = [early_one, by_three, swap_x(late_one, 1), swap_x(late_three, 3)]
    far_one, far_three, state, _ = lax.optimization_barrier((far_one, far_three, state, late_one))

    far_two = [swap_y(far_three[:half], 1), swap_y(far_one[half:PIECE], 3)]
    two = jnp.concatenate([far_one[PIECE:], far_three[PIECE:]], axis=0)
    state = run(1, *common, (two, far_one[:PIECE], far_three[:PIECE]), state)
    far_two, state = lax.optimization_barrier((far_two, state))
    state = run(2, *common, (jnp.concatenate(far_two, axis=0),), state)
    arrived, state = lax.optimization_barrier((arrived, state))
    own, others, small, pre_own, pre_other = state

    stay, *out = sum_blocks(stay, arrived)
    arrived = [swap_y(out[0], 1), swap_y(out[2], 3), swap_y(out[1], 2)]
    small = small + swap_core(small)
    small = small + swap_y(small, 1)
    arrived, small = lax.optimization_barrier((arrived, small))

    keep, out = join(pos, stay, arrived)
    out = swap_z(out, NEAR)
    pre_other, others = swap_core(pre_other), swap_core(others)
    out, small = lax.optimization_barrier((out, small))
    mine = (keep + out.astype(F32)).astype(BF16)
    out = swap_z(mine, NEXT)
    small = small + swap_y(small, 3)
    out, small = lax.optimization_barrier((out, small))
    mine = (mine.astype(F32) + out.astype(F32)).astype(BF16)
    out = swap_z(mine, FAR)
    small_far = swap_x(small, 2)
    result = ((pre_own + pre_other.astype(F32)) * out_scale).astype(BF16)
    grad_tokens = fill(pos, sum(orders, ()), others, own)
    out, small_far, result, grad_tokens = lax.optimization_barrier((out, small_far, result, grad_tokens))
    mine = (mine.astype(F32) + out.astype(F32)).astype(BF16)
    by_z, by_x = swap_z(mine, NEAR), swap_x(mine, 1)
    by_both = lax.ppermute(mine, (XL, Z), [(i, i ^ 9) for i in range(16)])
    grad_in_scale, grad_out_scale = finish(small, small_far, member_norm)
    grad_weight = place(pos, (mine, by_z, by_x, by_both), total_norm)
    return result, grad_tokens, grad_weight, grad_in_scale, grad_out_scale


def solution(mesh):
    wide = Mesh(mesh.devices.reshape(2, 8, 2, 4, 2), (XL, Z, XH, Y, C))
    row, member, shard = P((XL, Z, XH, Y, C), None), P((XL, Z), None), P((XH, Y, C), None)
    return jax.shard_map(
        on_device,
        mesh=wide,
        in_specs=(row, row, shard, member, member),
        out_specs=(row, row, shard, member, member),
        check_vma=False,
    )
```

time: 114 us -> 105 us (0.921)
  waiting for transfers between devices: 49.4 us -> 38.3 us
  starting transfers between devices: 39.4 us -> 42.2 us
    ppermute x24, waiting for transfers between devices: 48.2 us -> 37.6 us  [the longest x11 17.2 us: swap_y(): return lax.ppermute(a, Y, [(i, i ^ flip) for i in range(4)])]
    ppermute x24, starting transfers between devices: 38.4 us -> 41.3 us  [the longest x11 16.2 us: swap_y(): return lax.ppermute(a, Y, [(i, i ^ flip) for i in range(4)])]
    pallas_call x4 -> x5, Pallas kernels: 11.7 us -> 12 us  [the longest x3 10.2 us: layer(): pl.pallas_call(functools.partial(layer_body, order, first, last), out_sha...]
  transfers between devices with their start and end apart: 30 -> 29, of which waited for: 16 -> 19; matrix products, arithmetic and copies ran while one was open for 1% -> 1% of each run, Pallas kernels for 15% -> 17%
where the time goes in v3:
time: 105 us
  starting transfers between devices  42.2 us (40%)
  waiting for transfers between devices  38.3 us (36%)
  Pallas kernels  20.2 us (19%)
  local copies, waits for them, and re-layouts  1.93 us (2%)
  other arithmetic  1.35 us (1%)
    ppermute x11, waiting for transfers between devices, swap_y(): return lax.ppermute(a, Y, [(i, i ^ flip) for i in range(4)])  17.2 us
    ppermute x11, starting transfers between devices, swap_y(): return lax.ppermute(a, Y, [(i, i ^ flip) for i in range(4)])  16.2 us
    ppermute x8, starting transfers between devices, swap_x(): lax.ppermute(a, (XL, XH), [(x_index(i), x_index(i ^ flip)) for i in range...  13.4 us
    ppermute x4, starting transfers between devices, swap_z(): return lax.ppermute(a, Z, list(enumerate(partners)))  11.6 us
    ppermute x8, waiting for transfers between devices, swap_x(): lax.ppermute(a, (XL, XH), [(x_index(i), x_index(i ^ flip)) for i in range...  10.7 us
    pallas_call x3, Pallas kernels, layer(): pl.pallas_call(functools.partial(layer_body, order, first, last), out_sha...  10.2 us
    ppermute x4, waiting for transfers between devices, swap_z(): return lax.ppermute(a, Z, list(enumerate(partners)))  7.8 us
    pallas_call x1, Pallas kernels, partials(): pl.pallas_call(partial_body, out_shape=[jax.ShapeDtypeStruct((2 * ROWS, W...  4.12 us
  transfers between devices with their start and end apart: 29, of which 19 were waited for; matrix products, arithmetic and copies ran while one was open for 1% of the time, Pallas kernels for 17%

profile of v3, /device:TPU:2, one launch (start us, length us, event | category | flops | bytes accessed | tf_op | source)
XLA Modules:
  0.0 104.9 jit_solution(17579216220396589859)
XLA Ops:
  6.8 2.2 %collective-permute-start.9 = (bf16[256,1024]{1,0:T(8,128)(2,1)S(1)}, bf16[256,1024]{1,0:T(8,128)(2,1)S(1)}, u32[]{:S(2)}, u32[]{:S(2)}) collective-permute-start(bf16[256,1024]{1,0:T(8,128)(2,1)S(1)} %copy-done.3), channel_id=1, source_target_pairs={{0,6},{2,4},{4,2},{6,0},{1,7},{3,5},{5,3},{7,1},{8,14},{10,12},{12... | collective-permute-start | bytes 1572872 | tf_op jit(solution)/shard_map/ppermute | solution.py:25
  9.0 4.1 %shard_map.93 = (bf16[512,1024]{1,0:T(8,128)(2,1)S(1)}, bf16[4,128,1024]{2,1,0:T(8,128)(2,1)S(1)}, bf16[4,128,640]{2,1,0:T(8,128)(2,1)S(1)}, bf16[4,128,640]{2,1...) custom-call(s32[4]{0:T(128)S(1)} %pad_add_fusion.pos, ...), custom_call_target="tpu_custom_call" | custom-call | flops 2147483648 | bytes 9437184 | tf_op jit(solution)/shard_map/pallas_call | solution.py:118
  15.5 2.2 %collective-permute-done.8.refs_1_ = bf16[256,1024]{1,0:T(8,128)(2,1)S(1)} collective-permute-done((bf16[256,1024]{1,0:T(8,128)(2,1)S(1)}, bf16[256,1024]{1,0:T(8,128)(2,1)S(1)}, u32[]{:S(2)}, u32[]{:S(2)}) %collective-permute-start.8) | collective-permute-done | bytes 524320 | tf_op jit(solution)/shard_map/ppermute | solution.py:25
  17.7 2.4 %collective-permute-done.7.refs_3_ = bf16[256,1024]{1,0:T(8,128)(2,1)S(1)} collective-permute-done((bf16[256,1024]{1,0:T(8,128)(2,1)S(1)}, bf16[256,1024]{1,0:T(8,128)(2,1)S(1)}, u32[]{:S(2)}, u32[]{:S(2)}) %collective-permute-start.7) | collective-permute-done | bytes 524320 | tf_op jit(solution)/shard_map/ppermute | solution.py:33
  21.6 2.3 %collective-permute-start.11 = (bf16[384,1024]{1,0:T(8,128)(2,1)S(1)}, bf16[384,1024]{1,0:T(8,128)(2,1)S(1)}, u32[]{:S(2)}, u32[]{:S(2)}) collective-permute-start(bf16[384,1024]{1,0:T(8,128)(2,1)S(1)} %get-tuple-element.143), channel_id=1, source_target_pairs={{0,6},{2,4},{4,2},{6,0},{1,7},{3,5},{5,3},{7,1},{8,14},{10,12},{12... | collective-permute-start | bytes 2359304 | tf_op jit(solution)/shard_map/ppermute | solution.py:25
  23.9 1.8 %collective-permute-start.2 = (bf16[4,128,640]{2,1,0:T(8,128)(2,1)S(1)}, bf16[4,128,640]{2,1,0:T(8,128)(2,1)S(1)}, u32[]{:S(2)}, u32[]{:S(2)}) collective-permute-start(bf16[4,128,640]{2,1,0:T(8,128)(2,1)S(1)} %get-tuple-element.73), channel_id=1, source_target_pairs={{0,128},{128,0},{8,136},{136,8},{1,129},{129,1},{9,137},{137,9},{2... | collective-permute-start | bytes 1966088 | tf_op jit(solution)/shard_map/ppermute | solution.py:33
  25.7 4.5 %shard_map.95 = (bf16[256,4096]{1,0:T(8,128)(2,1)}, bf16[256,2048]{1,0:T(8,128)(2,1)S(1)}, f32[8,1024]{1,0:T(8,128)S(1)}, f32[512,1024]{1,0:T(8,128)S(1)}) custom-call(s32[4]{0:T(128)S(1)} %pad_add_fusion.pos, bf16[256,4096]{1,0:T(8,128)(2,1)S(1)} %copy-done, bf16[256,2048]{1,0:T(8,128)(2,1)S(1)} %collective-permute-done.tok_other, ...), custom_call_target="tpu_custom_call" | custom-call | flops 1 | bytes 1 | tf_op jit(solution)/shard_map/pallas_call | solution.py:311
  31.5 4.4 %collective-permute-done.3.three = bf16[4,128,768]{2,1,0:T(8,128)(2,1)S(1)} collective-permute-done((bf16[4,128,768]{2,1,0:T(8,128)(2,1)S(1)}, bf16[4,128,768]{2,1,0:T(8,128)(2,1)S(1)}, u32[]{:S(2)}, u32[]{:S(2)}) %collective-permute-start.3) | collective-permute-done | bytes 786464 | tf_op jit(solution)/shard_map/ppermute | solution.py:33
  36.1 2.3 %collective-permute-start.5 = (bf16[4,128,384]{2,1,0:T(8,128)(2,1)S(1)}, bf16[4,128,384]{2,1,0:T(8,128)(2,1)S(1)}, u32[]{:S(2)}, u32[]{:S(2)}) collective-permute-start(bf16[4,128,384]{2,1,0:T(8,128)(2,1)S(1)} %get-tuple-element.78), channel_id=1, source_target_pairs={{0,128},{128,0},{8,136},{136,8},{1,129},{129,1},{9,137},{137,9},{2... | collective-permute-start | bytes 1179656 | tf_op jit(solution)/shard_map/ppermute | solution.py:33
  42.2 1.8 %collective-permute-start.13 = (bf16[128,1024]{1,0:T(8,128)(2,1)S(1)}, bf16[128,1024]{1,0:T(8,128)(2,1)S(1)}, u32[]{:S(2)}, u32[]{:S(2)}) collective-permute-start(bf16[128,1024]{1,0:T(8,128)(2,1)S(1)} %get-tuple-element.140), channel_id=1, source_target_pairs={{0,6},{2,4},{4,2},{6,0},{1,7},{3,5},{5,3},{7,1},{8,14},{10,12},{12... | collective-permute-start | bytes 786440 | tf_op jit(solution)/shard_map/ppermute | solution.py:25
  44.2 3.7 %shard_map.96 = (bf16[256,4096]{1,0:T(8,128)(2,1)}, bf16[256,2048]{1,0:T(8,128)(2,1)S(1)}, f32[8,1024]{1,0:T(8,128)S(1)}, f32[512,1024]{1,0:T(8,128)S(1)}) custom-call(s32[4]{0:T(128)S(1)} %pad_add_fusion.pos, bf16[256,4096]{1,0:T(8,128)(2,1)S(1)} %copy-done.1, ...), custom_call_target="tpu_custom_call", output_to_operand_aliasing={{0}: (12, {}), {1}: (13, {})} | custom-call | flops 1 | bytes 1 | tf_op jit(solution)/shard_map/pallas_call | solution.py:311
  48.3 1.8 %collective-permute-done.13 = bf16[128,1024]{1,0:T(8,128)(2,1)S(1)} collective-permute-done((bf16[128,1024]{1,0:T(8,128)(2,1)S(1)}, bf16[128,1024]{1,0:T(8,128)(2,1)S(1)}, u32[]{:S(2)}, u32[]{:S(2)}) %collective-permute-start.13) | collective-permute-done | bytes 262176 | tf_op jit(solution)/shard_map/ppermute | solution.py:25
  50.1 2.0 %shard_map.97 = (bf16[256,4096]{1,0:T(8,128)(2,1)}, bf16[256,2048]{1,0:T(8,128)(2,1)S(1)}, f32[8,1024]{1,0:T(8,128)S(1)}, f32[256,1024]{1,0:T(8,128)S(1)}, bf16[256,1024]{1,0:T(8,128)(2,1)S(1)}) custom-call(s32[4]{0:T(128)S(1)} %pad_add_fusion.pos, bf16[256,4096]{1,0:T(8,128)(2,1)S(1)} %copy-done.1, ...), custom_call_target="tpu_custom_call", output_to_operand_aliasing={{0}: (10, {}), {1}: (11, {})} | custom-call | flops 1 | bytes 1 | tf_op jit(solution)/shard_map/pallas_call | solution.py:311
  52.1 2.1 %collective-permute-done.6.late_three = bf16[4,128,640]{2,1,0:T(8,128)(2,1)S(1)} collective-permute-done((bf16[4,128,640]{2,1,0:T(8,128)(2,1)S(1)}, bf16[4,128,640]{2,1,0:T(8,128)(2,1)S(1)}, u32[]{:S(2)}, u32[]{:S(2)}) %collective-permute-start.6) | collective-permute-done | bytes 655392 | tf_op jit(solution)/shard_map/ppermute | solution.py:33
  61.3 6.0 %collective-permute-done.18 = f32[8,1024]{1,0:T(8,128)S(1)} collective-permute-done((f32[8,1024]{1,0:T(8,128)S(1)}, f32[8,1024]{1,0:T(8,128)S(1)}, u32[]{:S(2)}, u32[]{:S(2)}) %collective-permute-start.18) | collective-permute-done | bytes 32800 | tf_op jit(solution)/shard_map/ppermute | solution.py:25
  70.8 3.5 %collective-permute-done.19 = bf16[64,1024]{1,0:T(8,128)(2,1)S(1)} collective-permute-done((bf16[64,1024]{1,0:T(8,128)(2,1)S(1)}, bf16[64,1024]{1,0:T(8,128)(2,1)S(1)}, u32[]{:S(2)}, u32[]{:S(2)}) %collective-permute-start.19) | collective-permute-done | bytes 131104 | tf_op jit(solution)/shard_map/ppermute | solution.py:37
  74.3 5.5 %collective-permute-start.20 = (bf16[64,1024]{1,0:T(8,128)(2,1)S(1)}, bf16[64,1024]{1,0:T(8,128)(2,1)S(1)}, u32[]{:S(2)}, u32[]{:S(2)}) collective-permute-start(bf16[64,1024]{1,0:T(8,128)(2,1)S(1)} %add_convert_fusion.2), channel_id=1, source_target_pairs={{0,112},{16,32},{32,16},{48,64},{64,48},{80,96},{96,80},{112,0},{1... | collective-permute-start | bytes 393224 | tf_op jit(solution)/shard_map/ppermute | solution.py:37
  79.8 2.4 %collective-permute-start.21 = (f32[8,1024]{1,0:T(8,128)S(1)}, f32[8,1024]{1,0:T(8,128)S(1)}, u32[]{:S(2)}, u32[]{:S(2)}) collective-permute-start(f32[8,1024]{1,0:T(8,128)S(1)} %add.32), channel_id=1, source_target_pairs={{0,6},{2,4},{4,2},{6,0},{1,7},{3,5},{5,3},{7,1},{8,14},{10,12},{12... | collective-permute-start | bytes 98312 | tf_op jit(solution)/shard_map/ppermute | solution.py:25
  82.2 2.7 %collective-permute-done.21 = f32[8,1024]{1,0:T(8,128)S(1)} collective-permute-done((f32[8,1024]{1,0:T(8,128)S(1)}, f32[8,1024]{1,0:T(8,128)S(1)}, u32[]{:S(2)}, u32[]{:S(2)}) %collective-permute-start.21) | collective-permute-done | bytes 32800 | tf_op jit(solution)/shard_map/ppermute | solution.py:25
  84.9 2.9 %collective-permute-start.23 = (f32[8,1024]{1,0:T(8,128)S(1)}, f32[8,1024]{1,0:T(8,128)S(1)}, u32[]{:S(2)}, u32[]{:S(2)}) collective-permute-start(f32[8,1024]{1,0:T(8,128)S(1)} %add.34.mine), channel_id=1, source_target_pairs={{0,8},{128,136},{8,0},{136,128},{1,9},{129,137},{9,1},{137,129},{2... | collective-permute-start | bytes 98312 | tf_op jit(solution)/shard_map/ppermute | solution.py:33
  87.8 2.0 %collective-permute-start.22 = (bf16[64,1024]{1,0:T(8,128)(2,1)S(1)}, bf16[64,1024]{1,0:T(8,128)(2,1)S(1)}, u32[]{:S(2)}, u32[]{:S(2)}) collective-permute-start(bf16[64,1024]{1,0:T(8,128)(2,1)S(1)} %add_convert_fusion.1), channel_id=1, source_target_pairs={{0,48},{16,96},{32,80},{48,0},{64,112},{80,32},{96,16},{112,64},{1... | collective-permute-start | bytes 393224 | tf_op jit(solution)/shard_map/ppermute | solution.py:37
  92.4 4.1 %collective-permute-done.22 = bf16[64,1024]{1,0:T(8,128)(2,1)S(1)} collective-permute-done((bf16[64,1024]{1,0:T(8,128)(2,1)S(1)}, bf16[64,1024]{1,0:T(8,128)(2,1)S(1)}, u32[]{:S(2)}, u32[]{:S(2)}) %collective-permute-start.22) | collective-permute-done | bytes 131104 | tf_op jit(solution)/shard_map/ppermute | solution.py:37
  97.5 2.6 %collective-permute-start.26 = (bf16[64,1024]{1,0:T(8,128)(2,1)S(1)}, bf16[64,1024]{1,0:T(8,128)(2,1)S(1)}, u32[]{:S(2)}, u32[]{:S(2)}) collective-permute-start(bf16[64,1024]{1,0:T(8,128)(2,1)S(1)} %add_convert_fusion.own), channel_id=1, source_target_pairs={{0,16},{16,0},{32,48},{48,32},{64,80},{80,64},{96,112},{112,96},{1... | collective-permute-start | bytes 393224 | tf_op jit(solution)/shard_map/ppermute | solution.py:37
  100.8 1.9 %collective-permute-done.28.by_both = bf16[64,1024]{1,0:T(8,128)(2,1)S(1)} collective-permute-done((bf16[64,1024]{1,0:T(8,128)(2,1)S(1)}, bf16[64,1024]{1,0:T(8,128)(2,1)S(1)}, u32[]{:S(2)}, u32[]{:S(2)}) %collective-permute-start.28) | collective-permute-done | bytes 131104 | tf_op jit(solution)/shard_map/ppermute | solution.py:427
  (74 shorter events, 32.7 us)
Async XLA Ops:
  3.2 5.9 %collective-permute-start = (bf16[256,2048]{1,0:T(8,128)(2,1)S(1)}, bf16[256,2048]{1,0:T(8,128)(2,1)S(1)}, u32[]{:S(2)}, u32[]{:S(2)}) collective-permute-start(bf16[256,2048]{1,0:T(8,128)(2,1)S(1)} %shard_map.92), channel_id=1, source_target_pairs={{0,1},{1,0},{2,3},{3,2},{4,5},{5,4},{6,7},{7,6},{8,9},{9,8},{10,11... | collective-permute-start | bytes 3145736 | tf_op jit(solution)/shard_map/ppermute | solution.py:21
  3.8 14.0 %collective-permute-start.8 = (bf16[256,1024]{1,0:T(8,128)(2,1)S(1)}, bf16[256,1024]{1,0:T(8,128)(2,1)S(1)}, u32[]{:S(2)}, u32[]{:S(2)}) collective-permute-start(bf16[256,1024]{1,0:T(8,128)(2,1)S(1)} %copy-done.3), channel_id=1, source_target_pairs={{0,2},{2,0},{4,6},{6,4},{1,3},{3,1},{5,7},{7,5},{8,10},{10,8},{12,... | collective-permute-start | bytes 1572872 | tf_op jit(solution)/shard_map/ppermute | solution.py:25
  5.3 14.8 %collective-permute-start.7 = (bf16[256,1024]{1,0:T(8,128)(2,1)S(1)}, bf16[256,1024]{1,0:T(8,128)(2,1)S(1)}, u32[]{:S(2)}, u32[]{:S(2)}) collective-permute-start(bf16[256,1024]{1,0:T(8,128)(2,1)S(1)} %copy-done.3), channel_id=1, source_target_pairs={{0,136},{128,8},{8,128},{136,0},{1,137},{129,9},{9,129},{137,1},{2... | collective-permute-start | bytes 1572872 | tf_op jit(solution)/shard_map/ppermute | solution.py:33
  6.8 14.6 %collective-permute-start.9 = (bf16[256,1024]{1,0:T(8,128)(2,1)S(1)}, bf16[256,1024]{1,0:T(8,128)(2,1)S(1)}, u32[]{:S(2)}, u32[]{:S(2)}) collective-permute-start(bf16[256,1024]{1,0:T(8,128)(2,1)S(1)} %copy-done.3), channel_id=1, source_target_pairs={{0,6},{2,4},{4,2},{6,0},{1,7},{3,5},{5,3},{7,1},{8,14},{10,12},{12... | collective-permute-start | bytes 1572872 | tf_op jit(solution)/shard_map/ppermute | solution.py:25
  13.2 22.7 %collective-permute-start.3 = (bf16[4,128,768]{2,1,0:T(8,128)(2,1)S(1)}, bf16[4,128,768]{2,1,0:T(8,128)(2,1)S(1)}, u32[]{:S(2)}, u32[]{:S(2)}) collective-permute-start(bf16[4,128,768]{2,1,0:T(8,128)(2,1)S(1)} %get-tuple-element.74), channel_id=1, source_target_pairs={{0,136},{128,8},{8,128},{136,0},{1,137},{129,9},{9,129},{137,1},{2... | collective-permute-start | bytes 2359304 | tf_op jit(solution)/shard_map/ppermute | solution.py:33
  13.8 17.7 %collective-permute-start.4 = (bf16[4,128,640]{2,1,0:T(8,128)(2,1)S(1)}, bf16[4,128,640]{2,1,0:T(8,128)(2,1)S(1)}, u32[]{:S(2)}, u32[]{:S(2)}) collective-permute-start(bf16[4,128,640]{2,1,0:T(8,128)(2,1)S(1)} %get-tuple-element.77), channel_id=1, source_target_pairs={{0,128},{128,0},{8,136},{136,8},{1,129},{129,1},{9,137},{137,9},{2... | collective-permute-start | bytes 1966088 | tf_op jit(solution)/shard_map/ppermute | solution.py:33
  21.6 19.4 %collective-permute-start.11 = (bf16[384,1024]{1,0:T(8,128)(2,1)S(1)}, bf16[384,1024]{1,0:T(8,128)(2,1)S(1)}, u32[]{:S(2)}, u32[]{:S(2)}) collective-permute-start(bf16[384,1024]{1,0:T(8,128)(2,1)S(1)} %get-tuple-element.143), channel_id=1, source_target_pairs={{0,6},{2,4},{4,2},{6,0},{1,7},{3,5},{5,3},{7,1},{8,14},{10,12},{12... | collective-permute-start | bytes 2359304 | tf_op jit(solution)/shard_map/ppermute | solution.py:25
  23.9 17.8 %collective-permute-start.10 = (bf16[384,1024]{1,0:T(8,128)(2,1)S(1)}, bf16[384,1024]{1,0:T(8,128)(2,1)S(1)}, u32[]{:S(2)}, u32[]{:S(2)}) collective-permute-start(bf16[384,1024]{1,0:T(8,128)(2,1)S(1)} %get-tuple-element.144), channel_id=1, source_target_pairs={{0,2},{2,0},{4,6},{6,4},{1,3},{3,1},{5,7},{7,5},{8,10},{10,8},{12,... | collective-permute-start | bytes 2359304 | tf_op jit(solution)/shard_map/ppermute | solution.py:25
  23.9 28.2 %collective-permute-start.2 = (bf16[4,128,640]{2,1,0:T(8,128)(2,1)S(1)}, bf16[4,128,640]{2,1,0:T(8,128)(2,1)S(1)}, u32[]{:S(2)}, u32[]{:S(2)}) collective-permute-start(bf16[4,128,640]{2,1,0:T(8,128)(2,1)S(1)} %get-tuple-element.73), channel_id=1, source_target_pairs={{0,128},{128,0},{8,136},{136,8},{1,129},{129,1},{9,137},{137,9},{2... | collective-permute-start | bytes 1966088 | tf_op jit(solution)/shard_map/ppermute | solution.py:33
  36.1 15.9 %collective-permute-start.5 = (bf16[4,128,384]{2,1,0:T(8,128)(2,1)S(1)}, bf16[4,128,384]{2,1,0:T(8,128)(2,1)S(1)}, u32[]{:S(2)}, u32[]{:S(2)}) collective-permute-start(bf16[4,128,384]{2,1,0:T(8,128)(2,1)S(1)} %get-tuple-element.78), channel_id=1, source_target_pairs={{0,128},{128,0},{8,136},{136,8},{1,129},{129,1},{9,137},{137,9},{2... | collective-permute-start | bytes 1179656 | tf_op jit(solution)/shard_map/ppermute | solution.py:33
  38.5 15.7 %collective-permute-start.6 = (bf16[4,128,640]{2,1,0:T(8,128)(2,1)S(1)}, bf16[4,128,640]{2,1,0:T(8,128)(2,1)S(1)}, u32[]{:S(2)}, u32[]{:S(2)}) collective-permute-start(bf16[4,128,640]{2,1,0:T(8,128)(2,1)S(1)} %get-tuple-element.79), channel_id=1, source_target_pairs={{0,136},{128,8},{8,128},{136,0},{1,137},{129,9},{9,129},{137,1},{2... | collective-permute-start | bytes 1966088 | tf_op jit(solution)/shard_map/ppermute | solution.py:33
  41.8 6.5 %collective-permute-start.12 = (bf16[128,1024]{1,0:T(8,128)(2,1)S(1)}, bf16[128,1024]{1,0:T(8,128)(2,1)S(1)}, u32[]{:S(2)}, u32[]{:S(2)}) collective-permute-start(bf16[128,1024]{1,0:T(8,128)(2,1)S(1)} %get-tuple-element.142), channel_id=1, source_target_pairs={{0,2},{2,0},{4,6},{6,4},{1,3},{3,1},{5,7},{7,5},{8,10},{10,8},{12,... | collective-permute-start | bytes 786440 | tf_op jit(solution)/shard_map/ppermute | solution.py:25
  42.2 7.8 %collective-permute-start.13 = (bf16[128,1024]{1,0:T(8,128)(2,1)S(1)}, bf16[128,1024]{1,0:T(8,128)(2,1)S(1)}, u32[]{:S(2)}, u32[]{:S(2)}) collective-permute-start(bf16[128,1024]{1,0:T(8,128)(2,1)S(1)} %get-tuple-element.140), channel_id=1, source_target_pairs={{0,6},{2,4},{4,2},{6,0},{1,7},{3,5},{5,3},{7,1},{8,14},{10,12},{12... | collective-permute-start | bytes 786440 | tf_op jit(solution)/shard_map/ppermute | solution.py:25
  54.6 12.8 %collective-permute-start.14 = (bf16[128,1024]{1,0:T(8,128)(2,1)S(1)}, bf16[128,1024]{1,0:T(8,128)(2,1)S(1)}, u32[]{:S(2)}, u32[]{:S(2)}) collective-permute-start(bf16[128,1024]{1,0:T(8,128)(2,1)S(1)} %get-tuple-element.115), channel_id=1, source_target_pairs={{0,2},{2,0},{4,6},{6,4},{1,3},{3,1},{5,7},{7,5},{8,10},{10,8},{12,... | collective-permute-start | bytes 786440 | tf_op jit(solution)/shard_map/ppermute | solution.py:25
  56.0 12.6 %collective-permute-start.15 = (bf16[128,1024]{1,0:T(8,128)(2,1)S(1)}, bf16[128,1024]{1,0:T(8,128)(2,1)S(1)}, u32[]{:S(2)}, u32[]{:S(2)}) collective-permute-start(bf16[128,1024]{1,0:T(8,128)(2,1)S(1)} %get-tuple-element.116), channel_id=1, source_target_pairs={{0,6},{2,4},{4,2},{6,0},{1,7},{3,5},{5,3},{7,1},{8,14},{10,12},{12... | collective-permute-start | bytes 786440 | tf_op jit(solution)/shard_map/ppermute | solution.py:25
  57.7 10.9 %collective-permute-start.16 = (bf16[128,1024]{1,0:T(8,128)(2,1)S(1)}, bf16[128,1024]{1,0:T(8,128)(2,1)S(1)}, u32[]{:S(2)}, u32[]{:S(2)}) collective-permute-start(bf16[128,1024]{1,0:T(8,128)(2,1)S(1)} %get-tuple-element.117), channel_id=1, source_target_pairs={{0,4},{2,6},{4,0},{6,2},{1,5},{3,7},{5,1},{7,3},{8,12},{10,14},{12... | collective-permute-start | bytes 786440 | tf_op jit(solution)/shard_map/ppermute | solution.py:25
  58.8 32.0 %collective-permute-start.25 = (bf16[256,2048]{1,0:T(8,128)(2,1)S(1)}, bf16[256,2048]{1,0:T(8,128)(2,1)S(1)}, u32[]{:S(2)}, u32[]{:S(2)}) collective-permute-start(bf16[256,2048]{1,0:T(8,128)(2,1)S(1)} %get-tuple-element.131), channel_id=1, source_target_pairs={{0,1},{1,0},{2,3},{3,2},{4,5},{5,4},{6,7},{7,6},{8,9},{9,8},{10,11... | collective-permute-start | bytes 3145736 | tf_op jit(solution)/shard_map/ppermute | solution.py:21
  60.0 7.4 %collective-permute-start.18 = (f32[8,1024]{1,0:T(8,128)S(1)}, f32[8,1024]{1,0:T(8,128)S(1)}, u32[]{:S(2)}, u32[]{:S(2)}) collective-permute-start(f32[8,1024]{1,0:T(8,128)S(1)} %add.31), channel_id=1, source_target_pairs={{0,2},{2,0},{4,6},{6,4},{1,3},{3,1},{5,7},{7,5},{8,10},{10,8},{12,... | collective-permute-start | bytes 98312 | tf_op jit(solution)/shard_map/ppermute | solution.py:25
  70.8 19.1 %collective-permute-start.24 = (bf16[256,1024]{1,0:T(8,128)(2,1)S(1)}, bf16[256,1024]{1,0:T(8,128)(2,1)S(1)}, u32[]{:S(2)}, u32[]{:S(2)}) collective-permute-start(bf16[256,1024]{1,0:T(8,128)(2,1)S(1)} %get-tuple-element.130), channel_id=1, source_target_pairs={{0,1},{1,0},{2,3},{3,2},{4,5},{5,4},{6,7},{7,6},{8,9},{9,8},{10,11... | collective-permute-start | bytes 1572872 | tf_op jit(solution)/shard_map/ppermute | solution.py:21
  74.3 10.6 %collective-permute-start.20 = (bf16[64,1024]{1,0:T(8,128)(2,1)S(1)}, bf16[64,1024]{1,0:T(8,128)(2,1)S(1)}, u32[]{:S(2)}, u32[]{:S(2)}) collective-permute-start(bf16[64,1024]{1,0:T(8,128)(2,1)S(1)} %add_convert_fusion.2), channel_id=1, source_target_pairs={{0,112},{16,32},{32,16},{48,64},{64,48},{80,96},{96,80},{112,0},{1... | collective-permute-start | bytes 393224 | tf_op jit(solution)/shard_map/ppermute | solution.py:37
  84.9 7.4 %collective-permute-start.23 = (f32[8,1024]{1,0:T(8,128)S(1)}, f32[8,1024]{1,0:T(8,128)S(1)}, u32[]{:S(2)}, u32[]{:S(2)}) collective-permute-start(f32[8,1024]{1,0:T(8,128)S(1)} %add.34.mine), channel_id=1, source_target_pairs={{0,8},{128,136},{8,0},{136,128},{1,9},{129,137},{9,1},{137,129},{2... | collective-permute-start | bytes 98312 | tf_op jit(solution)/shard_map/ppermute | solution.py:33
  87.8 8.7 %collective-permute-start.22 = (bf16[64,1024]{1,0:T(8,128)(2,1)S(1)}, bf16[64,1024]{1,0:T(8,128)(2,1)S(1)}, u32[]{:S(2)}, u32[]{:S(2)}) collective-permute-start(bf16[64,1024]{1,0:T(8,128)(2,1)S(1)} %add_convert_fusion.1), channel_id=1, source_target_pairs={{0,48},{16,96},{32,80},{48,0},{64,112},{80,32},{96,16},{112,64},{1... | collective-permute-start | bytes 393224 | tf_op jit(solution)/shard_map/ppermute | solution.py:37
  96.6 6.1 %collective-permute-start.28 = (bf16[64,1024]{1,0:T(8,128)(2,1)S(1)}, bf16[64,1024]{1,0:T(8,128)(2,1)S(1)}, u32[]{:S(2)}, u32[]{:S(2)}) collective-permute-start(bf16[64,1024]{1,0:T(8,128)(2,1)S(1)} %add_convert_fusion.own), channel_id=1, source_target_pairs={{0,144},{16,128},{32,176},{48,160},{64,208},{80,192},{96,240},{112... | collective-permute-start | bytes 393224 | tf_op jit(solution)/shard_map/ppermute | solution.py:427
  96.7 6.5 %collective-permute-start.27 = (bf16[64,1024]{1,0:T(8,128)(2,1)S(1)}, bf16[64,1024]{1,0:T(8,128)(2,1)S(1)}, u32[]{:S(2)}, u32[]{:S(2)}) collective-permute-start(bf16[64,1024]{1,0:T(8,128)(2,1)S(1)} %add_convert_fusion.own), channel_id=1, source_target_pairs={{0,128},{128,0},{8,136},{136,8},{1,129},{129,1},{9,137},{137,9},{2... | collective-permute-start | bytes 393224 | tf_op jit(solution)/shard_map/ppermute | solution.py:33
  (11 other events, 46.0 us)

commit v4 on v3

--- a/solution.py
+++ b/solution.py
@@ -12,7 +12,7 @@
 ROWS, DEPTH, WIDTH, PIECE = 256, 4096, 1024, 256
 LOW, LANE = 640, PIECE // 2
 HIGH = WIDTH - LOW
-PASSING = 4 * 2**30
+PASSING = 2 * 2**30
 VMEM = pl.BlockSpec(memory_space=pltpu.VMEM)
 PARAMS = pltpu.CompilerParams(vmem_limit_bytes=40 * 2**20)
 
@@ -21,16 +21,20 @@
     return lax.ppermute(a, C, [(0, 1), (1, 0)])
 
 
-def swap_y(a, flip):
-    return lax.ppermute(a, Y, [(i, i ^ flip) for i in range(4)])
+BOTH, ONE = (0, 1), (1,)
+
+
+def swap_y(a, flip, cores=BOTH):
+    return lax.ppermute(a, (Y, C), [(i * 2 + c, (i ^ flip) * 2 + c) for i in range(4) for c in cores])
 
 
 def x_index(place):
     return (place % 2) * 2 + place // 2
 
 
-def swap_x(a, flip):
-    return lax.ppermute(a, (XL, XH), [(x_index(i), x_index(i ^ flip)) for i in range(4)])
+def swap_x(a, flip, cores=BOTH):
+    pairs = [(x_index(i), x_index(i ^ flip)) for i in range(4)]
+    return lax.ppermute(a, (XL, XH, C), [(i * 2 + c, j * 2 + c) for i, j in pairs for c in cores])
 
 
 def swap_z(a, partners):
@@ -81,74 +85,80 @@
     )(pos, tokens)
 
 
-def partial_body(pos, tok, tok_other, cot, cot_other, in_scale, out_scale, grad_ref, *refs):
-    stay, one, early_one, three, late_one, late_three, left = refs
-    i = pl.program_id(0)
-
-    @pl.when(i == 0)
-    def _():
-        grad_ref[:ROWS] = (cot[...].astype(F32) * out_scale[...]).astype(BF16)
-        grad_ref[ROWS:] = (cot_other[...].astype(F32) * out_scale[...]).astype(BF16)
-
-    y_at = pos[1] ^ i
-    for k in range(4):
+def scaled_pieces(pos, flips, tok, tok_other, in_scale, left):
+    y_at = pos[1] ^ pl.program_id(0)
+    for n, k in enumerate(flips):
         x_at = pos[0] ^ k
         place = (x_at // 2) * 4 + y_at
         wide = pl.ds(pl.multiple_of(((place * 2 + pos[2]) * 2 + x_at % 2) * LANE, LANE), LANE)
         narrow = pl.ds(pl.multiple_of((place * 2 + x_at % 2) * LANE, LANE), LANE)
         scale = in_scale[:, wide]
-        left[:ROWS, k * LANE : (k + 1) * LANE] = (tok[:, wide].astype(F32) * scale).astype(BF16)
-        left[ROWS:, k * LANE : (k + 1) * LANE] = (tok_other[:, narrow].astype(F32) * scale).astype(BF16)
-    part = lax.dot_general(
-        left[...], grad_ref[...], (((0,), (0,)), ((), ())), preferred_element_type=F32
-    ).astype(BF16)
+        left[:ROWS, n * LANE : (n + 1) * LANE] = (tok[:, wide].astype(F32) * scale).astype(BF16)
+        left[ROWS:, n * LANE : (n + 1) * LANE] = (tok_other[:, narrow].astype(F32) * scale).astype(BF16)
+
+
+def product(left, grad):
+    return lax.dot_general(left, grad, (((0,), (0,)), ((), ())), preferred_element_type=F32).astype(BF16)
+
+
+def first_body(pos, tok, tok_other, in_scale, cot, cot_other, out_scale, grad_ref, one, three, left):
+    @pl.when(pl.program_id(0) == 0)
+    def _():
+        grad_ref[:ROWS] = (cot[...].astype(F32) * out_scale[...]).astype(BF16)
+        grad_ref[ROWS:] = (cot_other[...].astype(F32) * out_scale[...]).astype(BF16)
+
+    scaled_pieces(pos, (2, 3), tok, tok_other, in_scale, left)
+    one[0] = product(left[:, :LANE], grad_ref[:, :LOW])
+    part = product(left[...], grad_ref[:, LOW:])
+    three[0, :, :HIGH] = part[:LANE]
+    three[0, :, HIGH:] = part[LANE:]
+
+
+def rest_body(pos, tok, tok_other, in_scale, grad_ref, stay, early_one, late_one, late_three, left):
+    scaled_pieces(pos, (0, 1, 3), tok, tok_other, in_scale, left)
+    part = product(left[:, : 2 * LANE], grad_ref[...])
     stay[0] = part[:LANE]
-    low, high = slice(0, LOW), slice(LOW, WIDTH)
-    one[0] = part[2 * LANE : 3 * LANE, low]
-    early_one[0] = part[LANE : 2 * LANE, low]
-    three[0, :, :HIGH] = part[2 * LANE : 3 * LANE, high]
-    three[0, :, HIGH:] = part[3 * LANE :, high]
-    late_one[0] = part[LANE : 2 * LANE, high]
-    late_three[0] = part[3 * LANE :, low]
-
-
-def partials(pos, tokens, tok_other, cot, cot_other, in_scale, out_scale):
+    early_one[0] = part[LANE:, :LOW]
+    late_one[0] = part[LANE:, LOW:]
+    late_three[0] = product(left[:, 2 * LANE :], grad_ref[:, :LOW])
+
+
+def partials(body, pieces, columns, pos, tokens, tok_other, in_scale, grads):
     whole = lambda shape: pl.BlockSpec(shape, lambda i, pos: (0,) * len(shape))
-    columns = (WIDTH, LOW, LOW, 2 * HIGH, HIGH, LOW)
-    return pl.pallas_call(
-        partial_body,
-        out_shape=[jax.ShapeDtypeStruct((2 * ROWS, WIDTH), BF16)]
-        + [jax.ShapeDtypeStruct((4, LANE, n), BF16) for n in columns],
+    out_shape = [jax.ShapeDtypeStruct((4, LANE, n), BF16) for n in columns]
+    out_specs = [pl.BlockSpec((1, LANE, n), lambda i, pos: (i, 0, 0)) for n in columns]
+    if len(grads) > 1:
+        out_shape = [jax.ShapeDtypeStruct((2 * ROWS, WIDTH), BF16)] + out_shape
+        out_specs = [whole((2 * ROWS, WIDTH))] + out_specs
+    return pl.pallas_call(
+        body,
+        out_shape=out_shape,
         grid_spec=pltpu.PrefetchScalarGridSpec(
             num_scalar_prefetch=1,
             grid=(4,),
-            in_specs=[
-                whole((ROWS, DEPTH)), whole((ROWS, DEPTH // 2)), whole((ROWS, WIDTH)),
-                whole((ROWS, WIDTH)), whole((1, DEPTH)), whole((1, WIDTH)),
-            ],
-            out_specs=[whole((2 * ROWS, WIDTH))]
-            + [pl.BlockSpec((1, LANE, n), lambda i, pos: (i, 0, 0)) for n in columns],
-            scratch_shapes=[pltpu.VMEM((2 * ROWS, 4 * LANE), BF16)],
+            in_specs=[whole((ROWS, DEPTH)), whole((ROWS, DEPTH // 2)), whole((1, DEPTH))]
+            + [whole(g.shape) for g in grads],
+            out_specs=out_specs,
+            scratch_shapes=[pltpu.VMEM((2 * ROWS, pieces * LANE), BF16)],
         ),
         compiler_params=PARAMS,
-        cost_estimate=cost(2 * 2 * ROWS * DEPTH // 2 * WIDTH, 9 * 2**20),
-    )(pos, tokens, tok_other, cot, cot_other, in_scale, out_scale)
-
-
-def add_body(late_one, late_three, one, three, one_out, three_out):
-    one_out[...] = (late_one[...].astype(F32) + three[:, :, :HIGH].astype(F32)).astype(BF16)
-    three_out[...] = (late_three[...].astype(F32) + one[...].astype(F32)).astype(BF16)
-
-
-def add_passing(late_one, late_three, one, three):
+        cost_estimate=cost(2 * ROWS * DEPTH // 2 * WIDTH, 5 * 2**20),
+    )(pos, tokens, tok_other, in_scale, *grads)
+
+
+def add_body(late, passing, out):
+    out[...] = (late[...].astype(F32) + passing[:, :, : out.shape[2]].astype(F32)).astype(BF16)
+
+
+def add_passing(late, passing):
     return pl.pallas_call(
         add_body,
-        out_shape=[jax.ShapeDtypeStruct(late_one.shape, BF16), jax.ShapeDtypeStruct(late_three.shape, BF16)],
-        in_specs=[VMEM] * 4,
-        out_specs=[VMEM] * 2,
+        out_shape=jax.ShapeDtypeStruct(late.shape, BF16),
+        in_specs=[VMEM] * 2,
+        out_specs=VMEM,
         compiler_params=PARAMS,
         cost_estimate=cost(PASSING, 3 * 2**20),
-    )(late_one, late_three, one, three)
+    )(late, passing)
 
 
 def sum_body(own, early_one, three, late_one, late_three, keep, s1, s2, s3):
@@ -349,22 +359,22 @@
     )(pos, others, own)
 
 
-def finish_body(scale, mine, other, in_ref, out_ref):
-    total = (mine[...] + other[...]) * scale
+def finish_body(scale, pos, mine, other, in_ref, out_ref):
+    total = jnp.where(pos[2] == 1, mine[...], other[...]) * scale
     for k in range(4):
         in_ref[:, k * WIDTH : (k + 1) * WIDTH] = total[k : k + 1]
     out_ref[...] = total[4:5]
 
 
-def finish(mine, other, scale):
+def finish(pos, mine, other, scale):
     return pl.pallas_call(
         functools.partial(finish_body, scale),
         out_shape=[jax.ShapeDtypeStruct((1, DEPTH), F32), jax.ShapeDtypeStruct((1, WIDTH), F32)],
-        in_specs=[VMEM] * 2,
+        in_specs=[SCALARS] + [VMEM] * 2,
         out_specs=[VMEM] * 2,
         compiler_params=PARAMS,
         cost_estimate=cost(2**14, 2**16),
-    )(mine, other)
+    )(pos, mine, other)
 
 
 def on_device(tokens, cotangent, slow_weight, in_scale, out_scale):
@@ -377,11 +387,15 @@
     one, three = swap_y(slow_weight, 1), swap_y(slow_weight, 3)
     far = swap_x(slow_weight, 3)
     tok_other = swap_core(other_half(pos, tokens))
-    grad, stay, by_one, early_one, by_three, late_one, late_three = partials(
-        pos, tokens, tok_other, cotangent, cot_other, in_scale, out_scale
+    grad, by_one, by_three = partials(
+        first_body, 2, (LOW, 2 * HIGH), pos, tokens, tok_other, in_scale, (cotangent, cot_other, out_scale)
     )
-    by_one, early_one, by_three = swap_x(by_one, 1), swap_x(early_one, 1), swap_x(by_three, 3)
-    far, one, three, grad = lax.optimization_barrier((far, one, three, grad))
+    by_one, by_three = swap_x(by_one, 1), swap_x(by_three, 3)
+    stay, early_one, late_one, late_three = partials(
+        rest_body, 3, (WIDTH, LOW, HIGH, LOW), pos, tokens, tok_other, in_scale, (grad,)
+    )
+    early_one = swap_x(early_one, 1)
+    far, one, three, grad, stay = lax.optimization_barrier((far, one, three, grad, stay))
 
     half = PIECE // 2
     far_one = swap_y(jnp.concatenate([far, three[:half]], axis=0), 1)
@@ -390,7 +404,8 @@
     run = functools.partial(layer, pos, orders)
     common = (tokens, tok_other, grad, in_scale, cotangent, cot_other)
     state = run(0, *common, (slow_weight, one, three, far))
-    late_one, late_three = add_passing(late_one, late_three, by_one, by_three)
+    late_three = add_passing(late_three, by_one)
+    late_one = add_passing(late_one, by_three)
     arrived = [early_one, by_three, swap_x(late_one, 1), swap_x(late_three, 3)]
     far_one, far_three, state, _ = lax.optimization_barrier((far_one, far_three, state, late_one))
 
@@ -398,34 +413,36 @@
     two = jnp.concatenate([far_one[PIECE:], far_three[PIECE:]], axis=0)
     state = run(1, *common, (two, far_one[:PIECE], far_three[:PIECE]), state)
     far_two, state = lax.optimization_barrier((far_two, state))
+    arrived, _ = lax.optimization_barrier((arrived, state[3]))
     state = run(2, *common, (jnp.concatenate(far_two, axis=0),), state)
-    arrived, state = lax.optimization_barrier((arrived, state))
     own, others, small, pre_own, pre_other = state
 
     stay, *out = sum_blocks(stay, arrived)
-    arrived = [swap_y(out[0], 1), swap_y(out[2], 3), swap_y(out[1], 2)]
+    two = swap_y(out[1], 2)
+    arrived = [two, swap_y(out[0], 1), swap_y(out[2], 3)]
     small = small + swap_core(small)
-    small = small + swap_y(small, 1)
+    small = small + swap_y(small, 1, ONE)
     arrived, small = lax.optimization_barrier((arrived, small))
 
     keep, out = join(pos, stay, arrived)
     out = swap_z(out, NEAR)
-    pre_other, others = swap_core(pre_other), swap_core(others)
+    small = small + swap_y(small, 3, ONE)
     out, small = lax.optimization_barrier((out, small))
     mine = (keep + out.astype(F32)).astype(BF16)
     out = swap_z(mine, NEXT)
-    small = small + swap_y(small, 3)
+    small = small + swap_x(small, 2, ONE)
     out, small = lax.optimization_barrier((out, small))
+    pre_other, others = swap_core(pre_other), swap_core(others)
     mine = (mine.astype(F32) + out.astype(F32)).astype(BF16)
     out = swap_z(mine, FAR)
-    small_far = swap_x(small, 2)
     result = ((pre_own + pre_other.astype(F32)) * out_scale).astype(BF16)
     grad_tokens = fill(pos, sum(orders, ()), others, own)
-    out, small_far, result, grad_tokens = lax.optimization_barrier((out, small_far, result, grad_tokens))
+    out, small, result, grad_tokens = lax.optimization_barrier((out, small, result, grad_tokens))
     mine = (mine.astype(F32) + out.astype(F32)).astype(BF16)
     by_z, by_x = swap_z(mine, NEAR), swap_x(mine, 1)
     by_both = lax.ppermute(mine, (XL, Z), [(i, i ^ 9) for i in range(16)])
-    grad_in_scale, grad_out_scale = finish(small, small_far, member_norm)
+    small_one = lax.ppermute(small, C, [(1, 0)])
+    grad_in_scale, grad_out_scale = finish(pos, small, small_one, member_norm)
     grad_weight = place(pos, (mine, by_z, by_x, by_both), total_norm)
     return result, grad_tokens, grad_weight, grad_in_scale, grad_out_scale
 

time: 105 us -> 104 us (level); the launches traced: 105 us -> 103 us
  waiting for transfers between devices: 38.3 us -> 34.8 us
  Pallas kernels: 20.2 us -> 22.6 us
  starting transfers between devices: 42.2 us -> 41 us
    ppermute x19 -> x20, waiting for transfers between devices: 27.9 us -> 23.7 us  [the longest x11 13.3 us: swap_y(): lax.ppermute(a, (Y, C), [(i * 2 + c, (i ^ flip) * 2 + c) for i in range(4...]
    ppermute x19 -> x20, starting transfers between devices: 29.5 us -> 25.8 us  [the longest x11 13.4 us: swap_y(): lax.ppermute(a, (Y, C), [(i * 2 + c, (i ^ flip) * 2 + c) for i in range(4...]
    ppermute x5, starting transfers between devices: 0.97 us -> 3.78 us  [swap_core(): return lax.ppermute(a, C, [(0, 1), (1, 0)])]
    ppermute x4, waiting for transfers between devices: 7.8 us -> 10.3 us  [swap_z(): return lax.ppermute(a, Z, list(enumerate(partners)))]
    ppermute x1, waiting for transfers between devices: 1.87 us -> 0.01 us  [on_device(): by_both = lax.ppermute(mine, (XL, Z), [(i, i ^ 9) for i in range(16)])]
    pallas_call x2 -> x4, Pallas kernels: 4.37 us -> 6.22 us  [the longest x2 5.97 us: partials(): pl.pallas_call(body, out_shape=out_shape, grid_spec=pltpu.PrefetchScalarG...]
  transfers between devices with their start and end apart: 29 -> 30, of which waited for: 19 -> 18; matrix products, arithmetic and copies ran while one was open for 1% -> 1% of each run, Pallas kernels for 17% -> 19%
where the time goes in v4:
time: 104 us; the launch traced here: 103 us
  starting transfers between devices  41 us (39%)
  waiting for transfers between devices  34.8 us (33%)
  Pallas kernels  22.6 us (22%)
  local copies, waits for them, and re-layouts  1.93 us (2%)
  other arithmetic  1.41 us (1%)
    ppermute x11, starting transfers between devices, swap_y(): lax.ppermute(a, (Y, C), [(i * 2 + c, (i ^ flip) * 2 + c) for i in range(4...  13.4 us
    ppermute x11, waiting for transfers between devices, swap_y(): lax.ppermute(a, (Y, C), [(i * 2 + c, (i ^ flip) * 2 + c) for i in range(4...  13.3 us
    ppermute x4, starting transfers between devices, swap_z(): return lax.ppermute(a, Z, list(enumerate(partners)))  11.3 us
    ppermute x8, starting transfers between devices, swap_x(): lax.ppermute(a, (XL, XH, C), [(i * 2 + c, j * 2 + c) for i, j in pairs fo...  11.2 us
    ppermute x4, waiting for transfers between devices, swap_z(): return lax.ppermute(a, Z, list(enumerate(partners)))  10.3 us
    pallas_call x3, Pallas kernels, layer(): pl.pallas_call(functools.partial(layer_body, order, first, last), out_sha...  10.2 us
    ppermute x8, waiting for transfers between devices, swap_x(): lax.ppermute(a, (XL, XH, C), [(i * 2 + c, j * 2 + c) for i, j in pairs fo...  8.69 us
    pallas_call x2, Pallas kernels, partials(): pl.pallas_call(body, out_shape=out_shape, grid_spec=pltpu.PrefetchScalarG...  5.97 us
  transfers between devices with their start and end apart: 30, of which 18 were waited for; matrix products, arithmetic and copies ran while one was open for 1% of the time, Pallas kernels for 19%

profile of v4, /device:TPU:2, one launch (start us, length us, event | category | flops | bytes accessed | tf_op | source)
XLA Modules:
  0.0 102.7 jit_solution(366195342301243915)
XLA Ops:
  6.8 2.2 %collective-permute-start.2 = (bf16[256,1024]{1,0:T(8,128)(2,1)S(1)}, bf16[256,1024]{1,0:T(8,128)(2,1)S(1)}, u32[]{:S(2)}, u32[]{:S(2)}) collective-permute-start(bf16[256,1024]{1,0:T(8,128)(2,1)S(1)} %copy-done.3), channel_id=1, source_target_pairs={{0,6},{1,7},{2,4},{3,5},{4,2},{5,3},{6,0},{7,1},{8,14},{9,15},{10,... | collective-permute-start | bytes 1572872 | tf_op jit(solution)/shard_map/ppermute | solution.py:28
  9.0 2.8 %shard_map.93 = (bf16[512,1024]{1,0:T(8,128)(2,1)S(1)}, bf16[4,128,640]{2,1,0:T(8,128)(2,1)S(1)}, bf16[4,128,768]{2,1,0:T(8,128)(2,1)S(1)}) custom-call(s32[4]{0:T(128)S(1)} %pad_add_fusion.pos, bf16[256,4096]{1,0:T(8,128)(2,1)S(1)} %copy-done, bf16[256,2048]{1,0:T(8,128)(2,1)S(1)} %collective-permute-done.3.tok_other, f32[1,4096]{1,0:T(1,128)S(1)} %copy-done.4, ...), custom_call_target="tpu_custom_call" | custom-call | flops 1073741824 | bytes 5242880 | tf_op jit(solution)/shard_map/pallas_call | solution.py:133
  11.8 1.9 %collective-permute-start.8 = (bf16[4,128,640]{2,1,0:T(8,128)(2,1)S(1)}, bf16[4,128,640]{2,1,0:T(8,128)(2,1)S(1)}, u32[]{:S(2)}, u32[]{:S(2)}) collective-permute-start(bf16[4,128,640]{2,1,0:T(8,128)(2,1)S(1)} %get-tuple-element.73), channel_id=1, source_target_pairs={{0,128},{1,129},{128,0},{129,1},{8,136},{9,137},{136,8},{137,9},{2... | collective-permute-start | bytes 1966088 | tf_op jit(solution)/shard_map/ppermute | solution.py:37
  13.7 3.2 %shard_map.94 = (bf16[4,128,1024]{2,1,0:T(8,128)(2,1)S(1)}, bf16[4,128,640]{2,1,0:T(8,128)(2,1)S(1)}, bf16[4,128,384]{2,1,0:T(8,128)(2,1)S(1)}, bf16[4,128,640]{2,1,0:T(8,128)(2,1)S(1)}) custom-call(s32[4]{0:T(128)S(1)} %pad_add_fusion.pos, bf16[256,4096]{1,0:T(8,128)(2,1)S(1)} %copy-done, bf16[256,2048]{1,0:T(8,128)(2,1)S(1)} %collective-permute-done.3.tok_other, ...), custom_call_target="tpu_custom_call" | custom-call | flops 1073741824 | bytes 5242880 | tf_op jit(solution)/shard_map/pallas_call | solution.py:133
  17.7 2.4 %collective-permute-done.refs_3_ = bf16[256,1024]{1,0:T(8,128)(2,1)S(1)} collective-permute-done((bf16[256,1024]{1,0:T(8,128)(2,1)S(1)}, bf16[256,1024]{1,0:T(8,128)(2,1)S(1)}, u32[]{:S(2)}, u32[]{:S(2)}) %collective-permute-start) | collective-permute-done | bytes 524320 | tf_op jit(solution)/shard_map/ppermute | solution.py:37
  21.7 2.3 %collective-permute-start.11 = (bf16[384,1024]{1,0:T(8,128)(2,1)S(1)}, bf16[384,1024]{1,0:T(8,128)(2,1)S(1)}, u32[]{:S(2)}, u32[]{:S(2)}) collective-permute-start(bf16[384,1024]{1,0:T(8,128)(2,1)S(1)} %get-tuple-element.131), channel_id=1, source_target_pairs={{0,6},{1,7},{2,4},{3,5},{4,2},{5,3},{6,0},{7,1},{8,14},{9,15},{10,... | collective-permute-start | bytes 2359304 | tf_op jit(solution)/shard_map/ppermute | solution.py:28
  24.0 1.8 %collective-permute-start.5 = (bf16[4,128,640]{2,1,0:T(8,128)(2,1)S(1)}, bf16[4,128,640]{2,1,0:T(8,128)(2,1)S(1)}, u32[]{:S(2)}, u32[]{:S(2)}) collective-permute-start(bf16[4,128,640]{2,1,0:T(8,128)(2,1)S(1)} %get-tuple-element.69), channel_id=1, source_target_pairs={{0,128},{1,129},{128,0},{129,1},{8,136},{9,137},{136,8},{137,9},{2... | collective-permute-start | bytes 1966088 | tf_op jit(solution)/shard_map/ppermute | solution.py:37
  25.8 4.5 %shard_map.97 = (bf16[256,4096]{1,0:T(8,128)(2,1)}, bf16[256,2048]{1,0:T(8,128)(2,1)S(1)}, f32[8,1024]{1,0:T(8,128)S(1)}, f32[512,1024]{1,0:T(8,128)S(1)}) custom-call(s32[4]{0:T(128)S(1)} %pad_add_fusion.pos, bf16[256,4096]{1,0:T(8,128)(2,1)S(1)} %copy-done, bf16[256,2048]{1,0:T(8,128)(2,1)S(1)} %collective-permute-done.3.tok_other, ...), custom_call_target="tpu_custom_call" | custom-call | flops 1 | bytes 1 | tf_op jit(solution)/shard_map/pallas_call | solution.py:321
  32.0 5.0 %collective-permute-done.6.passing.three = bf16[4,128,768]{2,1,0:T(8,128)(2,1)S(1)} collective-permute-done((bf16[4,128,768]{2,1,0:T(8,128)(2,1)S(1)}, bf16[4,128,768]{2,1,0:T(8,128)(2,1)S(1)}, u32[]{:S(2)}, u32[]{:S(2)}) %collective-permute-start.6) | collective-permute-done | bytes 786464 | tf_op jit(solution)/shard_map/ppermute | solution.py:37
  37.1 2.0 %collective-permute-start.7 = (bf16[4,128,384]{2,1,0:T(8,128)(2,1)S(1)}, bf16[4,128,384]{2,1,0:T(8,128)(2,1)S(1)}, u32[]{:S(2)}, u32[]{:S(2)}) collective-permute-start(bf16[4,128,384]{2,1,0:T(8,128)(2,1)S(1)} %shard_map.95), channel_id=1, source_target_pairs={{0,128},{1,129},{128,0},{129,1},{8,136},{9,137},{136,8},{137,9},{2... | collective-permute-start | bytes 1179656 | tf_op jit(solution)/shard_map/ppermute | solution.py:37
  39.1 2.1 %collective-permute-done.11 = bf16[384,1024]{1,0:T(8,128)(2,1)S(1)} collective-permute-done((bf16[384,1024]{1,0:T(8,128)(2,1)S(1)}, bf16[384,1024]{1,0:T(8,128)(2,1)S(1)}, u32[]{:S(2)}, u32[]{:S(2)}) %collective-permute-start.11) | collective-permute-done | bytes 786464 | tf_op jit(solution)/shard_map/ppermute | solution.py:28
  43.9 3.7 %shard_map.98 = (bf16[256,4096]{1,0:T(8,128)(2,1)}, bf16[256,2048]{1,0:T(8,128)(2,1)S(1)}, f32[8,1024]{1,0:T(8,128)S(1)}, f32[512,1024]{1,0:T(8,128)S(1)}) custom-call(s32[4]{0:T(128)S(1)} %pad_add_fusion.pos, bf16[256,4096]{1,0:T(8,128)(2,1)S(1)} %copy-done.1, ...), custom_call_target="tpu_custom_call", output_to_operand_aliasing={{0}: (12, {}), {1}: (13, {})} | custom-call | flops 1 | bytes 1 | tf_op jit(solution)/shard_map/pallas_call | solution.py:321
  50.8 2.5 %collective-permute-start.14 = (bf16[128,1024]{1,0:T(8,128)(2,1)S(1)}, bf16[128,1024]{1,0:T(8,128)(2,1)S(1)}, u32[]{:S(2)}, u32[]{:S(2)}) collective-permute-start(bf16[128,1024]{1,0:T(8,128)(2,1)S(1)} %get-tuple-element.98), channel_id=1, source_target_pairs={{0,4},{1,5},{2,6},{3,7},{4,0},{5,1},{6,2},{7,3},{8,12},{9,13},{10,... | collective-permute-start | bytes 786440 | tf_op jit(solution)/shard_map/ppermute | solution.py:28
  55.0 2.0 %shard_map.100 = (bf16[256,4096]{1,0:T(8,128)(2,1)}, bf16[256,2048]{1,0:T(8,128)(2,1)S(1)}, f32[8,1024]{1,0:T(8,128)S(1)}, f32[256,1024]{1,0:T(8,128)S(1)}, bf16[256,1024]{1,0:T(8,128)(2,1)S(1)}) custom-call(s32[4]{0:T(128)S(1)} %pad_add_fusion.pos, bf16[256,4096]{1,0:T(8,128)(2,1)S(1)} %copy-done.1, ...), custom_call_target="tpu_custom_call", output_to_operand_aliasing={{0}: (10, {}), {1}: (11, {})} | custom-call | flops 1 | bytes 1 | tf_op jit(solution)/shard_map/pallas_call | solution.py:321
  58.9 2.7 %collective-permute-done.14.r1 = bf16[128,1024]{1,0:T(8,128)(2,1)S(1)} collective-permute-done((bf16[128,1024]{1,0:T(8,128)(2,1)S(1)}, bf16[128,1024]{1,0:T(8,128)(2,1)S(1)}, u32[]{:S(2)}, u32[]{:S(2)}) %collective-permute-start.14) | collective-permute-done | bytes 262176 | tf_op jit(solution)/shard_map/ppermute | solution.py:28
  61.6 3.0 %collective-permute-done.15.r2 = bf16[128,1024]{1,0:T(8,128)(2,1)S(1)} collective-permute-done((bf16[128,1024]{1,0:T(8,128)(2,1)S(1)}, bf16[128,1024]{1,0:T(8,128)(2,1)S(1)}, u32[]{:S(2)}, u32[]{:S(2)}) %collective-permute-start.15) | collective-permute-done | bytes 262176 | tf_op jit(solution)/shard_map/ppermute | solution.py:28
  65.4 2.0 %collective-permute-start.19 = (bf16[64,1024]{1,0:T(8,128)(2,1)S(1)}, bf16[64,1024]{1,0:T(8,128)(2,1)S(1)}, u32[]{:S(2)}, u32[]{:S(2)}) collective-permute-start(bf16[64,1024]{1,0:T(8,128)(2,1)S(1)} %get-tuple-element.111), channel_id=1, source_target_pairs={{0,16},{16,0},{32,48},{48,32},{64,80},{80,64},{96,112},{112,96},{1... | collective-permute-start | bytes 393224 | tf_op jit(solution)/shard_map/ppermute | solution.py:41
  68.1 2.8 %collective-permute-start.24 = (bf16[256,1024]{1,0:T(8,128)(2,1)S(1)}, bf16[256,1024]{1,0:T(8,128)(2,1)S(1)}, u32[]{:S(2)}, u32[]{:S(2)}) collective-permute-start(bf16[256,1024]{1,0:T(8,128)(2,1)S(1)} %get-tuple-element.118), channel_id=1, source_target_pairs={{0,1},{1,0},{2,3},{3,2},{4,5},{5,4},{6,7},{7,6},{8,9},{9,8},{10,11... | collective-permute-start | bytes 1572872 | tf_op jit(solution)/shard_map/ppermute | solution.py:21
  70.9 5.5 %collective-permute-start.21 = (bf16[64,1024]{1,0:T(8,128)(2,1)S(1)}, bf16[64,1024]{1,0:T(8,128)(2,1)S(1)}, u32[]{:S(2)}, u32[]{:S(2)}) collective-permute-start(bf16[64,1024]{1,0:T(8,128)(2,1)S(1)} %add_convert_fusion.2), channel_id=1, source_target_pairs={{0,112},{16,32},{32,16},{48,64},{64,48},{80,96},{96,80},{112,0},{1... | collective-permute-start | bytes 393224 | tf_op jit(solution)/shard_map/ppermute | solution.py:41
  77.1 3.5 %collective-permute-done.21 = bf16[64,1024]{1,0:T(8,128)(2,1)S(1)} collective-permute-done((bf16[64,1024]{1,0:T(8,128)(2,1)S(1)}, bf16[64,1024]{1,0:T(8,128)(2,1)S(1)}, u32[]{:S(2)}, u32[]{:S(2)}) %collective-permute-start.21) | collective-permute-done | bytes 131104 | tf_op jit(solution)/shard_map/ppermute | solution.py:41
  80.6 2.2 %collective-permute-start.23 = (bf16[64,1024]{1,0:T(8,128)(2,1)S(1)}, bf16[64,1024]{1,0:T(8,128)(2,1)S(1)}, u32[]{:S(2)}, u32[]{:S(2)}) collective-permute-start(bf16[64,1024]{1,0:T(8,128)(2,1)S(1)} %add_convert_fusion.1), channel_id=1, source_target_pairs={{0,48},{16,96},{32,80},{48,0},{64,112},{80,32},{96,16},{112,64},{1... | collective-permute-start | bytes 393224 | tf_op jit(solution)/shard_map/ppermute | solution.py:41
  85.4 5.7 %collective-permute-done.23 = bf16[64,1024]{1,0:T(8,128)(2,1)S(1)} collective-permute-done((bf16[64,1024]{1,0:T(8,128)(2,1)S(1)}, bf16[64,1024]{1,0:T(8,128)(2,1)S(1)}, u32[]{:S(2)}, u32[]{:S(2)}) %collective-permute-start.23) | collective-permute-done | bytes 131104 | tf_op jit(solution)/shard_map/ppermute | solution.py:41
  91.2 1.8 %collective-permute-start.27 = (bf16[64,1024]{1,0:T(8,128)(2,1)S(1)}, bf16[64,1024]{1,0:T(8,128)(2,1)S(1)}, u32[]{:S(2)}, u32[]{:S(2)}) collective-permute-start(bf16[64,1024]{1,0:T(8,128)(2,1)S(1)} %add_convert_fusion.own), channel_id=1, source_target_pairs={{0,128},{1,129},{128,0},{129,1},{8,136},{9,137},{136,8},{137,9},{2... | collective-permute-start | bytes 393224 | tf_op jit(solution)/shard_map/ppermute | solution.py:37
  96.0 1.8 %collective-permute-done.29.other = f32[8,1024]{1,0:T(8,128)S(1)} collective-permute-done((f32[8,1024]{1,0:T(8,128)S(1)}, f32[8,1024]{1,0:T(8,128)S(1)}, u32[]{:S(2)}, u32[]{:S(2)}) %collective-permute-start.29) | collective-permute-done | bytes 32800 | tf_op jit(solution)/shard_map/ppermute | solution.py:444
  (79 shorter events, 32.4 us)
Async XLA Ops:
  3.2 5.9 %collective-permute-start.3 = (bf16[256,2048]{1,0:T(8,128)(2,1)S(1)}, bf16[256,2048]{1,0:T(8,128)(2,1)S(1)}, u32[]{:S(2)}, u32[]{:S(2)}) collective-permute-start(bf16[256,2048]{1,0:T(8,128)(2,1)S(1)} %shard_map.92), channel_id=1, source_target_pairs={{0,1},{1,0},{2,3},{3,2},{4,5},{5,4},{6,7},{7,6},{8,9},{9,8},{10,11... | collective-permute-start | bytes 3145736 | tf_op jit(solution)/shard_map/ppermute | solution.py:21
  3.4 5.6 %collective-permute-start.4 = (bf16[256,1024]{1,0:T(8,128)(2,1)S(1)}, bf16[256,1024]{1,0:T(8,128)(2,1)S(1)}, u32[]{:S(2)}, u32[]{:S(2)}) collective-permute-start(bf16[256,1024]{1,0:T(8,128)(2,1)S(1)} %copy-done.2), channel_id=1, source_target_pairs={{0,1},{1,0},{2,3},{3,2},{4,5},{5,4},{6,7},{7,6},{8,9},{9,8},{10,11... | collective-permute-start | bytes 1572872 | tf_op jit(solution)/shard_map/ppermute | solution.py:21
  3.8 14.0 %collective-permute-start.1 = (bf16[256,1024]{1,0:T(8,128)(2,1)S(1)}, bf16[256,1024]{1,0:T(8,128)(2,1)S(1)}, u32[]{:S(2)}, u32[]{:S(2)}) collective-permute-start(bf16[256,1024]{1,0:T(8,128)(2,1)S(1)} %copy-done.3), channel_id=1, source_target_pairs={{0,2},{1,3},{2,0},{3,1},{4,6},{5,7},{6,4},{7,5},{8,10},{9,11},{10,... | collective-permute-start | bytes 1572872 | tf_op jit(solution)/shard_map/ppermute | solution.py:28
  5.3 14.8 %collective-permute-start = (bf16[256,1024]{1,0:T(8,128)(2,1)S(1)}, bf16[256,1024]{1,0:T(8,128)(2,1)S(1)}, u32[]{:S(2)}, u32[]{:S(2)}) collective-permute-start(bf16[256,1024]{1,0:T(8,128)(2,1)S(1)} %copy-done.3), channel_id=1, source_target_pairs={{0,136},{1,137},{128,8},{129,9},{8,128},{9,129},{136,0},{137,1},{2... | collective-permute-start | bytes 1572872 | tf_op jit(solution)/shard_map/ppermute | solution.py:37
  6.8 14.6 %collective-permute-start.2 = (bf16[256,1024]{1,0:T(8,128)(2,1)S(1)}, bf16[256,1024]{1,0:T(8,128)(2,1)S(1)}, u32[]{:S(2)}, u32[]{:S(2)}) collective-permute-start(bf16[256,1024]{1,0:T(8,128)(2,1)S(1)} %copy-done.3), channel_id=1, source_target_pairs={{0,6},{1,7},{2,4},{3,5},{4,2},{5,3},{6,0},{7,1},{8,14},{9,15},{10,... | collective-permute-start | bytes 1572872 | tf_op jit(solution)/shard_map/ppermute | solution.py:28
  11.8 18.5 %collective-permute-start.8 = (bf16[4,128,640]{2,1,0:T(8,128)(2,1)S(1)}, bf16[4,128,640]{2,1,0:T(8,128)(2,1)S(1)}, u32[]{:S(2)}, u32[]{:S(2)}) collective-permute-start(bf16[4,128,640]{2,1,0:T(8,128)(2,1)S(1)} %get-tuple-element.73), channel_id=1, source_target_pairs={{0,128},{1,129},{128,0},{129,1},{8,136},{9,137},{136,8},{137,9},{2... | collective-permute-start | bytes 1966088 | tf_op jit(solution)/shard_map/ppermute | solution.py:37
  13.7 23.3 %collective-permute-start.6 = (bf16[4,128,768]{2,1,0:T(8,128)(2,1)S(1)}, bf16[4,128,768]{2,1,0:T(8,128)(2,1)S(1)}, u32[]{:S(2)}, u32[]{:S(2)}) collective-permute-start(bf16[4,128,768]{2,1,0:T(8,128)(2,1)S(1)} %get-tuple-element.70), channel_id=1, source_target_pairs={{0,136},{1,137},{128,8},{129,9},{8,128},{9,129},{136,0},{137,1},{2... | collective-permute-start | bytes 2359304 | tf_op jit(solution)/shard_map/ppermute | solution.py:37
  21.7 19.4 %collective-permute-start.11 = (bf16[384,1024]{1,0:T(8,128)(2,1)S(1)}, bf16[384,1024]{1,0:T(8,128)(2,1)S(1)}, u32[]{:S(2)}, u32[]{:S(2)}) collective-permute-start(bf16[384,1024]{1,0:T(8,128)(2,1)S(1)} %get-tuple-element.131), channel_id=1, source_target_pairs={{0,6},{1,7},{2,4},{3,5},{4,2},{5,3},{6,0},{7,1},{8,14},{9,15},{10,... | collective-permute-start | bytes 2359304 | tf_op jit(solution)/shard_map/ppermute | solution.py:28
  24.0 17.8 %collective-permute-start.10 = (bf16[384,1024]{1,0:T(8,128)(2,1)S(1)}, bf16[384,1024]{1,0:T(8,128)(2,1)S(1)}, u32[]{:S(2)}, u32[]{:S(2)}) collective-permute-start(bf16[384,1024]{1,0:T(8,128)(2,1)S(1)} %get-tuple-element.132), channel_id=1, source_target_pairs={{0,2},{1,3},{2,0},{3,1},{4,6},{5,7},{6,4},{7,5},{8,10},{9,11},{10,... | collective-permute-start | bytes 2359304 | tf_op jit(solution)/shard_map/ppermute | solution.py:28
  24.0 26.2 %collective-permute-start.5 = (bf16[4,128,640]{2,1,0:T(8,128)(2,1)S(1)}, bf16[4,128,640]{2,1,0:T(8,128)(2,1)S(1)}, u32[]{:S(2)}, u32[]{:S(2)}) collective-permute-start(bf16[4,128,640]{2,1,0:T(8,128)(2,1)S(1)} %get-tuple-element.69), channel_id=1, source_target_pairs={{0,128},{1,129},{128,0},{129,1},{8,136},{9,137},{136,8},{137,9},{2... | collective-permute-start | bytes 1966088 | tf_op jit(solution)/shard_map/ppermute | solution.py:37
  30.4 20.0 %collective-permute-start.9 = (bf16[4,128,640]{2,1,0:T(8,128)(2,1)S(1)}, bf16[4,128,640]{2,1,0:T(8,128)(2,1)S(1)}, u32[]{:S(2)}, u32[]{:S(2)}) collective-permute-start(bf16[4,128,640]{2,1,0:T(8,128)(2,1)S(1)} %shard_map.96), channel_id=1, source_target_pairs={{0,136},{1,137},{128,8},{129,9},{8,128},{9,129},{136,0},{137,1},{2... | collective-permute-start | bytes 1966088 | tf_op jit(solution)/shard_map/ppermute | solution.py:37
  37.1 13.3 %collective-permute-start.7 = (bf16[4,128,384]{2,1,0:T(8,128)(2,1)S(1)}, bf16[4,128,384]{2,1,0:T(8,128)(2,1)S(1)}, u32[]{:S(2)}, u32[]{:S(2)}) collective-permute-start(bf16[4,128,384]{2,1,0:T(8,128)(2,1)S(1)} %shard_map.95), channel_id=1, source_target_pairs={{0,128},{1,129},{128,0},{129,1},{8,136},{9,137},{136,8},{137,9},{2... | collective-permute-start | bytes 1179656 | tf_op jit(solution)/shard_map/ppermute | solution.py:37
  41.9 6.6 %collective-permute-start.12 = (bf16[128,1024]{1,0:T(8,128)(2,1)S(1)}, bf16[128,1024]{1,0:T(8,128)(2,1)S(1)}, u32[]{:S(2)}, u32[]{:S(2)}) collective-permute-start(bf16[128,1024]{1,0:T(8,128)(2,1)S(1)} %get-tuple-element.130), channel_id=1, source_target_pairs={{0,2},{1,3},{2,0},{3,1},{4,6},{5,7},{6,4},{7,5},{8,10},{9,11},{10,... | collective-permute-start | bytes 786440 | tf_op jit(solution)/shard_map/ppermute | solution.py:28
  42.5 7.7 %collective-permute-start.13 = (bf16[128,1024]{1,0:T(8,128)(2,1)S(1)}, bf16[128,1024]{1,0:T(8,128)(2,1)S(1)}, u32[]{:S(2)}, u32[]{:S(2)}) collective-permute-start(bf16[128,1024]{1,0:T(8,128)(2,1)S(1)} %get-tuple-element.128), channel_id=1, source_target_pairs={{0,6},{1,7},{2,4},{3,5},{4,2},{5,3},{6,0},{7,1},{8,14},{9,15},{10,... | collective-permute-start | bytes 786440 | tf_op jit(solution)/shard_map/ppermute | solution.py:28
  50.8 10.8 %collective-permute-start.14 = (bf16[128,1024]{1,0:T(8,128)(2,1)S(1)}, bf16[128,1024]{1,0:T(8,128)(2,1)S(1)}, u32[]{:S(2)}, u32[]{:S(2)}) collective-permute-start(bf16[128,1024]{1,0:T(8,128)(2,1)S(1)} %get-tuple-element.98), channel_id=1, source_target_pairs={{0,4},{1,5},{2,6},{3,7},{4,0},{5,1},{6,2},{7,3},{8,12},{9,13},{10,... | collective-permute-start | bytes 786440 | tf_op jit(solution)/shard_map/ppermute | solution.py:28
  53.3 11.3 %collective-permute-start.15 = (bf16[128,1024]{1,0:T(8,128)(2,1)S(1)}, bf16[128,1024]{1,0:T(8,128)(2,1)S(1)}, u32[]{:S(2)}, u32[]{:S(2)}) collective-permute-start(bf16[128,1024]{1,0:T(8,128)(2,1)S(1)} %get-tuple-element.99), channel_id=1, source_target_pairs={{0,2},{1,3},{2,0},{3,1},{4,6},{5,7},{6,4},{7,5},{8,10},{9,11},{10,... | collective-permute-start | bytes 786440 | tf_op jit(solution)/shard_map/ppermute | solution.py:28
  53.4 11.3 %collective-permute-start.16 = (bf16[128,1024]{1,0:T(8,128)(2,1)S(1)}, bf16[128,1024]{1,0:T(8,128)(2,1)S(1)}, u32[]{:S(2)}, u32[]{:S(2)}) collective-permute-start(bf16[128,1024]{1,0:T(8,128)(2,1)S(1)} %get-tuple-element.100), channel_id=1, source_target_pairs={{0,6},{1,7},{2,4},{3,5},{4,2},{5,3},{6,0},{7,1},{8,14},{9,15},{10,... | collective-permute-start | bytes 786440 | tf_op jit(solution)/shard_map/ppermute | solution.py:28
  57.0 26.8 %collective-permute-start.25 = (bf16[256,2048]{1,0:T(8,128)(2,1)S(1)}, bf16[256,2048]{1,0:T(8,128)(2,1)S(1)}, u32[]{:S(2)}, u32[]{:S(2)}) collective-permute-start(bf16[256,2048]{1,0:T(8,128)(2,1)S(1)} %get-tuple-element.119), channel_id=1, source_target_pairs={{0,1},{1,0},{2,3},{3,2},{4,5},{5,4},{6,7},{7,6},{8,9},{9,8},{10,11... | collective-permute-start | bytes 3145736 | tf_op jit(solution)/shard_map/ppermute | solution.py:21
  68.1 14.7 %collective-permute-start.24 = (bf16[256,1024]{1,0:T(8,128)(2,1)S(1)}, bf16[256,1024]{1,0:T(8,128)(2,1)S(1)}, u32[]{:S(2)}, u32[]{:S(2)}) collective-permute-start(bf16[256,1024]{1,0:T(8,128)(2,1)S(1)} %get-tuple-element.118), channel_id=1, source_target_pairs={{0,1},{1,0},{2,3},{3,2},{4,5},{5,4},{6,7},{7,6},{8,9},{9,8},{10,11... | collective-permute-start | bytes 1572872 | tf_op jit(solution)/shard_map/ppermute | solution.py:21
  70.9 9.6 %collective-permute-start.21 = (bf16[64,1024]{1,0:T(8,128)(2,1)S(1)}, bf16[64,1024]{1,0:T(8,128)(2,1)S(1)}, u32[]{:S(2)}, u32[]{:S(2)}) collective-permute-start(bf16[64,1024]{1,0:T(8,128)(2,1)S(1)} %add_convert_fusion.2), channel_id=1, source_target_pairs={{0,112},{16,32},{32,16},{48,64},{64,48},{80,96},{96,80},{112,0},{1... | collective-permute-start | bytes 393224 | tf_op jit(solution)/shard_map/ppermute | solution.py:41
  80.6 10.5 %collective-permute-start.23 = (bf16[64,1024]{1,0:T(8,128)(2,1)S(1)}, bf16[64,1024]{1,0:T(8,128)(2,1)S(1)}, u32[]{:S(2)}, u32[]{:S(2)}) collective-permute-start(bf16[64,1024]{1,0:T(8,128)(2,1)S(1)} %add_convert_fusion.1), channel_id=1, source_target_pairs={{0,48},{16,96},{32,80},{48,0},{64,112},{80,32},{96,16},{112,64},{1... | collective-permute-start | bytes 393224 | tf_op jit(solution)/shard_map/ppermute | solution.py:41
  91.1 7.8 %collective-permute-start.28 = (bf16[64,1024]{1,0:T(8,128)(2,1)S(1)}, bf16[64,1024]{1,0:T(8,128)(2,1)S(1)}, u32[]{:S(2)}, u32[]{:S(2)}) collective-permute-start(bf16[64,1024]{1,0:T(8,128)(2,1)S(1)} %add_convert_fusion.own), channel_id=1, source_target_pairs={{0,144},{16,128},{32,176},{48,160},{64,208},{80,192},{96,240},{112... | collective-permute-start | bytes 393224 | tf_op jit(solution)/shard_map/ppermute | solution.py:443
  91.2 8.7 %collective-permute-start.27 = (bf16[64,1024]{1,0:T(8,128)(2,1)S(1)}, bf16[64,1024]{1,0:T(8,128)(2,1)S(1)}, u32[]{:S(2)}, u32[]{:S(2)}) collective-permute-start(bf16[64,1024]{1,0:T(8,128)(2,1)S(1)} %add_convert_fusion.own), channel_id=1, source_target_pairs={{0,128},{1,129},{128,0},{129,1},{8,136},{9,137},{136,8},{137,9},{2... | collective-permute-start | bytes 393224 | tf_op jit(solution)/shard_map/ppermute | solution.py:37
  93.0 8.0 %collective-permute-start.26 = (bf16[64,1024]{1,0:T(8,128)(2,1)S(1)}, bf16[64,1024]{1,0:T(8,128)(2,1)S(1)}, u32[]{:S(2)}, u32[]{:S(2)}) collective-permute-start(bf16[64,1024]{1,0:T(8,128)(2,1)S(1)} %add_convert_fusion.own), channel_id=1, source_target_pairs={{0,16},{16,0},{32,48},{48,32},{64,80},{80,64},{96,112},{112,96},{1... | collective-permute-start | bytes 393224 | tf_op jit(solution)/shard_map/ppermute | solution.py:41
  (12 other events, 37.4 us)

commit v5 on v4

--- a/solution.py
+++ b/solution.py
@@ -21,20 +21,16 @@
     return lax.ppermute(a, C, [(0, 1), (1, 0)])
 
 
-BOTH, ONE = (0, 1), (1,)
-
-
-def swap_y(a, flip, cores=BOTH):
-    return lax.ppermute(a, (Y, C), [(i * 2 + c, (i ^ flip) * 2 + c) for i in range(4) for c in cores])
+def swap_y(a, flip):
+    return lax.ppermute(a, Y, [(i, i ^ flip) for i in range(4)])
 
 
 def x_index(place):
     return (place % 2) * 2 + place // 2
 
 
-def swap_x(a, flip, cores=BOTH):
-    pairs = [(x_index(i), x_index(i ^ flip)) for i in range(4)]
-    return lax.ppermute(a, (XL, XH, C), [(i * 2 + c, j * 2 + c) for i, j in pairs for c in cores])
+def swap_x(a, flip):
+    return lax.ppermute(a, (XL, XH), [(x_index(i), x_index(i ^ flip)) for i in range(4)])
 
 
 def swap_z(a, partners):
@@ -359,22 +355,22 @@
     )(pos, others, own)
 
 
-def finish_body(scale, pos, mine, other, in_ref, out_ref):
-    total = jnp.where(pos[2] == 1, mine[...], other[...]) * scale
+def finish_body(scale, small, in_ref, out_ref):
+    total = small[...] * scale
     for k in range(4):
         in_ref[:, k * WIDTH : (k + 1) * WIDTH] = total[k : k + 1]
     out_ref[...] = total[4:5]
 
 
-def finish(pos, mine, other, scale):
+def finish(small, scale):
     return pl.pallas_call(
         functools.partial(finish_body, scale),
         out_shape=[jax.ShapeDtypeStruct((1, DEPTH), F32), jax.ShapeDtypeStruct((1, WIDTH), F32)],
-        in_specs=[SCALARS] + [VMEM] * 2,
+        in_specs=[VMEM],
         out_specs=[VMEM] * 2,
         compiler_params=PARAMS,
         cost_estimate=cost(2**14, 2**16),
-    )(pos, mine, other)
+    )(small)
 
 
 def on_device(tokens, cotangent, slow_weight, in_scale, out_scale):
@@ -421,30 +417,28 @@
     two = swap_y(out[1], 2)
     arrived = [two, swap_y(out[0], 1), swap_y(out[2], 3)]
     small = small + swap_core(small)
-    small = small + swap_y(small, 1, ONE)
+    small = small + swap_y(small, 1)
     arrived, small = lax.optimization_barrier((arrived, small))
 
     keep, out = join(pos, stay, arrived)
     out = swap_z(out, NEAR)
-    small = small + swap_y(small, 3, ONE)
+    small = small + swap_y(small, 3)
     out, small = lax.optimization_barrier((out, small))
     mine = (keep + out.astype(F32)).astype(BF16)
     out = swap_z(mine, NEXT)
-    small = small + swap_x(small, 2, ONE)
-    out, small = lax.optimization_barrier((out, small))
+    small = small + swap_x(small, 2)
     pre_other, others = swap_core(pre_other), swap_core(others)
     mine = (mine.astype(F32) + out.astype(F32)).astype(BF16)
     out = swap_z(mine, FAR)
     result = ((pre_own + pre_other.astype(F32)) * out_scale).astype(BF16)
     grad_tokens = fill(pos, sum(orders, ()), others, own)
-    out, small, result, grad_tokens = lax.optimization_barrier((out, small, result, grad_tokens))
+    scale_grads = finish(small, member_norm)
+    out, scale_grads, result, grad_tokens = lax.optimization_barrier((out, scale_grads, result, grad_tokens))
     mine = (mine.astype(F32) + out.astype(F32)).astype(BF16)
     by_z, by_x = swap_z(mine, NEAR), swap_x(mine, 1)
     by_both = lax.ppermute(mine, (XL, Z), [(i, i ^ 9) for i in range(16)])
-    small_one = lax.ppermute(small, C, [(1, 0)])
-    grad_in_scale, grad_out_scale = finish(pos, small, small_one, member_norm)
     grad_weight = place(pos, (mine, by_z, by_x, by_both), total_norm)
-    return result, grad_tokens, grad_weight, grad_in_scale, grad_out_scale
+    return result, grad_tokens, grad_weight, *scale_grads
 
 
 def solution(mesh):

time: 104 us -> 102 us (0.981)
    ppermute x4, waiting for transfers between devices: 10.3 us -> 4.5 us  [swap_z(): return lax.ppermute(a, Z, list(enumerate(partners)))]
    ppermute x20 -> x19, waiting for transfers between devices: 23.7 us -> 27.1 us  [the longest x11 16.8 us: swap_y(): return lax.ppermute(a, Y, [(i, i ^ flip) for i in range(4)])]
    ppermute x20 -> x19, starting transfers between devices: 25.8 us -> 28.8 us  [the longest x11 14.6 us: swap_y(): return lax.ppermute(a, Y, [(i, i ^ flip) for i in range(4)])]
    ppermute x5, starting transfers between devices: 3.78 us -> 0.97 us  [swap_core(): return lax.ppermute(a, C, [(0, 1), (1, 0)])]
    ppermute x1, waiting for transfers between devices: 0.01 us -> 2.44 us  [on_device(): by_both = lax.ppermute(mine, (XL, Z), [(i, i ^ 9) for i in range(16)])]
  transfers between devices with their start and end apart: 30 -> 29, of which waited for: 18 -> 17; matrix products, arithmetic and copies ran while one was open for 1% -> 1% of each run, Pallas kernels for 19% -> 19%
where the time goes in v5:
time: 102 us; the launch traced here: 101 us
  starting transfers between devices  40.3 us (40%)
  waiting for transfers between devices  34.7 us (34%)
  Pallas kernels  22 us (22%)
  local copies, waits for them, and re-layouts  1.93 us (2%)
  other arithmetic  1.41 us (1%)
    ppermute x11, waiting for transfers between devices, swap_y(): return lax.ppermute(a, Y, [(i, i ^ flip) for i in range(4)])  16.8 us
    ppermute x11, starting transfers between devices, swap_y(): return lax.ppermute(a, Y, [(i, i ^ flip) for i in range(4)])  14.6 us
    ppermute x8, starting transfers between devices, swap_x(): lax.ppermute(a, (XL, XH), [(x_index(i), x_index(i ^ flip)) for i in range...  14.2 us
    ppermute x4, starting transfers between devices, swap_z(): return lax.ppermute(a, Z, list(enumerate(partners)))  10.4 us
    ppermute x8, waiting for transfers between devices, swap_x(): lax.ppermute(a, (XL, XH), [(x_index(i), x_index(i ^ flip)) for i in range...  10.3 us
    pallas_call x3, Pallas kernels, layer(): pl.pallas_call(functools.partial(layer_body, order, first, last), out_sha...  10.2 us
    pallas_call x2, Pallas kernels, partials(): pl.pallas_call(body, out_shape=out_shape, grid_spec=pltpu.PrefetchScalarG...  5.96 us
    ppermute x4, waiting for transfers between devices, swap_z(): return lax.ppermute(a, Z, list(enumerate(partners)))  4.5 us
  transfers between devices with their start and end apart: 29, of which 17 were waited for; matrix products, arithmetic and copies ran while one was open for 1% of the time, Pallas kernels for 19%

profile of v5, /device:TPU:2, one launch (start us, length us, event | category | flops | bytes accessed | tf_op | source)
XLA Modules:
  0.0 101.3 jit_solution(5496113061211292435)
XLA Ops:
  6.8 2.2 %collective-permute-start.2 = (bf16[256,1024]{1,0:T(8,128)(2,1)S(1)}, bf16[256,1024]{1,0:T(8,128)(2,1)S(1)}, u32[]{:S(2)}, u32[]{:S(2)}) collective-permute-start(bf16[256,1024]{1,0:T(8,128)(2,1)S(1)} %copy-done.3), channel_id=1, source_target_pairs={{0,6},{2,4},{4,2},{6,0},{1,7},{3,5},{5,3},{7,1},{8,14},{10,12},{12... | collective-permute-start | bytes 1572872 | tf_op jit(solution)/shard_map/ppermute | solution.py:25
  9.0 2.8 %shard_map.93 = (bf16[512,1024]{1,0:T(8,128)(2,1)S(1)}, bf16[4,128,640]{2,1,0:T(8,128)(2,1)S(1)}, bf16[4,128,768]{2,1,0:T(8,128)(2,1)S(1)}) custom-call(s32[4]{0:T(128)S(1)} %pad_add_fusion.pos, bf16[256,4096]{1,0:T(8,128)(2,1)S(1)} %copy-done, bf16[256,2048]{1,0:T(8,128)(2,1)S(1)} %collective-permute-done.3.tok_other, f32[1,4096]{1,0:T(1,128)S(1)} %copy-done.4, ...), custom_call_target="tpu_custom_call" | custom-call | flops 1073741824 | bytes 5242880 | tf_op jit(solution)/shard_map/pallas_call | solution.py:129
  11.8 1.9 %collective-permute-start.8 = (bf16[4,128,640]{2,1,0:T(8,128)(2,1)S(1)}, bf16[4,128,640]{2,1,0:T(8,128)(2,1)S(1)}, u32[]{:S(2)}, u32[]{:S(2)}) collective-permute-start(bf16[4,128,640]{2,1,0:T(8,128)(2,1)S(1)} %get-tuple-element.72), channel_id=1, source_target_pairs={{0,128},{128,0},{8,136},{136,8},{1,129},{129,1},{9,137},{137,9},{2... | collective-permute-start | bytes 1966088 | tf_op jit(solution)/shard_map/ppermute | solution.py:33
  13.7 3.2 %shard_map.94 = (bf16[4,128,1024]{2,1,0:T(8,128)(2,1)S(1)}, bf16[4,128,640]{2,1,0:T(8,128)(2,1)S(1)}, bf16[4,128,384]{2,1,0:T(8,128)(2,1)S(1)}, bf16[4,128,640]{2,1,0:T(8,128)(2,1)S(1)}) custom-call(s32[4]{0:T(128)S(1)} %pad_add_fusion.pos, bf16[256,4096]{1,0:T(8,128)(2,1)S(1)} %copy-done, bf16[256,2048]{1,0:T(8,128)(2,1)S(1)} %collective-permute-done.3.tok_other, ...), custom_call_target="tpu_custom_call" | custom-call | flops 1073741824 | bytes 5242880 | tf_op jit(solution)/shard_map/pallas_call | solution.py:129
  17.7 2.4 %collective-permute-done.refs_3_ = bf16[256,1024]{1,0:T(8,128)(2,1)S(1)} collective-permute-done((bf16[256,1024]{1,0:T(8,128)(2,1)S(1)}, bf16[256,1024]{1,0:T(8,128)(2,1)S(1)}, u32[]{:S(2)}, u32[]{:S(2)}) %collective-permute-start) | collective-permute-done | bytes 524320 | tf_op jit(solution)/shard_map/ppermute | solution.py:33
  21.7 2.3 %collective-permute-start.11 = (bf16[384,1024]{1,0:T(8,128)(2,1)S(1)}, bf16[384,1024]{1,0:T(8,128)(2,1)S(1)}, u32[]{:S(2)}, u32[]{:S(2)}) collective-permute-start(bf16[384,1024]{1,0:T(8,128)(2,1)S(1)} %get-tuple-element.129), channel_id=1, source_target_pairs={{0,6},{2,4},{4,2},{6,0},{1,7},{3,5},{5,3},{7,1},{8,14},{10,12},{12... | collective-permute-start | bytes 2359304 | tf_op jit(solution)/shard_map/ppermute | solution.py:25
  25.8 4.5 %shard_map.97 = (bf16[256,4096]{1,0:T(8,128)(2,1)}, bf16[256,2048]{1,0:T(8,128)(2,1)S(1)}, f32[8,1024]{1,0:T(8,128)S(1)}, f32[512,1024]{1,0:T(8,128)S(1)}) custom-call(s32[4]{0:T(128)S(1)} %pad_add_fusion.pos, bf16[256,4096]{1,0:T(8,128)(2,1)S(1)} %copy-done, bf16[256,2048]{1,0:T(8,128)(2,1)S(1)} %collective-permute-done.3.tok_other, ...), custom_call_target="tpu_custom_call" | custom-call | flops 1 | bytes 1 | tf_op jit(solution)/shard_map/pallas_call | solution.py:317
  32.0 5.0 %collective-permute-done.6.passing.three = bf16[4,128,768]{2,1,0:T(8,128)(2,1)S(1)} collective-permute-done((bf16[4,128,768]{2,1,0:T(8,128)(2,1)S(1)}, bf16[4,128,768]{2,1,0:T(8,128)(2,1)S(1)}, u32[]{:S(2)}, u32[]{:S(2)}) %collective-permute-start.6) | collective-permute-done | bytes 786464 | tf_op jit(solution)/shard_map/ppermute | solution.py:33
  37.1 2.0 %collective-permute-start.7 = (bf16[4,128,384]{2,1,0:T(8,128)(2,1)S(1)}, bf16[4,128,384]{2,1,0:T(8,128)(2,1)S(1)}, u32[]{:S(2)}, u32[]{:S(2)}) collective-permute-start(bf16[4,128,384]{2,1,0:T(8,128)(2,1)S(1)} %shard_map.95), channel_id=1, source_target_pairs={{0,128},{128,0},{8,136},{136,8},{1,129},{129,1},{9,137},{137,9},{2... | collective-permute-start | bytes 1179656 | tf_op jit(solution)/shard_map/ppermute | solution.py:33
  39.1 2.1 %collective-permute-done.11 = bf16[384,1024]{1,0:T(8,128)(2,1)S(1)} collective-permute-done((bf16[384,1024]{1,0:T(8,128)(2,1)S(1)}, bf16[384,1024]{1,0:T(8,128)(2,1)S(1)}, u32[]{:S(2)}, u32[]{:S(2)}) %collective-permute-start.11) | collective-permute-done | bytes 786464 | tf_op jit(solution)/shard_map/ppermute | solution.py:25
  43.9 3.7 %shard_map.98 = (bf16[256,4096]{1,0:T(8,128)(2,1)}, bf16[256,2048]{1,0:T(8,128)(2,1)S(1)}, f32[8,1024]{1,0:T(8,128)S(1)}, f32[512,1024]{1,0:T(8,128)S(1)}) custom-call(s32[4]{0:T(128)S(1)} %pad_add_fusion.pos, bf16[256,4096]{1,0:T(8,128)(2,1)S(1)} %copy-done.1, ...), custom_call_target="tpu_custom_call", output_to_operand_aliasing={{0}: (12, {}), {1}: (13, {})} | custom-call | flops 1 | bytes 1 | tf_op jit(solution)/shard_map/pallas_call | solution.py:317
  50.8 2.5 %collective-permute-start.14 = (bf16[128,1024]{1,0:T(8,128)(2,1)S(1)}, bf16[128,1024]{1,0:T(8,128)(2,1)S(1)}, u32[]{:S(2)}, u32[]{:S(2)}) collective-permute-start(bf16[128,1024]{1,0:T(8,128)(2,1)S(1)} %get-tuple-element.97), channel_id=1, source_target_pairs={{0,4},{2,6},{4,0},{6,2},{1,5},{3,7},{5,1},{7,3},{8,12},{10,14},{12... | collective-permute-start | bytes 786440 | tf_op jit(solution)/shard_map/ppermute | solution.py:25
  55.0 2.0 %shard_map.100 = (bf16[256,4096]{1,0:T(8,128)(2,1)}, bf16[256,2048]{1,0:T(8,128)(2,1)S(1)}, f32[8,1024]{1,0:T(8,128)S(1)}, f32[256,1024]{1,0:T(8,128)S(1)}, bf16[256,1024]{1,0:T(8,128)(2,1)S(1)}) custom-call(s32[4]{0:T(128)S(1)} %pad_add_fusion.pos, bf16[256,4096]{1,0:T(8,128)(2,1)S(1)} %copy-done.1, ...), custom_call_target="tpu_custom_call", output_to_operand_aliasing={{0}: (10, {}), {1}: (11, {})} | custom-call | flops 1 | bytes 1 | tf_op jit(solution)/shard_map/pallas_call | solution.py:317
  58.9 6.1 %collective-permute-done.18 = f32[8,1024]{1,0:T(8,128)S(1)} collective-permute-done((f32[8,1024]{1,0:T(8,128)S(1)}, f32[8,1024]{1,0:T(8,128)S(1)}, u32[]{:S(2)}, u32[]{:S(2)}) %collective-permute-start.18) | collective-permute-done | bytes 32800 | tf_op jit(solution)/shard_map/ppermute | solution.py:25
  65.7 2.0 %collective-permute-start.19 = (bf16[64,1024]{1,0:T(8,128)(2,1)S(1)}, bf16[64,1024]{1,0:T(8,128)(2,1)S(1)}, u32[]{:S(2)}, u32[]{:S(2)}) collective-permute-start(bf16[64,1024]{1,0:T(8,128)(2,1)S(1)} %get-tuple-element.110), channel_id=1, source_target_pairs={{0,16},{16,0},{32,48},{48,32},{64,80},{80,64},{96,112},{112,96},{1... | collective-permute-start | bytes 393224 | tf_op jit(solution)/shard_map/ppermute | solution.py:37
  67.7 1.9 %collective-permute-start.20 = (f32[8,1024]{1,0:T(8,128)S(1)}, f32[8,1024]{1,0:T(8,128)S(1)}, u32[]{:S(2)}, u32[]{:S(2)}) collective-permute-start(f32[8,1024]{1,0:T(8,128)S(1)} %add.35), channel_id=1, source_target_pairs={{0,6},{2,4},{4,2},{6,0},{1,7},{3,5},{5,3},{7,1},{8,14},{10,12},{12... | collective-permute-start | bytes 98312 | tf_op jit(solution)/shard_map/ppermute | solution.py:25
  69.6 3.2 %collective-permute-done.20 = f32[8,1024]{1,0:T(8,128)S(1)} collective-permute-done((f32[8,1024]{1,0:T(8,128)S(1)}, f32[8,1024]{1,0:T(8,128)S(1)}, u32[]{:S(2)}, u32[]{:S(2)}) %collective-permute-start.20) | collective-permute-done | bytes 32800 | tf_op jit(solution)/shard_map/ppermute | solution.py:25
  72.9 5.0 %collective-permute-start.21 = (bf16[64,1024]{1,0:T(8,128)(2,1)S(1)}, bf16[64,1024]{1,0:T(8,128)(2,1)S(1)}, u32[]{:S(2)}, u32[]{:S(2)}) collective-permute-start(bf16[64,1024]{1,0:T(8,128)(2,1)S(1)} %add_convert_fusion.2), channel_id=1, source_target_pairs={{0,112},{16,32},{32,16},{48,64},{64,48},{80,96},{96,80},{112,0},{1... | collective-permute-start | bytes 393224 | tf_op jit(solution)/shard_map/ppermute | solution.py:37
  77.9 3.3 %collective-permute-start.23 = (f32[8,1024]{1,0:T(8,128)S(1)}, f32[8,1024]{1,0:T(8,128)S(1)}, u32[]{:S(2)}, u32[]{:S(2)}) collective-permute-start(f32[8,1024]{1,0:T(8,128)S(1)} %add.36), channel_id=1, source_target_pairs={{0,8},{128,136},{8,0},{136,128},{1,9},{129,137},{9,1},{137,129},{2... | collective-permute-start | bytes 98312 | tf_op jit(solution)/shard_map/ppermute | solution.py:33
  81.2 2.1 %collective-permute-done.23 = f32[8,1024]{1,0:T(8,128)S(1)} collective-permute-done((f32[8,1024]{1,0:T(8,128)S(1)}, f32[8,1024]{1,0:T(8,128)S(1)}, u32[]{:S(2)}, u32[]{:S(2)}) %collective-permute-start.23) | collective-permute-done | bytes 32800 | tf_op jit(solution)/shard_map/ppermute | solution.py:33
  83.4 2.0 %collective-permute-start.22 = (bf16[64,1024]{1,0:T(8,128)(2,1)S(1)}, bf16[64,1024]{1,0:T(8,128)(2,1)S(1)}, u32[]{:S(2)}, u32[]{:S(2)}) collective-permute-start(bf16[64,1024]{1,0:T(8,128)(2,1)S(1)} %add_convert_fusion.1), channel_id=1, source_target_pairs={{0,48},{16,96},{32,80},{48,0},{64,112},{80,32},{96,16},{112,64},{1... | collective-permute-start | bytes 393224 | tf_op jit(solution)/shard_map/ppermute | solution.py:37
  88.5 3.1 %collective-permute-done.22 = bf16[64,1024]{1,0:T(8,128)(2,1)S(1)} collective-permute-done((bf16[64,1024]{1,0:T(8,128)(2,1)S(1)}, bf16[64,1024]{1,0:T(8,128)(2,1)S(1)}, u32[]{:S(2)}, u32[]{:S(2)}) %collective-permute-start.22) | collective-permute-done | bytes 131104 | tf_op jit(solution)/shard_map/ppermute | solution.py:37
  91.8 2.1 %collective-permute-start.27 = (bf16[64,1024]{1,0:T(8,128)(2,1)S(1)}, bf16[64,1024]{1,0:T(8,128)(2,1)S(1)}, u32[]{:S(2)}, u32[]{:S(2)}) collective-permute-start(bf16[64,1024]{1,0:T(8,128)(2,1)S(1)} %add_convert_fusion.own), channel_id=1, source_target_pairs={{0,128},{128,0},{8,136},{136,8},{1,129},{129,1},{9,137},{137,9},{2... | collective-permute-start | bytes 393224 | tf_op jit(solution)/shard_map/ppermute | solution.py:33
  95.3 2.4 %collective-permute-done.28.by_both = bf16[64,1024]{1,0:T(8,128)(2,1)S(1)} collective-permute-done((bf16[64,1024]{1,0:T(8,128)(2,1)S(1)}, bf16[64,1024]{1,0:T(8,128)(2,1)S(1)}, u32[]{:S(2)}, u32[]{:S(2)}) %collective-permute-start.28) | collective-permute-done | bytes 131104 | tf_op jit(solution)/shard_map/ppermute | solution.py:439
  (77 shorter events, 30.5 us)
Async XLA Ops:
  3.2 5.9 %collective-permute-start.3 = (bf16[256,2048]{1,0:T(8,128)(2,1)S(1)}, bf16[256,2048]{1,0:T(8,128)(2,1)S(1)}, u32[]{:S(2)}, u32[]{:S(2)}) collective-permute-start(bf16[256,2048]{1,0:T(8,128)(2,1)S(1)} %shard_map.92), channel_id=1, source_target_pairs={{0,1},{1,0},{2,3},{3,2},{4,5},{5,4},{6,7},{7,6},{8,9},{9,8},{10,11... | collective-permute-start | bytes 3145736 | tf_op jit(solution)/shard_map/ppermute | solution.py:21
  3.8 14.0 %collective-permute-start.1 = (bf16[256,1024]{1,0:T(8,128)(2,1)S(1)}, bf16[256,1024]{1,0:T(8,128)(2,1)S(1)}, u32[]{:S(2)}, u32[]{:S(2)}) collective-permute-start(bf16[256,1024]{1,0:T(8,128)(2,1)S(1)} %copy-done.3), channel_id=1, source_target_pairs={{0,2},{2,0},{4,6},{6,4},{1,3},{3,1},{5,7},{7,5},{8,10},{10,8},{12,... | collective-permute-start | bytes 1572872 | tf_op jit(solution)/shard_map/ppermute | solution.py:25
  5.3 14.8 %collective-permute-start = (bf16[256,1024]{1,0:T(8,128)(2,1)S(1)}, bf16[256,1024]{1,0:T(8,128)(2,1)S(1)}, u32[]{:S(2)}, u32[]{:S(2)}) collective-permute-start(bf16[256,1024]{1,0:T(8,128)(2,1)S(1)} %copy-done.3), channel_id=1, source_target_pairs={{0,136},{128,8},{8,128},{136,0},{1,137},{129,9},{9,129},{137,1},{2... | collective-permute-start | bytes 1572872 | tf_op jit(solution)/shard_map/ppermute | solution.py:33
  6.8 14.6 %collective-permute-start.2 = (bf16[256,1024]{1,0:T(8,128)(2,1)S(1)}, bf16[256,1024]{1,0:T(8,128)(2,1)S(1)}, u32[]{:S(2)}, u32[]{:S(2)}) collective-permute-start(bf16[256,1024]{1,0:T(8,128)(2,1)S(1)} %copy-done.3), channel_id=1, source_target_pairs={{0,6},{2,4},{4,2},{6,0},{1,7},{3,5},{5,3},{7,1},{8,14},{10,12},{12... | collective-permute-start | bytes 1572872 | tf_op jit(solution)/shard_map/ppermute | solution.py:25
  11.8 18.5 %collective-permute-start.8 = (bf16[4,128,640]{2,1,0:T(8,128)(2,1)S(1)}, bf16[4,128,640]{2,1,0:T(8,128)(2,1)S(1)}, u32[]{:S(2)}, u32[]{:S(2)}) collective-permute-start(bf16[4,128,640]{2,1,0:T(8,128)(2,1)S(1)} %get-tuple-element.72), channel_id=1, source_target_pairs={{0,128},{128,0},{8,136},{136,8},{1,129},{129,1},{9,137},{137,9},{2... | collective-permute-start | bytes 1966088 | tf_op jit(solution)/shard_map/ppermute | solution.py:33
  13.7 23.3 %collective-permute-start.6 = (bf16[4,128,768]{2,1,0:T(8,128)(2,1)S(1)}, bf16[4,128,768]{2,1,0:T(8,128)(2,1)S(1)}, u32[]{:S(2)}, u32[]{:S(2)}) collective-permute-start(bf16[4,128,768]{2,1,0:T(8,128)(2,1)S(1)} %get-tuple-element.69), channel_id=1, source_target_pairs={{0,136},{128,8},{8,128},{136,0},{1,137},{129,9},{9,129},{137,1},{2... | collective-permute-start | bytes 2359304 | tf_op jit(solution)/shard_map/ppermute | solution.py:33
  21.7 19.4 %collective-permute-start.11 = (bf16[384,1024]{1,0:T(8,128)(2,1)S(1)}, bf16[384,1024]{1,0:T(8,128)(2,1)S(1)}, u32[]{:S(2)}, u32[]{:S(2)}) collective-permute-start(bf16[384,1024]{1,0:T(8,128)(2,1)S(1)} %get-tuple-element.129), channel_id=1, source_target_pairs={{0,6},{2,4},{4,2},{6,0},{1,7},{3,5},{5,3},{7,1},{8,14},{10,12},{12... | collective-permute-start | bytes 2359304 | tf_op jit(solution)/shard_map/ppermute | solution.py:25
  24.0 17.8 %collective-permute-start.10 = (bf16[384,1024]{1,0:T(8,128)(2,1)S(1)}, bf16[384,1024]{1,0:T(8,128)(2,1)S(1)}, u32[]{:S(2)}, u32[]{:S(2)}) collective-permute-start(bf16[384,1024]{1,0:T(8,128)(2,1)S(1)} %get-tuple-element.130), channel_id=1, source_target_pairs={{0,2},{2,0},{4,6},{6,4},{1,3},{3,1},{5,7},{7,5},{8,10},{10,8},{12,... | collective-permute-start | bytes 2359304 | tf_op jit(solution)/shard_map/ppermute | solution.py:25
  24.0 26.2 %collective-permute-start.5 = (bf16[4,128,640]{2,1,0:T(8,128)(2,1)S(1)}, bf16[4,128,640]{2,1,0:T(8,128)(2,1)S(1)}, u32[]{:S(2)}, u32[]{:S(2)}) collective-permute-start(bf16[4,128,640]{2,1,0:T(8,128)(2,1)S(1)} %get-tuple-element.68), channel_id=1, source_target_pairs={{0,128},{128,0},{8,136},{136,8},{1,129},{129,1},{9,137},{137,9},{2... | collective-permute-start | bytes 1966088 | tf_op jit(solution)/shard_map/ppermute | solution.py:33
  30.4 20.0 %collective-permute-start.9 = (bf16[4,128,640]{2,1,0:T(8,128)(2,1)S(1)}, bf16[4,128,640]{2,1,0:T(8,128)(2,1)S(1)}, u32[]{:S(2)}, u32[]{:S(2)}) collective-permute-start(bf16[4,128,640]{2,1,0:T(8,128)(2,1)S(1)} %shard_map.96), channel_id=1, source_target_pairs={{0,136},{128,8},{8,128},{136,0},{1,137},{129,9},{9,129},{137,1},{2... | collective-permute-start | bytes 1966088 | tf_op jit(solution)/shard_map/ppermute | solution.py:33
  37.1 13.3 %collective-permute-start.7 = (bf16[4,128,384]{2,1,0:T(8,128)(2,1)S(1)}, bf16[4,128,384]{2,1,0:T(8,128)(2,1)S(1)}, u32[]{:S(2)}, u32[]{:S(2)}) collective-permute-start(bf16[4,128,384]{2,1,0:T(8,128)(2,1)S(1)} %shard_map.95), channel_id=1, source_target_pairs={{0,128},{128,0},{8,136},{136,8},{1,129},{129,1},{9,137},{137,9},{2... | collective-permute-start | bytes 1179656 | tf_op jit(solution)/shard_map/ppermute | solution.py:33
  41.9 6.6 %collective-permute-start.12 = (bf16[128,1024]{1,0:T(8,128)(2,1)S(1)}, bf16[128,1024]{1,0:T(8,128)(2,1)S(1)}, u32[]{:S(2)}, u32[]{:S(2)}) collective-permute-start(bf16[128,1024]{1,0:T(8,128)(2,1)S(1)} %get-tuple-element.128), channel_id=1, source_target_pairs={{0,2},{2,0},{4,6},{6,4},{1,3},{3,1},{5,7},{7,5},{8,10},{10,8},{12,... | collective-permute-start | bytes 786440 | tf_op jit(solution)/shard_map/ppermute | solution.py:25
  42.5 7.7 %collective-permute-start.13 = (bf16[128,1024]{1,0:T(8,128)(2,1)S(1)}, bf16[128,1024]{1,0:T(8,128)(2,1)S(1)}, u32[]{:S(2)}, u32[]{:S(2)}) collective-permute-start(bf16[128,1024]{1,0:T(8,128)(2,1)S(1)} %get-tuple-element.126), channel_id=1, source_target_pairs={{0,6},{2,4},{4,2},{6,0},{1,7},{3,5},{5,3},{7,1},{8,14},{10,12},{12... | collective-permute-start | bytes 786440 | tf_op jit(solution)/shard_map/ppermute | solution.py:25
  50.8 14.2 %collective-permute-start.14 = (bf16[128,1024]{1,0:T(8,128)(2,1)S(1)}, bf16[128,1024]{1,0:T(8,128)(2,1)S(1)}, u32[]{:S(2)}, u32[]{:S(2)}) collective-permute-start(bf16[128,1024]{1,0:T(8,128)(2,1)S(1)} %get-tuple-element.97), channel_id=1, source_target_pairs={{0,4},{2,6},{4,0},{6,2},{1,5},{3,7},{5,1},{7,3},{8,12},{10,14},{12... | collective-permute-start | bytes 786440 | tf_op jit(solution)/shard_map/ppermute | solution.py:25
  53.3 11.7 %collective-permute-start.15 = (bf16[128,1024]{1,0:T(8,128)(2,1)S(1)}, bf16[128,1024]{1,0:T(8,128)(2,1)S(1)}, u32[]{:S(2)}, u32[]{:S(2)}) collective-permute-start(bf16[128,1024]{1,0:T(8,128)(2,1)S(1)} %get-tuple-element.98), channel_id=1, source_target_pairs={{0,2},{2,0},{4,6},{6,4},{1,3},{3,1},{5,7},{7,5},{8,10},{10,8},{12,... | collective-permute-start | bytes 786440 | tf_op jit(solution)/shard_map/ppermute | solution.py:25
  53.4 11.6 %collective-permute-start.16 = (bf16[128,1024]{1,0:T(8,128)(2,1)S(1)}, bf16[128,1024]{1,0:T(8,128)(2,1)S(1)}, u32[]{:S(2)}, u32[]{:S(2)}) collective-permute-start(bf16[128,1024]{1,0:T(8,128)(2,1)S(1)} %get-tuple-element.99), channel_id=1, source_target_pairs={{0,6},{2,4},{4,2},{6,0},{1,7},{3,5},{5,3},{7,1},{8,14},{10,12},{12... | collective-permute-start | bytes 786440 | tf_op jit(solution)/shard_map/ppermute | solution.py:25
  57.0 29.9 %collective-permute-start.25 = (bf16[256,2048]{1,0:T(8,128)(2,1)S(1)}, bf16[256,2048]{1,0:T(8,128)(2,1)S(1)}, u32[]{:S(2)}, u32[]{:S(2)}) collective-permute-start(bf16[256,2048]{1,0:T(8,128)(2,1)S(1)} %get-tuple-element.118), channel_id=1, source_target_pairs={{0,1},{1,0},{2,3},{3,2},{4,5},{5,4},{6,7},{7,6},{8,9},{9,8},{10,11... | collective-permute-start | bytes 3145736 | tf_op jit(solution)/shard_map/ppermute | solution.py:21
  58.2 6.8 %collective-permute-start.18 = (f32[8,1024]{1,0:T(8,128)S(1)}, f32[8,1024]{1,0:T(8,128)S(1)}, u32[]{:S(2)}, u32[]{:S(2)}) collective-permute-start(f32[8,1024]{1,0:T(8,128)S(1)} %add.34), channel_id=1, source_target_pairs={{0,2},{2,0},{4,6},{6,4},{1,3},{3,1},{5,7},{7,5},{8,10},{10,8},{12,... | collective-permute-start | bytes 98312 | tf_op jit(solution)/shard_map/ppermute | solution.py:25
  65.7 7.1 %collective-permute-start.19 = (bf16[64,1024]{1,0:T(8,128)(2,1)S(1)}, bf16[64,1024]{1,0:T(8,128)(2,1)S(1)}, u32[]{:S(2)}, u32[]{:S(2)}) collective-permute-start(bf16[64,1024]{1,0:T(8,128)(2,1)S(1)} %get-tuple-element.110), channel_id=1, source_target_pairs={{0,16},{16,0},{32,48},{48,32},{64,80},{80,64},{96,112},{112,96},{1... | collective-permute-start | bytes 393224 | tf_op jit(solution)/shard_map/ppermute | solution.py:37
  69.6 15.8 %collective-permute-start.24 = (bf16[256,1024]{1,0:T(8,128)(2,1)S(1)}, bf16[256,1024]{1,0:T(8,128)(2,1)S(1)}, u32[]{:S(2)}, u32[]{:S(2)}) collective-permute-start(bf16[256,1024]{1,0:T(8,128)(2,1)S(1)} %get-tuple-element.117), channel_id=1, source_target_pairs={{0,1},{1,0},{2,3},{3,2},{4,5},{5,4},{6,7},{7,6},{8,9},{9,8},{10,11... | collective-permute-start | bytes 1572872 | tf_op jit(solution)/shard_map/ppermute | solution.py:21
  72.9 10.5 %collective-permute-start.21 = (bf16[64,1024]{1,0:T(8,128)(2,1)S(1)}, bf16[64,1024]{1,0:T(8,128)(2,1)S(1)}, u32[]{:S(2)}, u32[]{:S(2)}) collective-permute-start(bf16[64,1024]{1,0:T(8,128)(2,1)S(1)} %add_convert_fusion.2), channel_id=1, source_target_pairs={{0,112},{16,32},{32,16},{48,64},{64,48},{80,96},{96,80},{112,0},{1... | collective-permute-start | bytes 393224 | tf_op jit(solution)/shard_map/ppermute | solution.py:37
  83.4 8.3 %collective-permute-start.22 = (bf16[64,1024]{1,0:T(8,128)(2,1)S(1)}, bf16[64,1024]{1,0:T(8,128)(2,1)S(1)}, u32[]{:S(2)}, u32[]{:S(2)}) collective-permute-start(bf16[64,1024]{1,0:T(8,128)(2,1)S(1)} %add_convert_fusion.1), channel_id=1, source_target_pairs={{0,48},{16,96},{32,80},{48,0},{64,112},{80,32},{96,16},{112,64},{1... | collective-permute-start | bytes 393224 | tf_op jit(solution)/shard_map/ppermute | solution.py:37
  91.7 6.1 %collective-permute-start.28 = (bf16[64,1024]{1,0:T(8,128)(2,1)S(1)}, bf16[64,1024]{1,0:T(8,128)(2,1)S(1)}, u32[]{:S(2)}, u32[]{:S(2)}) collective-permute-start(bf16[64,1024]{1,0:T(8,128)(2,1)S(1)} %add_convert_fusion.own), channel_id=1, source_target_pairs={{0,144},{16,128},{32,176},{48,160},{64,208},{80,192},{96,240},{112... | collective-permute-start | bytes 393224 | tf_op jit(solution)/shard_map/ppermute | solution.py:439
  91.8 6.5 %collective-permute-start.27 = (bf16[64,1024]{1,0:T(8,128)(2,1)S(1)}, bf16[64,1024]{1,0:T(8,128)(2,1)S(1)}, u32[]{:S(2)}, u32[]{:S(2)}) collective-permute-start(bf16[64,1024]{1,0:T(8,128)(2,1)S(1)} %add_convert_fusion.own), channel_id=1, source_target_pairs={{0,128},{128,0},{8,136},{136,8},{1,129},{129,1},{9,137},{137,9},{2... | collective-permute-start | bytes 393224 | tf_op jit(solution)/shard_map/ppermute | solution.py:33
  (11 other events, 46.0 us)

commit v6 on v5

--- a/solution.py
+++ b/solution.py
@@ -414,8 +414,7 @@
     own, others, small, pre_own, pre_other = state
 
     stay, *out = sum_blocks(stay, arrived)
-    two = swap_y(out[1], 2)
-    arrived = [two, swap_y(out[0], 1), swap_y(out[2], 3)]
+    arrived = [swap_y(out[0], 1), swap_y(out[2], 3), swap_y(out[1], 2)]
     small = small + swap_core(small)
     small = small + swap_y(small, 1)
     arrived, small = lax.optimization_barrier((arrived, small))

time: 102 us -> 102 us (level)
  transfers between devices with their start and end apart: 29 -> 29, of which waited for: 17 -> 18; matrix products, arithmetic and copies ran while one was open for 1% -> 1% of each run, Pallas kernels for 19% -> 19%
where the time goes in v6:
time: 102 us; the launch traced here: 101 us
  starting transfers between devices  40.8 us (40%)
  waiting for transfers between devices  34.1 us (33%)
  Pallas kernels  22 us (22%)
  local copies, waits for them, and re-layouts  1.93 us (2%)
  other arithmetic  1.41 us (1%)
    ppermute x11, waiting for transfers between devices, swap_y(): return lax.ppermute(a, Y, [(i, i ^ flip) for i in range(4)])  16.4 us
    ppermute x11, starting transfers between devices, swap_y(): return lax.ppermute(a, Y, [(i, i ^ flip) for i in range(4)])  15.2 us
    ppermute x8, starting transfers between devices, swap_x(): lax.ppermute(a, (XL, XH), [(x_index(i), x_index(i ^ flip)) for i in range...  13.9 us
    ppermute x4, starting transfers between devices, swap_z(): return lax.ppermute(a, Z, list(enumerate(partners)))  10.6 us
    ppermute x8, waiting for transfers between devices, swap_x(): lax.ppermute(a, (XL, XH), [(x_index(i), x_index(i ^ flip)) for i in range...  10.3 us
    pallas_call x3, Pallas kernels, layer(): pl.pallas_call(functools.partial(layer_body, order, first, last), out_sha...  10.2 us
    pallas_call x2, Pallas kernels, partials(): pl.pallas_call(body, out_shape=out_shape, grid_spec=pltpu.PrefetchScalarG...  5.96 us
    ppermute x4, waiting for transfers between devices, swap_z(): return lax.ppermute(a, Z, list(enumerate(partners)))  4.26 us
  transfers between devices with their start and end apart: 29, of which 18 were waited for; matrix products, arithmetic and copies ran while one was open for 1% of the time, Pallas kernels for 19%

profile of v6, /device:TPU:2, one launch (start us, length us, event | category | flops | bytes accessed | tf_op | source)
XLA Modules:
  0.0 101.2 jit_solution(9905375878560941384)
XLA Ops:
  6.8 2.2 %collective-permute-start.2 = (bf16[256,1024]{1,0:T(8,128)(2,1)S(1)}, bf16[256,1024]{1,0:T(8,128)(2,1)S(1)}, u32[]{:S(2)}, u32[]{:S(2)}) collective-permute-start(bf16[256,1024]{1,0:T(8,128)(2,1)S(1)} %copy-done.3), channel_id=1, source_target_pairs={{0,6},{2,4},{4,2},{6,0},{1,7},{3,5},{5,3},{7,1},{8,14},{10,12},{12... | collective-permute-start | bytes 1572872 | tf_op jit(solution)/shard_map/ppermute | solution.py:25
  9.0 2.8 %shard_map.93 = (bf16[512,1024]{1,0:T(8,128)(2,1)S(1)}, bf16[4,128,640]{2,1,0:T(8,128)(2,1)S(1)}, bf16[4,128,768]{2,1,0:T(8,128)(2,1)S(1)}) custom-call(s32[4]{0:T(128)S(1)} %pad_add_fusion.pos, bf16[256,4096]{1,0:T(8,128)(2,1)S(1)} %copy-done, bf16[256,2048]{1,0:T(8,128)(2,1)S(1)} %collective-permute-done.3.tok_other, f32[1,4096]{1,0:T(1,128)S(1)} %copy-done.4, ...), custom_call_target="tpu_custom_call" | custom-call | flops 1073741824 | bytes 5242880 | tf_op jit(solution)/shard_map/pallas_call | solution.py:129
  11.8 1.9 %collective-permute-start.8 = (bf16[4,128,640]{2,1,0:T(8,128)(2,1)S(1)}, bf16[4,128,640]{2,1,0:T(8,128)(2,1)S(1)}, u32[]{:S(2)}, u32[]{:S(2)}) collective-permute-start(bf16[4,128,640]{2,1,0:T(8,128)(2,1)S(1)} %get-tuple-element.72), channel_id=1, source_target_pairs={{0,128},{128,0},{8,136},{136,8},{1,129},{129,1},{9,137},{137,9},{2... | collective-permute-start | bytes 1966088 | tf_op jit(solution)/shard_map/ppermute | solution.py:33
  13.7 3.2 %shard_map.94 = (bf16[4,128,1024]{2,1,0:T(8,128)(2,1)S(1)}, bf16[4,128,640]{2,1,0:T(8,128)(2,1)S(1)}, bf16[4,128,384]{2,1,0:T(8,128)(2,1)S(1)}, bf16[4,128,640]{2,1,0:T(8,128)(2,1)S(1)}) custom-call(s32[4]{0:T(128)S(1)} %pad_add_fusion.pos, bf16[256,4096]{1,0:T(8,128)(2,1)S(1)} %copy-done, bf16[256,2048]{1,0:T(8,128)(2,1)S(1)} %collective-permute-done.3.tok_other, ...), custom_call_target="tpu_custom_call" | custom-call | flops 1073741824 | bytes 5242880 | tf_op jit(solution)/shard_map/pallas_call | solution.py:129
  17.7 2.4 %collective-permute-done.refs_3_ = bf16[256,1024]{1,0:T(8,128)(2,1)S(1)} collective-permute-done((bf16[256,1024]{1,0:T(8,128)(2,1)S(1)}, bf16[256,1024]{1,0:T(8,128)(2,1)S(1)}, u32[]{:S(2)}, u32[]{:S(2)}) %collective-permute-start) | collective-permute-done | bytes 524320 | tf_op jit(solution)/shard_map/ppermute | solution.py:33
  21.7 2.3 %collective-permute-start.11 = (bf16[384,1024]{1,0:T(8,128)(2,1)S(1)}, bf16[384,1024]{1,0:T(8,128)(2,1)S(1)}, u32[]{:S(2)}, u32[]{:S(2)}) collective-permute-start(bf16[384,1024]{1,0:T(8,128)(2,1)S(1)} %get-tuple-element.129), channel_id=1, source_target_pairs={{0,6},{2,4},{4,2},{6,0},{1,7},{3,5},{5,3},{7,1},{8,14},{10,12},{12... | collective-permute-start | bytes 2359304 | tf_op jit(solution)/shard_map/ppermute | solution.py:25
  25.8 4.5 %shard_map.97 = (bf16[256,4096]{1,0:T(8,128)(2,1)}, bf16[256,2048]{1,0:T(8,128)(2,1)S(1)}, f32[8,1024]{1,0:T(8,128)S(1)}, f32[512,1024]{1,0:T(8,128)S(1)}) custom-call(s32[4]{0:T(128)S(1)} %pad_add_fusion.pos, bf16[256,4096]{1,0:T(8,128)(2,1)S(1)} %copy-done, bf16[256,2048]{1,0:T(8,128)(2,1)S(1)} %collective-permute-done.3.tok_other, ...), custom_call_target="tpu_custom_call" | custom-call | flops 1 | bytes 1 | tf_op jit(solution)/shard_map/pallas_call | solution.py:317
  32.0 5.0 %collective-permute-done.6.passing.three = bf16[4,128,768]{2,1,0:T(8,128)(2,1)S(1)} collective-permute-done((bf16[4,128,768]{2,1,0:T(8,128)(2,1)S(1)}, bf16[4,128,768]{2,1,0:T(8,128)(2,1)S(1)}, u32[]{:S(2)}, u32[]{:S(2)}) %collective-permute-start.6) | collective-permute-done | bytes 786464 | tf_op jit(solution)/shard_map/ppermute | solution.py:33
  37.1 2.0 %collective-permute-start.7 = (bf16[4,128,384]{2,1,0:T(8,128)(2,1)S(1)}, bf16[4,128,384]{2,1,0:T(8,128)(2,1)S(1)}, u32[]{:S(2)}, u32[]{:S(2)}) collective-permute-start(bf16[4,128,384]{2,1,0:T(8,128)(2,1)S(1)} %shard_map.95), channel_id=1, source_target_pairs={{0,128},{128,0},{8,136},{136,8},{1,129},{129,1},{9,137},{137,9},{2... | collective-permute-start | bytes 1179656 | tf_op jit(solution)/shard_map/ppermute | solution.py:33
  39.1 2.1 %collective-permute-done.11 = bf16[384,1024]{1,0:T(8,128)(2,1)S(1)} collective-permute-done((bf16[384,1024]{1,0:T(8,128)(2,1)S(1)}, bf16[384,1024]{1,0:T(8,128)(2,1)S(1)}, u32[]{:S(2)}, u32[]{:S(2)}) %collective-permute-start.11) | collective-permute-done | bytes 786464 | tf_op jit(solution)/shard_map/ppermute | solution.py:25
  43.9 3.7 %shard_map.98 = (bf16[256,4096]{1,0:T(8,128)(2,1)}, bf16[256,2048]{1,0:T(8,128)(2,1)S(1)}, f32[8,1024]{1,0:T(8,128)S(1)}, f32[512,1024]{1,0:T(8,128)S(1)}) custom-call(s32[4]{0:T(128)S(1)} %pad_add_fusion.pos, bf16[256,4096]{1,0:T(8,128)(2,1)S(1)} %copy-done.1, ...), custom_call_target="tpu_custom_call", output_to_operand_aliasing={{0}: (12, {}), {1}: (13, {})} | custom-call | flops 1 | bytes 1 | tf_op jit(solution)/shard_map/pallas_call | solution.py:317
  51.5 2.3 %collective-permute-start.15 = (bf16[128,1024]{1,0:T(8,128)(2,1)S(1)}, bf16[128,1024]{1,0:T(8,128)(2,1)S(1)}, u32[]{:S(2)}, u32[]{:S(2)}) collective-permute-start(bf16[128,1024]{1,0:T(8,128)(2,1)S(1)} %get-tuple-element.98), channel_id=1, source_target_pairs={{0,6},{2,4},{4,2},{6,0},{1,7},{3,5},{5,3},{7,1},{8,14},{10,12},{12... | collective-permute-start | bytes 786440 | tf_op jit(solution)/shard_map/ppermute | solution.py:25
  55.0 2.0 %shard_map.100 = (bf16[256,4096]{1,0:T(8,128)(2,1)}, bf16[256,2048]{1,0:T(8,128)(2,1)S(1)}, f32[8,1024]{1,0:T(8,128)S(1)}, f32[256,1024]{1,0:T(8,128)S(1)}, bf16[256,1024]{1,0:T(8,128)(2,1)S(1)}) custom-call(s32[4]{0:T(128)S(1)} %pad_add_fusion.pos, bf16[256,4096]{1,0:T(8,128)(2,1)S(1)} %copy-done.1, ...), custom_call_target="tpu_custom_call", output_to_operand_aliasing={{0}: (10, {}), {1}: (11, {})} | custom-call | flops 1 | bytes 1 | tf_op jit(solution)/shard_map/pallas_call | solution.py:317
  58.9 5.0 %collective-permute-done.18 = f32[8,1024]{1,0:T(8,128)S(1)} collective-permute-done((f32[8,1024]{1,0:T(8,128)S(1)}, f32[8,1024]{1,0:T(8,128)S(1)}, u32[]{:S(2)}, u32[]{:S(2)}) %collective-permute-start.18) | collective-permute-done | bytes 32800 | tf_op jit(solution)/shard_map/ppermute | solution.py:25
  65.9 2.0 %collective-permute-start.19 = (bf16[64,1024]{1,0:T(8,128)(2,1)S(1)}, bf16[64,1024]{1,0:T(8,128)(2,1)S(1)}, u32[]{:S(2)}, u32[]{:S(2)}) collective-permute-start(bf16[64,1024]{1,0:T(8,128)(2,1)S(1)} %get-tuple-element.110), channel_id=1, source_target_pairs={{0,16},{16,0},{32,48},{48,32},{64,80},{80,64},{96,112},{112,96},{1... | collective-permute-start | bytes 393224 | tf_op jit(solution)/shard_map/ppermute | solution.py:37
  67.9 2.4 %collective-permute-start.20 = (f32[8,1024]{1,0:T(8,128)S(1)}, f32[8,1024]{1,0:T(8,128)S(1)}, u32[]{:S(2)}, u32[]{:S(2)}) collective-permute-start(f32[8,1024]{1,0:T(8,128)S(1)} %add.35), channel_id=1, source_target_pairs={{0,6},{2,4},{4,2},{6,0},{1,7},{3,5},{5,3},{7,1},{8,14},{10,12},{12... | collective-permute-start | bytes 98312 | tf_op jit(solution)/shard_map/ppermute | solution.py:25
  70.3 2.7 %collective-permute-done.20 = f32[8,1024]{1,0:T(8,128)S(1)} collective-permute-done((f32[8,1024]{1,0:T(8,128)S(1)}, f32[8,1024]{1,0:T(8,128)S(1)}, u32[]{:S(2)}, u32[]{:S(2)}) %collective-permute-start.20) | collective-permute-done | bytes 32800 | tf_op jit(solution)/shard_map/ppermute | solution.py:25
  73.0 5.0 %collective-permute-start.21 = (bf16[64,1024]{1,0:T(8,128)(2,1)S(1)}, bf16[64,1024]{1,0:T(8,128)(2,1)S(1)}, u32[]{:S(2)}, u32[]{:S(2)}) collective-permute-start(bf16[64,1024]{1,0:T(8,128)(2,1)S(1)} %add_convert_fusion.2), channel_id=1, source_target_pairs={{0,112},{16,32},{32,16},{48,64},{64,48},{80,96},{96,80},{112,0},{1... | collective-permute-start | bytes 393224 | tf_op jit(solution)/shard_map/ppermute | solution.py:37
  78.1 3.3 %collective-permute-start.23 = (f32[8,1024]{1,0:T(8,128)S(1)}, f32[8,1024]{1,0:T(8,128)S(1)}, u32[]{:S(2)}, u32[]{:S(2)}) collective-permute-start(f32[8,1024]{1,0:T(8,128)S(1)} %add.36), channel_id=1, source_target_pairs={{0,8},{128,136},{8,0},{136,128},{1,9},{129,137},{9,1},{137,129},{2... | collective-permute-start | bytes 98312 | tf_op jit(solution)/shard_map/ppermute | solution.py:33
  81.4 2.1 %collective-permute-done.23 = f32[8,1024]{1,0:T(8,128)S(1)} collective-permute-done((f32[8,1024]{1,0:T(8,128)S(1)}, f32[8,1024]{1,0:T(8,128)S(1)}, u32[]{:S(2)}, u32[]{:S(2)}) %collective-permute-start.23) | collective-permute-done | bytes 32800 | tf_op jit(solution)/shard_map/ppermute | solution.py:33
  83.6 2.0 %collective-permute-start.22 = (bf16[64,1024]{1,0:T(8,128)(2,1)S(1)}, bf16[64,1024]{1,0:T(8,128)(2,1)S(1)}, u32[]{:S(2)}, u32[]{:S(2)}) collective-permute-start(bf16[64,1024]{1,0:T(8,128)(2,1)S(1)} %add_convert_fusion.1), channel_id=1, source_target_pairs={{0,48},{16,96},{32,80},{48,0},{64,112},{80,32},{96,16},{112,64},{1... | collective-permute-start | bytes 393224 | tf_op jit(solution)/shard_map/ppermute | solution.py:37
  88.7 3.0 %collective-permute-done.22 = bf16[64,1024]{1,0:T(8,128)(2,1)S(1)} collective-permute-done((bf16[64,1024]{1,0:T(8,128)(2,1)S(1)}, bf16[64,1024]{1,0:T(8,128)(2,1)S(1)}, u32[]{:S(2)}, u32[]{:S(2)}) %collective-permute-start.22) | collective-permute-done | bytes 131104 | tf_op jit(solution)/shard_map/ppermute | solution.py:37
  91.9 1.9 %collective-permute-start.27 = (bf16[64,1024]{1,0:T(8,128)(2,1)S(1)}, bf16[64,1024]{1,0:T(8,128)(2,1)S(1)}, u32[]{:S(2)}, u32[]{:S(2)}) collective-permute-start(bf16[64,1024]{1,0:T(8,128)(2,1)S(1)} %add_convert_fusion.own), channel_id=1, source_target_pairs={{0,128},{128,0},{8,136},{136,8},{1,129},{129,1},{9,137},{137,9},{2... | collective-permute-start | bytes 393224 | tf_op jit(solution)/shard_map/ppermute | solution.py:33
  95.4 2.5 %collective-permute-done.28.by_both = bf16[64,1024]{1,0:T(8,128)(2,1)S(1)} collective-permute-done((bf16[64,1024]{1,0:T(8,128)(2,1)S(1)}, bf16[64,1024]{1,0:T(8,128)(2,1)S(1)}, u32[]{:S(2)}, u32[]{:S(2)}) %collective-permute-start.28) | collective-permute-done | bytes 131104 | tf_op jit(solution)/shard_map/ppermute | solution.py:438
  (77 shorter events, 32.0 us)
Async XLA Ops:
  3.2 5.9 %collective-permute-start.3 = (bf16[256,2048]{1,0:T(8,128)(2,1)S(1)}, bf16[256,2048]{1,0:T(8,128)(2,1)S(1)}, u32[]{:S(2)}, u32[]{:S(2)}) collective-permute-start(bf16[256,2048]{1,0:T(8,128)(2,1)S(1)} %shard_map.92), channel_id=1, source_target_pairs={{0,1},{1,0},{2,3},{3,2},{4,5},{5,4},{6,7},{7,6},{8,9},{9,8},{10,11... | collective-permute-start | bytes 3145736 | tf_op jit(solution)/shard_map/ppermute | solution.py:21
  3.8 14.0 %collective-permute-start.1 = (bf16[256,1024]{1,0:T(8,128)(2,1)S(1)}, bf16[256,1024]{1,0:T(8,128)(2,1)S(1)}, u32[]{:S(2)}, u32[]{:S(2)}) collective-permute-start(bf16[256,1024]{1,0:T(8,128)(2,1)S(1)} %copy-done.3), channel_id=1, source_target_pairs={{0,2},{2,0},{4,6},{6,4},{1,3},{3,1},{5,7},{7,5},{8,10},{10,8},{12,... | collective-permute-start | bytes 1572872 | tf_op jit(solution)/shard_map/ppermute | solution.py:25
  5.3 14.8 %collective-permute-start = (bf16[256,1024]{1,0:T(8,128)(2,1)S(1)}, bf16[256,1024]{1,0:T(8,128)(2,1)S(1)}, u32[]{:S(2)}, u32[]{:S(2)}) collective-permute-start(bf16[256,1024]{1,0:T(8,128)(2,1)S(1)} %copy-done.3), channel_id=1, source_target_pairs={{0,136},{128,8},{8,128},{136,0},{1,137},{129,9},{9,129},{137,1},{2... | collective-permute-start | bytes 1572872 | tf_op jit(solution)/shard_map/ppermute | solution.py:33
  6.8 14.6 %collective-permute-start.2 = (bf16[256,1024]{1,0:T(8,128)(2,1)S(1)}, bf16[256,1024]{1,0:T(8,128)(2,1)S(1)}, u32[]{:S(2)}, u32[]{:S(2)}) collective-permute-start(bf16[256,1024]{1,0:T(8,128)(2,1)S(1)} %copy-done.3), channel_id=1, source_target_pairs={{0,6},{2,4},{4,2},{6,0},{1,7},{3,5},{5,3},{7,1},{8,14},{10,12},{12... | collective-permute-start | bytes 1572872 | tf_op jit(solution)/shard_map/ppermute | solution.py:25
  11.8 18.5 %collective-permute-start.8 = (bf16[4,128,640]{2,1,0:T(8,128)(2,1)S(1)}, bf16[4,128,640]{2,1,0:T(8,128)(2,1)S(1)}, u32[]{:S(2)}, u32[]{:S(2)}) collective-permute-start(bf16[4,128,640]{2,1,0:T(8,128)(2,1)S(1)} %get-tuple-element.72), channel_id=1, source_target_pairs={{0,128},{128,0},{8,136},{136,8},{1,129},{129,1},{9,137},{137,9},{2... | collective-permute-start | bytes 1966088 | tf_op jit(solution)/shard_map/ppermute | solution.py:33
  13.7 23.3 %collective-permute-start.6 = (bf16[4,128,768]{2,1,0:T(8,128)(2,1)S(1)}, bf16[4,128,768]{2,1,0:T(8,128)(2,1)S(1)}, u32[]{:S(2)}, u32[]{:S(2)}) collective-permute-start(bf16[4,128,768]{2,1,0:T(8,128)(2,1)S(1)} %get-tuple-element.69), channel_id=1, source_target_pairs={{0,136},{128,8},{8,128},{136,0},{1,137},{129,9},{9,129},{137,1},{2... | collective-permute-start | bytes 2359304 | tf_op jit(solution)/shard_map/ppermute | solution.py:33
  21.7 19.4 %collective-permute-start.11 = (bf16[384,1024]{1,0:T(8,128)(2,1)S(1)}, bf16[384,1024]{1,0:T(8,128)(2,1)S(1)}, u32[]{:S(2)}, u32[]{:S(2)}) collective-permute-start(bf16[384,1024]{1,0:T(8,128)(2,1)S(1)} %get-tuple-element.129), channel_id=1, source_target_pairs={{0,6},{2,4},{4,2},{6,0},{1,7},{3,5},{5,3},{7,1},{8,14},{10,12},{12... | collective-permute-start | bytes 2359304 | tf_op jit(solution)/shard_map/ppermute | solution.py:25
  24.0 17.8 %collective-permute-start.10 = (bf16[384,1024]{1,0:T(8,128)(2,1)S(1)}, bf16[384,1024]{1,0:T(8,128)(2,1)S(1)}, u32[]{:S(2)}, u32[]{:S(2)}) collective-permute-start(bf16[384,1024]{1,0:T(8,128)(2,1)S(1)} %get-tuple-element.130), channel_id=1, source_target_pairs={{0,2},{2,0},{4,6},{6,4},{1,3},{3,1},{5,7},{7,5},{8,10},{10,8},{12,... | collective-permute-start | bytes 2359304 | tf_op jit(solution)/shard_map/ppermute | solution.py:25
  24.0 26.2 %collective-permute-start.5 = (bf16[4,128,640]{2,1,0:T(8,128)(2,1)S(1)}, bf16[4,128,640]{2,1,0:T(8,128)(2,1)S(1)}, u32[]{:S(2)}, u32[]{:S(2)}) collective-permute-start(bf16[4,128,640]{2,1,0:T(8,128)(2,1)S(1)} %get-tuple-element.68), channel_id=1, source_target_pairs={{0,128},{128,0},{8,136},{136,8},{1,129},{129,1},{9,137},{137,9},{2... | collective-permute-start | bytes 1966088 | tf_op jit(solution)/shard_map/ppermute | solution.py:33
  30.4 20.0 %collective-permute-start.9 = (bf16[4,128,640]{2,1,0:T(8,128)(2,1)S(1)}, bf16[4,128,640]{2,1,0:T(8,128)(2,1)S(1)}, u32[]{:S(2)}, u32[]{:S(2)}) collective-permute-start(bf16[4,128,640]{2,1,0:T(8,128)(2,1)S(1)} %shard_map.96), channel_id=1, source_target_pairs={{0,136},{128,8},{8,128},{136,0},{1,137},{129,9},{9,129},{137,1},{2... | collective-permute-start | bytes 1966088 | tf_op jit(solution)/shard_map/ppermute | solution.py:33
  37.1 13.3 %collective-permute-start.7 = (bf16[4,128,384]{2,1,0:T(8,128)(2,1)S(1)}, bf16[4,128,384]{2,1,0:T(8,128)(2,1)S(1)}, u32[]{:S(2)}, u32[]{:S(2)}) collective-permute-start(bf16[4,128,384]{2,1,0:T(8,128)(2,1)S(1)} %shard_map.95), channel_id=1, source_target_pairs={{0,128},{128,0},{8,136},{136,8},{1,129},{129,1},{9,137},{137,9},{2... | collective-permute-start | bytes 1179656 | tf_op jit(solution)/shard_map/ppermute | solution.py:33
  41.9 6.6 %collective-permute-start.12 = (bf16[128,1024]{1,0:T(8,128)(2,1)S(1)}, bf16[128,1024]{1,0:T(8,128)(2,1)S(1)}, u32[]{:S(2)}, u32[]{:S(2)}) collective-permute-start(bf16[128,1024]{1,0:T(8,128)(2,1)S(1)} %get-tuple-element.128), channel_id=1, source_target_pairs={{0,2},{2,0},{4,6},{6,4},{1,3},{3,1},{5,7},{7,5},{8,10},{10,8},{12,... | collective-permute-start | bytes 786440 | tf_op jit(solution)/shard_map/ppermute | solution.py:25
  42.5 7.7 %collective-permute-start.13 = (bf16[128,1024]{1,0:T(8,128)(2,1)S(1)}, bf16[128,1024]{1,0:T(8,128)(2,1)S(1)}, u32[]{:S(2)}, u32[]{:S(2)}) collective-permute-start(bf16[128,1024]{1,0:T(8,128)(2,1)S(1)} %get-tuple-element.126), channel_id=1, source_target_pairs={{0,6},{2,4},{4,2},{6,0},{1,7},{3,5},{5,3},{7,1},{8,14},{10,12},{12... | collective-permute-start | bytes 786440 | tf_op jit(solution)/shard_map/ppermute | solution.py:25
  50.8 13.2 %collective-permute-start.14 = (bf16[128,1024]{1,0:T(8,128)(2,1)S(1)}, bf16[128,1024]{1,0:T(8,128)(2,1)S(1)}, u32[]{:S(2)}, u32[]{:S(2)}) collective-permute-start(bf16[128,1024]{1,0:T(8,128)(2,1)S(1)} %get-tuple-element.97), channel_id=1, source_target_pairs={{0,2},{2,0},{4,6},{6,4},{1,3},{3,1},{5,7},{7,5},{8,10},{10,8},{12,... | collective-permute-start | bytes 786440 | tf_op jit(solution)/shard_map/ppermute | solution.py:25
  51.5 12.4 %collective-permute-start.15 = (bf16[128,1024]{1,0:T(8,128)(2,1)S(1)}, bf16[128,1024]{1,0:T(8,128)(2,1)S(1)}, u32[]{:S(2)}, u32[]{:S(2)}) collective-permute-start(bf16[128,1024]{1,0:T(8,128)(2,1)S(1)} %get-tuple-element.98), channel_id=1, source_target_pairs={{0,6},{2,4},{4,2},{6,0},{1,7},{3,5},{5,3},{7,1},{8,14},{10,12},{12... | collective-permute-start | bytes 786440 | tf_op jit(solution)/shard_map/ppermute | solution.py:25
  53.9 11.3 %collective-permute-start.16 = (bf16[128,1024]{1,0:T(8,128)(2,1)S(1)}, bf16[128,1024]{1,0:T(8,128)(2,1)S(1)}, u32[]{:S(2)}, u32[]{:S(2)}) collective-permute-start(bf16[128,1024]{1,0:T(8,128)(2,1)S(1)} %get-tuple-element.99), channel_id=1, source_target_pairs={{0,4},{2,6},{4,0},{6,2},{1,5},{3,7},{5,1},{7,3},{8,12},{10,14},{12... | collective-permute-start | bytes 786440 | tf_op jit(solution)/shard_map/ppermute | solution.py:25
  57.0 30.1 %collective-permute-start.25 = (bf16[256,2048]{1,0:T(8,128)(2,1)S(1)}, bf16[256,2048]{1,0:T(8,128)(2,1)S(1)}, u32[]{:S(2)}, u32[]{:S(2)}) collective-permute-start(bf16[256,2048]{1,0:T(8,128)(2,1)S(1)} %get-tuple-element.118), channel_id=1, source_target_pairs={{0,1},{1,0},{2,3},{3,2},{4,5},{5,4},{6,7},{7,6},{8,9},{9,8},{10,11... | collective-permute-start | bytes 3145736 | tf_op jit(solution)/shard_map/ppermute | solution.py:21
  65.9 7.1 %collective-permute-start.19 = (bf16[64,1024]{1,0:T(8,128)(2,1)S(1)}, bf16[64,1024]{1,0:T(8,128)(2,1)S(1)}, u32[]{:S(2)}, u32[]{:S(2)}) collective-permute-start(bf16[64,1024]{1,0:T(8,128)(2,1)S(1)} %get-tuple-element.110), channel_id=1, source_target_pairs={{0,16},{16,0},{32,48},{48,32},{64,80},{80,64},{96,112},{112,96},{1... | collective-permute-start | bytes 393224 | tf_op jit(solution)/shard_map/ppermute | solution.py:37
  70.3 15.2 %collective-permute-start.24 = (bf16[256,1024]{1,0:T(8,128)(2,1)S(1)}, bf16[256,1024]{1,0:T(8,128)(2,1)S(1)}, u32[]{:S(2)}, u32[]{:S(2)}) collective-permute-start(bf16[256,1024]{1,0:T(8,128)(2,1)S(1)} %get-tuple-element.117), channel_id=1, source_target_pairs={{0,1},{1,0},{2,3},{3,2},{4,5},{5,4},{6,7},{7,6},{8,9},{9,8},{10,11... | collective-permute-start | bytes 1572872 | tf_op jit(solution)/shard_map/ppermute | solution.py:21
  73.0 10.5 %collective-permute-start.21 = (bf16[64,1024]{1,0:T(8,128)(2,1)S(1)}, bf16[64,1024]{1,0:T(8,128)(2,1)S(1)}, u32[]{:S(2)}, u32[]{:S(2)}) collective-permute-start(bf16[64,1024]{1,0:T(8,128)(2,1)S(1)} %add_convert_fusion.2), channel_id=1, source_target_pairs={{0,112},{16,32},{32,16},{48,64},{64,48},{80,96},{96,80},{112,0},{1... | collective-permute-start | bytes 393224 | tf_op jit(solution)/shard_map/ppermute | solution.py:37
  83.6 8.2 %collective-permute-start.22 = (bf16[64,1024]{1,0:T(8,128)(2,1)S(1)}, bf16[64,1024]{1,0:T(8,128)(2,1)S(1)}, u32[]{:S(2)}, u32[]{:S(2)}) collective-permute-start(bf16[64,1024]{1,0:T(8,128)(2,1)S(1)} %add_convert_fusion.1), channel_id=1, source_target_pairs={{0,48},{16,96},{32,80},{48,0},{64,112},{80,32},{96,16},{112,64},{1... | collective-permute-start | bytes 393224 | tf_op jit(solution)/shard_map/ppermute | solution.py:37
  91.8 6.1 %collective-permute-start.28 = (bf16[64,1024]{1,0:T(8,128)(2,1)S(1)}, bf16[64,1024]{1,0:T(8,128)(2,1)S(1)}, u32[]{:S(2)}, u32[]{:S(2)}) collective-permute-start(bf16[64,1024]{1,0:T(8,128)(2,1)S(1)} %add_convert_fusion.own), channel_id=1, source_target_pairs={{0,144},{16,128},{32,176},{48,160},{64,208},{80,192},{96,240},{112... | collective-permute-start | bytes 393224 | tf_op jit(solution)/shard_map/ppermute | solution.py:438
  91.9 6.4 %collective-permute-start.27 = (bf16[64,1024]{1,0:T(8,128)(2,1)S(1)}, bf16[64,1024]{1,0:T(8,128)(2,1)S(1)}, u32[]{:S(2)}, u32[]{:S(2)}) collective-permute-start(bf16[64,1024]{1,0:T(8,128)(2,1)S(1)} %add_convert_fusion.own), channel_id=1, source_target_pairs={{0,128},{128,0},{8,136},{136,8},{1,129},{129,1},{9,137},{137,9},{2... | collective-permute-start | bytes 393224 | tf_op jit(solution)/shard_map/ppermute | solution.py:33
  93.8 5.8 %collective-permute-start.26 = (bf16[64,1024]{1,0:T(8,128)(2,1)S(1)}, bf16[64,1024]{1,0:T(8,128)(2,1)S(1)}, u32[]{:S(2)}, u32[]{:S(2)}) collective-permute-start(bf16[64,1024]{1,0:T(8,128)(2,1)S(1)} %add_convert_fusion.own), channel_id=1, source_target_pairs={{0,16},{16,0},{32,48},{48,32},{64,80},{80,64},{96,112},{112,96},{1... | collective-permute-start | bytes 393224 | tf_op jit(solution)/shard_map/ppermute | solution.py:37
  (11 other events, 45.9 us)
